TPU v7x, 32 devices: a whole 2x2x4 slice. The times are simulated.
32 devices in a mesh: dp: 2 (over y), expert: 16 (over z, x, core).
Axes of the slice: x: 2, y: 2, z: 4, core: 2. Of those that a mesh axis runs over, the one named last changes fastest.
Arguments:
- pre_query: bfloat16 [512, 16, 576], P(('dp', 'expert')), may hold values from -25 to 25
- pre_latent: bfloat16 [512, 576], P(('dp', 'expert')), may hold values from -5 to 5
- pre_resid: bfloat16 [512, 2048], P(('dp', 'expert')), may hold values from -6 to 6
- dec_query: bfloat16 [32, 16, 576], P(('dp', 'expert')), may hold values from -25 to 25
- dec_latent: bfloat16 [32, 576], P(('dp', 'expert')), may hold values from -5 to 5
- dec_resid: bfloat16 [32, 2048], P(('dp', 'expert')), may hold values from -6 to 6
- cache_lengths: int32 [32], P(('dp', 'expert')), may hold values from 1 to 32768
- latent_cache: bfloat16 [32, 1024, 576], P(('dp', 'expert')), may hold values from -5 to 5
- sink_logits: float32 [16], replicated, may hold values from -1 to 3
- uv_weight: bfloat16 [16, 512, 128], P('dp', 'expert'), may hold values from -0.25 to 0.25
- out_weight: bfloat16 [16, 128, 2048], P('dp', 'expert'), may hold values from -0.125 to 0.125
- norm_gain: bfloat16 [2048], replicated, may hold values from 0.5 to 1.5
- router: bfloat16 [2048, 16], P(None, 'expert'), may hold values from -0.125 to 0.125
- routes: int32 [544, 6], P(('dp', 'expert')), may hold values from 0 to 15, all different within a row; in each aligned block of 17 rows (0 to 16, 17 to 33, ...) at most 7 rows name the same one
- gate_weight: bfloat16 [16, 2048, 1408], P('expert', None, 'dp'), may hold values from -0.125 to 0.125
- up_weight: bfloat16 [16, 2048, 1408], P('expert', None, 'dp'), may hold values from -0.125 to 0.125
- down_weight: bfloat16 [16, 1408, 2048], P('expert', None, 'dp'), may hold values from -0.15625 to 0.15625
- shared_gate: bfloat16 [2048, 1408], P('expert', 'dp'), may hold values from -0.125 to 0.125
- shared_up: bfloat16 [2048, 1408], P('expert', 'dp'), may hold values from -0.125 to 0.125
- shared_down: bfloat16 [1408, 2048], P('expert', 'dp'), may hold values from -0.15625 to 0.15625
Outputs:
- pre_out: bfloat16 [512, 2048], P(('dp', 'expert'))
- dec_out: bfloat16 [32, 2048], P(('dp', 'expert'))
Inputs may be any that keep to these rules, and one draw needn't show every extreme that they name: `routes`: each row names 6 different experts; in each aligned block of 17 rows no expert is named by more than 7 rows.
All inputs are finite; a program needn't handle non-finite values.
Results may differ from a plain program's by a relative error of at most 0.015.
Values may be sent and summed in bfloat16 or wider, within the bound.
No kernel may reach another device: no remote copies, remote signals or barrier semaphores. Data moves between devices by JAX's collectives and lax.ppermute only.
A program may use at most 64 MiB of HBM per device.

v0:
```python
from functools import partial

import jax
import jax.numpy as jnp
from jax import lax
from jax.sharding import PartitionSpec as P

D = 2048
LATENT = 512
ROPE = 64
QK_NOPE = 128
TOPK = 6


ROUTE_SCALE = 2.446
NORM_EPS = 1e-06
NEG_FILL = -1e30


def assign_slots(route_rows, experts):
    flat_routes = route_rows.reshape(-1)
    one_hot = (flat_routes[:, None] == jnp.arange(experts, dtype=jnp.int32)[None, :]).astype(
        jnp.int32
    )
    running = jnp.cumsum(one_hot, axis=0)
    slot_rank = jnp.sum(running * one_hot, axis=1) - 1
    return slot_rank.reshape(route_rows.shape)


def dispatch_matrix(route_rows, slot_rows, experts, capacity):
    target = route_rows * capacity + slot_rows
    places = jnp.arange(experts * capacity, dtype=jnp.int32)
    total = jnp.zeros((route_rows.shape[0], experts * capacity), jnp.bfloat16)
    for column in range(route_rows.shape[1]):
        total = total + (target[:, column][:, None] == places[None, :]).astype(jnp.bfloat16)
    return total


def shards(
    pre_query,
    pre_latent,
    pre_resid,
    dec_query,
    dec_latent,
    dec_resid,
    cache_lengths,
    latent_cache,
    sink_logits,
    uv_weight,
    out_weight,
    norm_gain,
    router,
    routes,
    gate_weight,
    up_weight,
    down_weight,
    shared_gate,
    shared_up,
    shared_down,
):
    groups = lax.axis_size("dp")
    members = lax.axis_size("expert")
    pre_rows = pre_query.shape[0]
    rows_dev = pre_rows + 1
    scale_qk = (QK_NOPE + ROPE) ** (-0.5)
    pre_scores = (
        jnp.einsum("thc,uc->thu", pre_query, pre_latent, preferred_element_type=jnp.float32)
        * scale_qk
    )
    places = jnp.arange(pre_rows, dtype=jnp.int32)
    allowed = (places[None, :] <= places[:, None])[:, None, :]
    masked = jnp.where(allowed, pre_scores, NEG_FILL)
    pre_max = jnp.maximum(jnp.max(masked, axis=2), sink_logits[None, :])
    exp_terms = jnp.where(allowed, jnp.exp(masked - pre_max[:, :, None]), 0.0)
    denominator = jnp.sum(exp_terms, axis=2) + jnp.exp(sink_logits[None, :] - pre_max)
    numerator = jnp.einsum(
        "thu,ul->thl",
        exp_terms.astype(jnp.bfloat16),
        pre_latent[:, :LATENT],
        preferred_element_type=jnp.float32,
    )
    pre_att = (numerator / denominator[:, :, None]).astype(jnp.bfloat16)
    window = latent_cache.shape[1]
    slot_ids = jnp.arange(window, dtype=jnp.int32)
    newest = cache_lengths - 1
    position = newest[:, None] - jnp.mod(newest[:, None] - slot_ids[None, :], window)
    usable = ((position >= 0) & (position > cache_lengths[:, None] - window))[:, None, :]
    cache_scores = (
        jnp.einsum("rhc,rsc->rhs", dec_query, latent_cache, preferred_element_type=jnp.float32)
        * scale_qk
    )
    own_scores = (
        jnp.einsum("rhc,rc->rh", dec_query, dec_latent, preferred_element_type=jnp.float32)
        * scale_qk
    )
    cache_masked = jnp.where(usable, cache_scores, NEG_FILL)
    top_score = jnp.maximum(
        jnp.maximum(jnp.max(cache_masked, axis=2), own_scores), sink_logits[None, :]
    )
    cache_exp = jnp.where(usable, jnp.exp(cache_masked - top_score[:, :, None]), 0.0)
    own_exp = jnp.exp(own_scores - top_score)
    dec_numer = jnp.einsum(
        "rhs,rsl->rhl",
        cache_exp.astype(jnp.bfloat16),
        latent_cache[:, :, :LATENT],
        preferred_element_type=jnp.float32,
    )
    dec_numer = dec_numer + own_exp.astype(jnp.bfloat16).astype(jnp.float32)[
        :, :, None
    ] * dec_latent[:, None, :LATENT].astype(jnp.float32)
    dec_total = jnp.sum(cache_exp, axis=2) + own_exp + jnp.exp(sink_logits[None, :] - top_score)
    dec_att = (dec_numer / dec_total[:, :, None]).astype(jnp.bfloat16)
    attention = jnp.concatenate([pre_att, dec_att], axis=0)
    spread = lax.all_to_all(attention, "dp", split_axis=1, concat_axis=0, tiled=True)
    uv_full, out_full = (
        lax.all_gather(uv_weight, "expert", axis=1, tiled=True),
        lax.all_gather(out_weight, "expert", axis=1, tiled=True),
    )
    head_values = jnp.einsum(
        "thl,hlv->thv", spread, uv_full, preferred_element_type=jnp.float32
    ).astype(jnp.bfloat16)
    head_partial = jnp.einsum(
        "thv,hvd->td", head_values, out_full, preferred_element_type=jnp.float32
    )
    attn_out = lax.psum_scatter(
        head_partial.astype(jnp.bfloat16), "dp", scatter_dimension=0, tiled=True
    ).astype(jnp.float32)
    resid = jnp.concatenate([pre_resid, dec_resid], axis=0)
    hidden = (resid.astype(jnp.float32) + attn_out).astype(jnp.bfloat16)
    hidden_up = lax.optimization_barrier(hidden).astype(jnp.float32)
    mean_square = jnp.mean(hidden_up * hidden_up, axis=1, keepdims=True)
    normed = (
        hidden_up * lax.rsqrt(mean_square + NORM_EPS) * norm_gain.astype(jnp.float32)[None, :]
    ).astype(jnp.bfloat16)
    capacity = max(2, (rows_dev * TOPK + members - 1) // members)
    group_tokens = lax.all_gather(normed, "dp", axis=0, tiled=True)
    group_routes = lax.all_gather(routes, "dp", axis=0, tiled=True)
    routes_by_group = group_routes.reshape(groups, rows_dev, TOPK)
    slots_by_group = jax.vmap(partial(assign_slots, experts=members))(routes_by_group)
    tokens_by_group = group_tokens.reshape(groups, rows_dev, D)
    all_matrix = jax.vmap(partial(dispatch_matrix, experts=members, capacity=capacity))(
        routes_by_group, slots_by_group
    )
    all_matrix = all_matrix.reshape(groups, rows_dev, members, capacity)
    outgoing = jnp.einsum(
        "grxc,grd->xgcd", all_matrix, tokens_by_group, preferred_element_type=jnp.bfloat16
    )
    expert_rows = lax.all_to_all(outgoing, "expert", split_axis=0, concat_axis=0, tiled=True)
    expert_rows = expert_rows.reshape(-1, D)
    gate_score = jax.nn.sigmoid(
        jnp.dot(expert_rows, router[:, 0], preferred_element_type=jnp.float32)
    )
    gate_proj = jnp.dot(expert_rows, gate_weight[0], preferred_element_type=jnp.float32)
    up_proj = jnp.dot(expert_rows, up_weight[0], preferred_element_type=jnp.float32)
    expert_act = (jax.nn.silu(gate_proj) * up_proj).astype(jnp.bfloat16)
    shared_gate_full, shared_up_full, shared_down_full = (
        lax.all_gather(shared_gate, "expert", axis=0, tiled=True),
        lax.all_gather(shared_up, "expert", axis=0, tiled=True),
        lax.all_gather(shared_down, "expert", axis=0, tiled=True),
    )
    shared_act = (
        jax.nn.silu(jnp.dot(group_tokens, shared_gate_full, preferred_element_type=jnp.float32))
        * jnp.dot(group_tokens, shared_up_full, preferred_element_type=jnp.float32)
    ).astype(jnp.bfloat16)
    down_local = down_weight[0]
    col_width = down_local.shape[1]
    routed_piece = lax.all_gather(expert_act, "dp", axis=1, tiled=True)
    shared_piece = lax.all_gather(shared_act, "dp", axis=1, tiled=True)
    routed_cols = jnp.dot(routed_piece, down_local, preferred_element_type=jnp.float32)
    shared_cols = jnp.dot(shared_piece, shared_down_full, preferred_element_type=jnp.float32)
    expert_out = routed_cols.astype(jnp.bfloat16)
    shared_out = shared_cols.astype(jnp.bfloat16)
    returned = lax.all_to_all(
        expert_out.reshape(members, groups * capacity, col_width),
        "expert",
        split_axis=0,
        concat_axis=0,
        tiled=True,
    )
    returned_scores = lax.all_to_all(
        gate_score.reshape(members, groups * capacity),
        "expert",
        split_axis=0,
        concat_axis=0,
        tiled=True,
    )
    group_offset = (jnp.arange(groups, dtype=jnp.int32) * capacity)[:, None, None]
    lookup = (routes_by_group * (groups * capacity) + group_offset + slots_by_group).reshape(
        groups * rows_dev, TOPK
    )
    picked = jnp.take(returned.reshape(-1, col_width), lookup, axis=0)
    picked_scores = jnp.take(returned_scores.reshape(-1), lookup, axis=0)
    route_weight = ROUTE_SCALE * picked_scores / jnp.sum(picked_scores, axis=1, keepdims=True)
    moe_cols = shared_out.astype(jnp.float32) + jnp.sum(
        route_weight[:, :, None] * picked.astype(jnp.float32), axis=1
    )
    moe_home = lax.all_to_all(
        moe_cols.reshape(groups, rows_dev, col_width).astype(jnp.bfloat16),
        "dp",
        split_axis=0,
        concat_axis=2,
        tiled=True,
    ).astype(jnp.float32)
    final = (hidden_up + moe_home[0]).astype(jnp.bfloat16)
    return (final[:pre_rows], final[pre_rows:])


def solution(mesh):
    in_specs = (
        P(("dp", "expert"), None, None),
        P(("dp", "expert"), None),
        P(("dp", "expert"), None),
        P(("dp", "expert"), None, None),
        P(("dp", "expert"), None),
        P(("dp", "expert"), None),
        P(("dp", "expert")),
        P(("dp", "expert"), None, None),
        P(),
        P("dp", "expert", None),
        P("dp", "expert", None),
        P(),
        P(None, "expert"),
        P(("dp", "expert"), None),
        P("expert", None, "dp"),
        P("expert", None, "dp"),
        P("expert", None, "dp"),
        P("expert", "dp"),
        P("expert", "dp"),
        P("expert", "dp"),
    )
    out_specs = (P(("dp", "expert"), None), P(("dp", "expert"), None))
    return jax.shard_map(shards, mesh=mesh, in_specs=in_specs, out_specs=out_specs, check_vma=False)
```

profile of v0, /device:TPU:0, one launch (start us, length us, event | category | flops | bytes accessed | tf_op | source)
XLA Modules:
  0.0 269.9 jit_solution(16119734852066937818)
XLA Ops:
  20.1 4.2 %all-to-all-start = ((bf16[17,16,512]{2,0,1:T(8,128)(2,1)}), bf16[17,16,512]{2,0,1:T(8,128)(2,1)S(1)}, u32[]{:S(2)}, u32[]{:S(2)}) async-start(bf16[17,16,512]{2,0,1:T(8,128)(2,1)} %copy.72), calls=%async_computation | async-start | bytes 786432 | tf_op jit(solution)/shard_map/all_to_all | solution.py:114
  25.0 6.9 %all-gather.2 = s32[2,17,6]{1,2,0:T(8,128)S(1)} all-gather(s32[1,17,6]{1,2,0:T(8,128)S(1)} %bitcast.131), channel_id=1, replica_groups=mesh['dp'=2,'expert'=16] {'dp'}, dimensions={0}, use_global_device_ids=true | all-gather | bytes 1224 | tf_op jit(solution)/shard_map/all_gather | solution.py:137
  34.0 15.8 %all-gather.10.cloned.1.call-done = bf16[8,512,128]{2,1,0:T(8,128)(2,1)} async-done(((bf16[8,32,128]{2,1,0:T(8,128)(2,1)}), bf16[8,512,128]{2,1,0:T(8,128)(2,1)}) %all-gather.10.cloned.1.call-update) | async-done | bytes 1048592 | tf_op jit(solution)/shard_map/all_gather | solution.py:116
  49.7 52.3 %all-gather.12.cloned.1.call-done = bf16[8,128,2048]{2,1,0:T(8,128)(2,1)} async-done(((bf16[8,8,2048]{2,1,0:T(8,128)(2,1)}), bf16[8,128,2048]{2,1,0:T(8,128)(2,1)}) %all-gather.12.cloned.1.call-update) | async-done | bytes 4194320 | tf_op jit(solution)/shard_map/all_gather | solution.py:117
  102.1 3.6 %fusion.7 = bf16[34,2048]{1,0:T(8,128)(2,1)S(1)} fusion(bf16[8,128,2048]{2,1,0:T(8,128)(2,1)} %all-gather.12.cloned.1.call-done, bf16[8,512,128]{2,1,0:T(8,128)(2,1)} %all-gather.10.cloned.1.call-done, bf16[34,8,512]{2,1,0:T(8,128)(2,1)S(1)} %bitcast.127), kind=kOutput, calls=%fused_computation.10 | convolution fusion | flops 178362368 | bytes 5660672 | tf_op jit(solution)/shard_map/thv,hvd->td/dot_general | solution.py:122
  105.6 7.8 %fusion = bf16[24,2048]{1,0:T(8,128)(2,1)S(1)} fusion(bf16[34,2048]{1,0:T(8,128)(2,1)S(1)} %fusion.7), kind=kCustom, calls=%all-reduce-scatter | all-reduce-scatter fusion | flops 98305 | bytes 238080
  113.5 2.4 collective-permute-start
  118.7 5.6 %all-gather = bf16[2,17,2048]{2,1,0:T(8,128)(2,1)S(1)} all-gather(bf16[1,17,2048]{2,1,0:T(8,128)(2,1)S(1)} %fusion.52), channel_id=1, replica_groups=mesh['dp'=2,'expert'=16] {'dp'}, dimensions={0}, use_global_device_ids=true | all-gather | bytes 208896 | tf_op jit(solution)/shard_map/all_gather | solution.py:136
  127.3 4.4 %all-to-all-start.1 = ((bf16[16,2,7,2048]{3,1,2,0:T(2,128)(2,1)}), bf16[16,2,7,2048]{3,1,2,0:T(2,128)(2,1)}, u32[]{:S(2)}, u32[]{:S(2)}) async-start(bf16[16,2,7,2048]{3,1,2,0:T(2,128)(2,1)} %copy.81), calls=%async_computation.1 | async-start | bytes 1835008 | tf_op jit(solution)/shard_map/all_to_all | solution.py:148
  132.5 28.0 %all-to-all-done.1 = bf16[16,2,7,2048]{3,1,2,0:T(2,128)(2,1)} async-done(((bf16[16,2,7,2048]{3,1,2,0:T(2,128)(2,1)}), bf16[16,2,7,2048]{3,1,2,0:T(2,128)(2,1)}, u32[]{:S(2)}, u32[]{:S(2)}) %all-to-all-start.1) | async-done | bytes 917536 | tf_op jit(solution)/shard_map/all_to_all | solution.py:148
  160.4 2.5 copy.82
  163.0 2.3 reshape.248
  167.6 5.9 %all-to-all-start.2 = ((f32[16,1,14]{2,1,0:T(1,128)}), f32[16,1,14]{2,1,0:T(1,128)S(1)}, u32[]{:S(2)}, u32[]{:S(2)}) async-start(f32[16,1,14]{2,1,0:T(1,128)} %bitcast.24), calls=%async_computation.2 | async-start | bytes 16384 | tf_op jit(solution)/shard_map/all_to_all | solution.py:180
  173.5 3.3 %fusion.5 = f32[224,704]{1,0:T(8,128)S(1)} fusion(bf16[224,2048]{1,0:T(8,128)(2,1)} %reshape.248, bf16[1,2048,704]{1,2,0:T(8,128)(2,1)} %param.34), kind=kOutput, calls=%fused_computation.6 | convolution fusion | flops 645922816 | bytes 4431872 | tf_op jit(solution)/shard_map/dot_general | solution.py:153
  177.9 11.4 %all-gather.3 = bf16[2,704,224]{1,2,0:T(8,128)(2,1)S(1)} all-gather(bf16[1,704,224]{1,2,0:T(8,128)(2,1)S(1)} %fusion.18), channel_id=1, replica_groups=mesh['dp'=2,'expert'=16] {'dp'}, dimensions={0}, use_global_device_ids=true | all-gather | bytes 946176 | tf_op jit(solution)/shard_map/all_gather | solution.py:167
  190.8 2.9 %reshape.282 = bf16[1408,224]{0,1:T(8,128)(2,1)} reshape(bf16[2,704,224]{1,0,2:T(2,128)(2,1)} %copy.88) | data formatting | bytes 1261568
  193.7 2.8 %fusion.11 = bf16[224,1024]{1,0:T(8,128)(2,1)} fusion(bf16[1408,224]{0,1:T(8,128)(2,1)} %reshape.282, bf16[1,1408,1024]{2,1,0:T(8,128)(2,1)S(1)} %copy-done), kind=kOutput, calls=%fused_computation.12 | convolution fusion | flops 646152192 | bytes 3973120 | tf_op jit(solution)/shard_map/dot_general | solution.py:169
  198.4 5.8 %all-to-all-start.3 = ((bf16[16,14,1024]{2,1,0:T(8,128)(2,1)}), bf16[16,14,1024]{2,1,0:T(8,128)(2,1)}, u32[]{:S(2)}, u32[]{:S(2)}) async-start(bf16[16,14,1024]{2,1,0:T(8,128)(2,1)} %reshape.250), calls=%async_computation.3 | async-start | bytes 1048576 | tf_op jit(solution)/shard_map/all_to_all | solution.py:173
  204.3 2.7 %fusion.91 = f32[34,704]{1,0:T(8,128)S(1)} fusion(bf16[34,2048]{1,0:T(8,128)(2,1)S(1)} %reshape.276, bf16[2048,704]{0,1:T(8,128)(2,1)} %all-gather.14.cloned.1.call-done), kind=kOutput, calls=%fused_computation.133 | convolution fusion | flops 98041856 | bytes 3118592 | tf_op jit(solution)/shard_map/dot_general | solution.py:162
  207.7 2.7 %fusion.35 = bf16[1,704,34]{1,2,0:T(8,128)(2,1)S(1)} fusion(bf16[34,2048]{1,0:T(8,128)(2,1)S(1)} %reshape.276, bf16[2048,704]{0,1:T(8,128)(2,1)} %all-gather.16.cloned.1.call-done, f32[34,704]{1,0:T(8,128)S(1)} %fusion.91), kind=kOutput, calls=%fused_computation.31 | convolution fusion | flops 98185472 | bytes 3166464 | tf_op jit(solution)/shard_map/dot_general | solution.py:163
  210.5 4.9 %all-gather.1 = bf16[2,704,34]{1,2,0:T(8,128)(2,1)S(1)} all-gather(bf16[1,704,34]{1,2,0:T(8,128)(2,1)S(1)} %fusion.35), channel_id=1, replica_groups=mesh['dp'=2,'expert'=16] {'dp'}, dimensions={0}, use_global_device_ids=true | all-gather | bytes 143616 | tf_op jit(solution)/shard_map/all_gather | solution.py:168
  226.6 26.0 %all-gather.18.cloned.1.call-done = bf16[1408,1024]{1,0:T(8,128)(2,1)} async-done(((bf16[88,1024]{1,0:T(8,128)(2,1)}), bf16[1408,1024]{1,0:T(8,128)(2,1)}) %all-gather.18.cloned.1.call-update) | async-done | bytes 2883600 | tf_op jit(solution)/shard_map/all_gather | solution.py:159
  252.5 2.4 fusion.26
  255.0 6.8 %all_to_all.46 = bf16[2,17,1024]{2,1,0:T(8,128)(2,1)S(1)} all-to-all(bf16[2,17,1024]{2,1,0:T(8,128)(2,1)S(1)} %convert_element_type.163), channel_id=1, replica_groups=mesh['dp'=2,'expert'=16] {'dp'}, dimensions={0} | all-to-all | bytes 139264 | tf_op jit(solution)/shard_map/all_to_all | solution.py:197
  (123 shorter events, 40.9 us)
Async XLA Ops:
  7.2 186.5 %copy-start = (bf16[1,1408,1024]{2,1,0:T(8,128)(2,1)S(1)}, bf16[1,1408,1024]{2,1,0:T(8,128)(2,1)}, u32[]{:S(2)}) copy-start(bf16[1,1408,1024]{2,1,0:T(8,128)(2,1)} %param.36) | copy-start | bytes 8650756
  7.2 11.6 %copy-start.8 = (f32[16]{0:T(128)S(1)}, f32[16]{0:T(128)}, u32[]{:S(2)}) copy-start(f32[16]{0:T(128)} %param.28) | copy-start | bytes 196
  7.2 11.6 %copy-start.13 = (bf16[16,576]{1,0:T(8,128)(2,1)S(1)}, bf16[16,576]{1,0:T(8,128)(2,1)}, u32[]{:S(2)}) copy-start(bf16[16,576]{1,0:T(8,128)(2,1)} %param.21) | copy-start | bytes 55300
  7.2 42.5 %all-gather.10.cloned.1.call-start = ((), (), s32[]{:S(2)}) async-start(), calls=%async_computation.5 | async-start | bytes 1114112 | tf_op jit(solution)/shard_map/all_gather | solution.py:116
  7.9 94.1 %all-gather.12.cloned.1.call-start = ((), (), s32[]{:S(2)}) async-start(), calls=%async_computation.6 | async-start | bytes 4456448 | tf_op jit(solution)/shard_map/all_gather | solution.py:117
  8.7 195.6 %all-gather.14.cloned.1.call-start = ((), (), s32[]{:S(2)}) async-start(), calls=%async_computation.7 | async-start | bytes 3063808 | tf_op jit(solution)/shard_map/all_gather | solution.py:157
  9.4 198.3 %all-gather.16.cloned.1.call-start = ((), (), s32[]{:S(2)}) async-start(), calls=%async_computation.8 | async-start | bytes 3063808 | tf_op jit(solution)/shard_map/all_gather | solution.py:158
  15.0 9.9 %copy-start.9 = (s32[17,6]{0,1:T(8,128)S(1)}, s32[17,6]{0,1:T(8,128)}, u32[]{:S(2)}) copy-start(s32[17,6]{0,1:T(8,128)} %param.33) | copy-start | bytes 1228
  20.1 13.7 %all-to-all-start = ((bf16[17,16,512]{2,0,1:T(8,128)(2,1)}), bf16[17,16,512]{2,0,1:T(8,128)(2,1)S(1)}, u32[]{:S(2)}, u32[]{:S(2)}) async-start(bf16[17,16,512]{2,0,1:T(8,128)(2,1)} %copy.72), calls=%async_computation | async-start | bytes 786432 | tf_op jit(solution)/shard_map/all_to_all | solution.py:114
  24.4 228.1 %all-gather.18.cloned.1.call-start = ((), (), s32[]{:S(2)}) async-start(), calls=%async_computation.9 | async-start | bytes 3063808 | tf_op jit(solution)/shard_map/all_gather | solution.py:159
  31.8 0.6 copy-start.2
  32.9 1.0 copy-start.5
  102.1 13.9 %copy-start.11 = (u32[32]{0:T(128)S(1)}, u32[32]{0:T(128)}, u32[]{:S(2)}) copy-start(u32[32]{0:T(128)} %constant.110) | copy-start | bytes 388
  102.1 15.3 %copy-start.10 = (bf16[2048]{0:T(1024)(128)(2,1)S(1)}, bf16[2048]{0:T(1024)(128)(2,1)}, u32[]{:S(2)}) copy-start(bf16[2048]{0:T(1024)(128)(2,1)} %param.31) | copy-start | bytes 12292
  102.1 15.6 %copy-start.4 = (bf16[16,2048]{1,0:T(8,128)(2,1)S(1)}, bf16[16,2048]{1,0:T(8,128)(2,1)}, u32[]{:S(2)}) copy-start(bf16[16,2048]{1,0:T(8,128)(2,1)} %param.22) | copy-start | bytes 196612
  113.5 4.0 %collective-permute-start = (bf16[7,2048]{1,0:T(8,128)(2,1)S(1)}, bf16[7,2048]{1,0:T(8,128)(2,1)S(1)}, u32[]{:S(2)}, u32[]{:S(2)}) collective-permute-start(bf16[7,2048]{1,0:T(8,128)(2,1)S(1)} %slice.56), channel_id=1, source_target_pairs={{0,16},{1,17},{2,18},{3,19},{4,20},{5,21},{6,22},{7,23},{8,24},{9,... | collective-permute-start | bytes 86024
  117.7 14.1 %copy-start.6 = (s32[2,102]{1,0:T(2,128)S(1)}, s32[2,102]{1,0:T(2,128)}, u32[]{:S(2)}) copy-start(s32[2,102]{1,0:T(2,128)} %copy-done.5) | copy-start | bytes 2452
  117.7 14.2 %copy-start.3 = (s32[2,17,6]{1,2,0:T(8,128)S(1)}, s32[2,17,6]{1,2,0:T(8,128)}, u32[]{:S(2)}) copy-start(s32[2,17,6]{1,2,0:T(8,128)} %copy-done.2) | copy-start | bytes 2452
  127.3 38.0 %copy-start.7 = (bf16[2048,1]{0,1:T(2,128)(2,1)S(1)}, bf16[2048,1]{0,1:T(2,128)(2,1)}, u32[]{:S(2)}) copy-start(bf16[2048,1]{0,1:T(2,128)(2,1)} %param.32) | copy-start | bytes 12292
  127.3 33.1 %all-to-all-start.1 = ((bf16[16,2,7,2048]{3,1,2,0:T(2,128)(2,1)}), bf16[16,2,7,2048]{3,1,2,0:T(2,128)(2,1)}, u32[]{:S(2)}, u32[]{:S(2)}) async-start(bf16[16,2,7,2048]{3,1,2,0:T(2,128)(2,1)} %copy.81), calls=%async_computation.1 | async-start | bytes 1835008 | tf_op jit(solution)/shard_map/all_to_all | solution.py:148
  167.6 30.9 %all-to-all-start.2 = ((f32[16,1,14]{2,1,0:T(1,128)}), f32[16,1,14]{2,1,0:T(1,128)S(1)}, u32[]{:S(2)}, u32[]{:S(2)}) async-start(f32[16,1,14]{2,1,0:T(1,128)} %bitcast.24), calls=%async_computation.2 | async-start | bytes 16384 | tf_op jit(solution)/shard_map/all_to_all | solution.py:180
  173.5 3.3 %copy-start.1 = (bf16[224,2048]{1,0:T(8,128)(2,1)S(1)}, bf16[224,2048]{1,0:T(8,128)(2,1)}, u32[]{:S(2)}) copy-start(bf16[224,2048]{1,0:T(8,128)(2,1)} %reshape.248) | copy-start | bytes 2752516
  173.5 3.3 %copy-start.12 = (bf16[1,2048,704]{1,2,0:T(8,128)(2,1)S(1)}, bf16[1,2048,704]{1,2,0:T(8,128)(2,1)}, u32[]{:S(2)}) copy-start(bf16[1,2048,704]{1,2,0:T(8,128)(2,1)} %param.35) | copy-start | bytes 8650756
  198.4 22.1 %all-to-all-start.3 = ((bf16[16,14,1024]{2,1,0:T(8,128)(2,1)}), bf16[16,14,1024]{2,1,0:T(8,128)(2,1)}, u32[]{:S(2)}, u32[]{:S(2)}) async-start(bf16[16,14,1024]{2,1,0:T(8,128)(2,1)} %reshape.250), calls=%async_computation.3 | async-start | bytes 1048576 | tf_op jit(solution)/shard_map/all_to_all | solution.py:173
Sparse Core Ops, SparseCore 0:
  10.2 39.5 all-gather.9
  51.9 50.0 all-gather.11
  104.2 56.5 all-gather.13
  162.8 44.8 all-gather.15
  209.9 42.6 all-gather.17
where the time goes:
time: 271 us; the launch traced here: 270 us
  waiting for transfers between devices  126 us (46%)
  blocking collectives  43.3 us (16%)
  local copies, waits for them, and re-layouts  28 us (10%)
  matrix products  27.4 us (10%)
  starting transfers between devices  23 us (8%)
  between operations  15.6 us (6%)
  other arithmetic  6.51 us (2%)
    all_gather x1, waiting for transfers between devices, shards(): lax.all_gather(out_weight, 'expert', axis=1, tiled=True)  52.3 us
    all_to_all x1, waiting for transfers between devices, shards(): lax.all_to_all(outgoing, 'expert', split_axis=0, concat_axis=0, tiled=True)  28 us
    all_gather x1, waiting for transfers between devices, shards(): lax.all_gather(shared_down, 'expert', axis=0, tiled=True)  26 us
    all_gather x1, waiting for transfers between devices, shards(): lax.all_gather(uv_weight, 'expert', axis=1, tiled=True)  15.8 us
    all_gather x1, blocking collectives, shards(): routed_piece = lax.all_gather(expert_act, 'dp', axis=1, tiled=True)  11.4 us
    unnamed x1, blocking collectives  7.8 us
    all_gather x1, blocking collectives, shards(): group_routes = lax.all_gather(routes, 'dp', axis=0, tiled=True)  6.86 us
    all_to_all x1, blocking collectives, shards(): lax.all_to_all(moe_cols.reshape(groups, rows_dev, col_width).astype(jnp.b...  6.84 us
  transfers between devices with their start and end apart: 10, of which 6 were waited for; matrix products, arithmetic and copies ran while one was open for 24% of the time, Pallas kernels for 0%

commit v1 on v0

--- a/solution.py
+++ b/solution.py
@@ -205,6 +205,423 @@
     return (final[:pre_rows], final[pre_rows:])
 
 
+OUTER = 4
+DEC_ROWS = 16
+
+
+def fold_row(row):
+    return row.reshape(row.shape[:-2] + (DEC_ROWS, row.shape[-1] // DEC_ROWS))
+
+
+def unfold_row(block):
+    return block.reshape(block.shape[:-2] + (block.shape[-2] * block.shape[-1],))
+
+
+def swap(value, axis, bit):
+    size = lax.axis_size(axis)
+    return lax.ppermute(value, axis, [(i, i ^ bit) for i in range(size)])
+
+
+def attention_rows(
+    pre_query, pre_latent, dec_query, dec_latent, cache_lengths, latent_cache, sink_logits
+):
+    pre_rows = pre_query.shape[0]
+    scale_qk = (QK_NOPE + ROPE) ** (-0.5)
+    pre_scores = (
+        jnp.einsum("thc,uc->thu", pre_query, pre_latent, preferred_element_type=jnp.float32)
+        * scale_qk
+    )
+    places = jnp.arange(pre_rows, dtype=jnp.int32)
+    allowed = (places[None, :] <= places[:, None])[:, None, :]
+    masked = jnp.where(allowed, pre_scores, NEG_FILL)
+    pre_max = jnp.maximum(jnp.max(masked, axis=2), sink_logits[None, :])
+    exp_terms = jnp.where(allowed, jnp.exp(masked - pre_max[:, :, None]), 0.0)
+    denominator = jnp.sum(exp_terms, axis=2) + jnp.exp(sink_logits[None, :] - pre_max)
+    numerator = jnp.einsum(
+        "thu,ul->thl",
+        exp_terms.astype(jnp.bfloat16),
+        pre_latent[:, :LATENT],
+        preferred_element_type=jnp.float32,
+    )
+    pre_att = (numerator / denominator[:, :, None]).astype(jnp.bfloat16)
+    window = latent_cache.shape[1]
+    slot_ids = jnp.arange(window, dtype=jnp.int32)
+    newest = cache_lengths - 1
+    position = newest[:, None] - jnp.mod(newest[:, None] - slot_ids[None, :], window)
+    usable = ((position >= 0) & (position > cache_lengths[:, None] - window))[:, None, :]
+    cache_scores = (
+        jnp.einsum("rhc,rsc->rhs", dec_query, latent_cache, preferred_element_type=jnp.float32)
+        * scale_qk
+    )
+    own_scores = (
+        jnp.einsum("rhc,rc->rh", dec_query, dec_latent, preferred_element_type=jnp.float32)
+        * scale_qk
+    )
+    cache_masked = jnp.where(usable, cache_scores, NEG_FILL)
+    top_score = jnp.maximum(
+        jnp.maximum(jnp.max(cache_masked, axis=2), own_scores), sink_logits[None, :]
+    )
+    cache_exp = jnp.where(usable, jnp.exp(cache_masked - top_score[:, :, None]), 0.0)
+    own_exp = jnp.exp(own_scores - top_score)
+    dec_numer = jnp.einsum(
+        "rhs,rsl->rhl",
+        cache_exp.astype(jnp.bfloat16),
+        latent_cache[:, :, :LATENT],
+        preferred_element_type=jnp.float32,
+    )
+    dec_numer = dec_numer + own_exp.astype(jnp.bfloat16).astype(jnp.float32)[
+        :, :, None
+    ] * dec_latent[:, None, :LATENT].astype(jnp.float32)
+    dec_total = jnp.sum(cache_exp, axis=2) + own_exp + jnp.exp(sink_logits[None, :] - top_score)
+    dec_att = (dec_numer / dec_total[:, :, None]).astype(jnp.bfloat16)
+    return pre_att, dec_att
+
+
+def normalize(hidden, norm_gain):
+    hidden_up = hidden.astype(jnp.float32)
+    mean_square = jnp.mean(hidden_up * hidden_up, axis=1, keepdims=True)
+    return (
+        hidden_up * lax.rsqrt(mean_square + NORM_EPS) * norm_gain.astype(jnp.float32)[None, :]
+    ).astype(jnp.bfloat16)
+
+
+def token_shards(
+    pre_query,
+    pre_latent,
+    pre_resid,
+    dec_query,
+    dec_latent,
+    dec_resid,
+    cache_lengths,
+    latent_cache,
+    sink_logits,
+    uv_weight,
+    out_weight,
+    norm_gain,
+    router,
+    routes,
+    gate_weight,
+    up_weight,
+    down_weight,
+    shared_gate,
+    shared_up,
+    shared_down,
+):
+    groups = lax.axis_size("dp")
+    members = lax.axis_size("expert")
+    inner = members // OUTER
+    homes = groups * members
+    me = lax.axis_index("expert")
+    my_group = lax.axis_index("dp")
+    my_outer = me // inner
+    pre_rows = pre_query.shape[0]
+    rows_dev = pre_rows + 1
+    capacity = max(2, (rows_dev * TOPK + members - 1) // members)
+
+    heads_dev, latent_rows, value_dim = uv_weight.shape
+    value_rows = out_weight.shape[1]
+    heads_outer = heads_dev // OUTER
+    out_blocks = out_weight.reshape(OUTER, heads_outer * value_rows, D)
+    uv_tiles = heads_outer * latent_rows // DEC_ROWS
+    uv_blocks = (
+        uv_weight.reshape(OUTER, uv_tiles, DEC_ROWS, value_dim)
+        .transpose(0, 2, 1, 3)
+        .reshape(OUTER, DEC_ROWS, uv_tiles * value_dim)
+    )
+    router_block = router[:, 0].reshape(DEC_ROWS, D // DEC_ROWS)
+    routes_low = routes.astype(jnp.bfloat16)
+    routes_block = jnp.concatenate(
+        [
+            routes_low[:pre_rows],
+            jnp.broadcast_to(routes_low[pre_rows:], (pre_rows, TOPK)),
+            jnp.zeros((pre_rows, 128 - 2 * TOPK), jnp.bfloat16),
+        ],
+        axis=1,
+    )
+    side = jnp.concatenate([router_block, routes_block], axis=1)
+    packed = jnp.concatenate(
+        [out_blocks, uv_blocks, jnp.broadcast_to(side[None], (OUTER,) + side.shape)], axis=2
+    )
+    pieces = [lax.dynamic_index_in_dim(packed, my_outer, 0, keepdims=True)]
+    for step in range(1, OUTER):
+        block = lax.dynamic_index_in_dim(packed, my_outer ^ step, 0, keepdims=True)
+        pieces.append(swap(block, "expert", step * inner))
+    gathered = jnp.concatenate(pieces, axis=0)
+    chain = [step * inner for step in range(OUTER)]
+    bit = inner // 2
+    while bit:
+        gathered = jnp.concatenate([gathered, swap(gathered, "expert", bit)], axis=0)
+        chain = chain + [offset | bit for offset in chain]
+        bit //= 2
+    chain_array = jnp.array(chain, jnp.int32)
+    holders = me ^ chain_array
+    out_rel = gathered[:, :, :D].reshape(heads_outer * members * value_rows, D)
+    uv_rel = (
+        gathered[:, :, D : D + uv_tiles * value_dim]
+        .reshape(members, DEC_ROWS, heads_outer, latent_rows // DEC_ROWS, value_dim)
+        .transpose(2, 0, 3, 1, 4)
+        .reshape(heads_outer, members * latent_rows, value_dim)
+    )
+    side_all = gathered[:, :, D + uv_tiles * value_dim :]
+    router_rel = side_all[:, :, : D // DEC_ROWS].reshape(members, D)
+    routes_plane = side_all[:, :, D // DEC_ROWS :]
+    routes_other = swap(routes_plane, "dp", 1)
+    latent_abs = jnp.arange(members * latent_rows, dtype=jnp.int32)
+    latent_rel_abs = (holders[:, None] * latent_rows + jnp.arange(latent_rows)[None, :]).reshape(-1)
+    latent_order = (latent_abs[:, None] == latent_rel_abs[None, :]).astype(jnp.bfloat16)
+    uv_full = jnp.einsum(
+        "ab,hbv->hav", latent_order, uv_rel, preferred_element_type=jnp.float32
+    ).astype(jnp.bfloat16)
+    value_ids = jnp.arange(heads_outer * value_dim, dtype=jnp.int32)
+    wanted = (
+        jnp.arange(heads_outer)[None, :, None] * value_dim
+        + holders[:, None, None] * value_rows
+        + jnp.arange(value_rows)[None, None, :]
+    ).reshape(-1)
+    value_order = (value_ids[:, None] == wanted[None, :]).astype(jnp.bfloat16)
+
+    units = shared_gate.shape[1] // members
+    depth = shared_gate.shape[0]
+    shared_cols = jnp.stack(
+        [shared_gate.T.reshape(members, units, depth), shared_up.T.reshape(members, units, depth)],
+        axis=1,
+    )
+    shared_got = lax.all_to_all(shared_cols, "expert", split_axis=0, concat_axis=0, tiled=True)
+    shared_in = shared_got.transpose(1, 2, 0, 3).reshape(2, units, members * depth)
+    half = members // 2
+    low = me < half
+    first, second = shared_down[:units], shared_down[units:]
+    down_a = lax.ppermute(
+        jnp.where(low, first, second),
+        "expert",
+        [(i, 2 * i if i < half else 2 * (i - half) + 1) for i in range(members)],
+    )
+    down_b = lax.ppermute(
+        jnp.where(low, second, first),
+        "expert",
+        [(i, 2 * i + 1 if i < half else 2 * (i - half)) for i in range(members)],
+    )
+    mine_first = (me % 2) == my_group
+    shared_down_own = jnp.where(mine_first, down_a, down_b)
+    shared_down_other = jnp.where(mine_first, down_b, down_a)
+
+    pre_att, dec_att = attention_rows(
+        pre_query, pre_latent, dec_query, dec_latent, cache_lengths, latent_cache, sink_logits
+    )
+    peers = groups * OUTER
+    heads_block = heads_outer * LATENT
+    att_blocks = jnp.concatenate(
+        [
+            pre_att.reshape(pre_rows, peers, heads_block).transpose(1, 0, 2),
+            fold_row(dec_att.reshape(peers, 1, heads_block)),
+        ],
+        axis=2,
+    )
+    lines = [
+        [g * members + o * inner + i for g in range(groups) for o in range(OUTER)]
+        for i in range(inner)
+    ]
+    both = ("dp", "expert")
+    att_got = lax.all_to_all(
+        att_blocks, both, split_axis=0, concat_axis=0, axis_index_groups=lines, tiled=True
+    )
+    att_rows = jnp.concatenate(
+        [
+            att_got[:, :, :heads_block].reshape(peers * pre_rows, heads_block),
+            unfold_row(att_got[:, :, heads_block:]),
+        ],
+        axis=0,
+    )
+    head_values = jnp.concatenate(
+        [
+            jnp.dot(
+                att_rows[:, h * LATENT : (h + 1) * LATENT],
+                uv_full[h],
+                preferred_element_type=jnp.float32,
+            ).astype(jnp.bfloat16)
+            for h in range(heads_outer)
+        ],
+        axis=1,
+    )
+    head_values = jnp.dot(
+        head_values, value_order, preferred_element_type=jnp.float32
+    ).astype(jnp.bfloat16)
+    head_partial = jnp.dot(head_values, out_rel, preferred_element_type=jnp.float32).astype(
+        jnp.bfloat16
+    )
+    split = peers * pre_rows
+    partial_blocks = jnp.concatenate(
+        [
+            head_partial[:split].reshape(peers, pre_rows, D),
+            fold_row(head_partial[split:].reshape(peers, 1, D)),
+        ],
+        axis=2,
+    )
+    partial_got = lax.all_to_all(
+        partial_blocks, both, split_axis=0, concat_axis=0, axis_index_groups=lines, tiled=True
+    )
+    attn_out = jnp.sum(partial_got.astype(jnp.float32), axis=0)
+    pre_hidden = (pre_resid.astype(jnp.float32) + attn_out[:, :D]).astype(jnp.bfloat16)
+    dec_hidden = (
+        dec_resid.astype(jnp.float32) + unfold_row(attn_out[:, D:])[None, :]
+    ).astype(jnp.bfloat16)
+    pre_hidden = lax.optimization_barrier(pre_hidden)
+    dec_hidden = lax.optimization_barrier(dec_hidden)
+    normed = jnp.concatenate(
+        [normalize(pre_hidden, norm_gain), fold_row(normalize(dec_hidden, norm_gain))], axis=1
+    )
+
+    blocks = [normed] + [swap(normed, "expert", step * inner) for step in range(1, OUTER)]
+    tags = [(0, step * inner) for step in range(OUTER)]
+    middle = OUTER // 2
+    bits = []
+    bit = inner // 2
+    while bit:
+        bits.append(bit)
+        bit //= 2
+
+    def widen(value, names, group_bit, member_bit):
+        if group_bit:
+            other = swap(value, "dp", 1)
+        else:
+            other = swap(value, "expert", member_bit)
+        return (
+            jnp.concatenate([value, other], axis=0),
+            names + [(g ^ group_bit, m ^ member_bit) for g, m in names],
+        )
+
+    half_a, tags_a = jnp.concatenate(blocks[:middle], axis=0), tags[:middle]
+    half_b, tags_b = jnp.concatenate(blocks[middle:], axis=0), tags[middle:]
+    half_a, tags_a = widen(half_a, tags_a, 0, bits[0])
+    half_b, tags_b = widen(half_b, tags_b, 1, 0)
+    half_a, tags_a = widen(half_a, tags_a, 1, 0)
+    half_b, tags_b = widen(half_b, tags_b, 0, bits[0])
+    rows_all, tags = jnp.concatenate([half_a, half_b], axis=0), tags_a + tags_b
+    for bit in bits[1:]:
+        rows_all, tags = widen(rows_all, tags, 0, bit)
+    pre_total = homes * pre_rows
+    tokens = jnp.concatenate(
+        [
+            rows_all[:, :D],
+            unfold_row(rows_all[:, D:].reshape(homes, DEC_ROWS, D // DEC_ROWS)),
+        ],
+        axis=0,
+    )
+    total = pre_total + homes
+
+    positions = [g * members + chain.index(m) for g, m in tags]
+    routes_all = jnp.concatenate([routes_plane, routes_other], axis=0)
+    routes_all = jnp.concatenate([routes_all[p : p + 1] for p in positions], axis=0)
+    token_routes = jnp.concatenate(
+        [
+            routes_all[:, :, :TOPK].reshape(pre_total, TOPK),
+            routes_all[:, 0, TOPK : 2 * TOPK],
+        ],
+        axis=0,
+    ).astype(jnp.int32)
+    chosen = jnp.sum(
+        (token_routes[:, :, None] == holders[None, None, :]).astype(jnp.float32), axis=1
+    )
+    mine = chosen[:, 0]
+    earlier = (
+        jnp.arange(total, dtype=jnp.int32)[:, None] <= jnp.arange(total, dtype=jnp.int32)[None, :]
+    ).astype(jnp.bfloat16)
+    home_group = jnp.array([g for g, _ in tags], jnp.int32) ^ my_group
+    home_member = jnp.array([m for _, m in tags], jnp.int32) ^ me
+    home_place = (
+        ((home_member ^ me) % 2) * (homes // 2) + home_group * (members // 2) + home_member // 2
+    )
+    place = jnp.concatenate(
+        [
+            (home_place[:, None] * pre_rows + jnp.arange(pre_rows)[None, :]).reshape(-1),
+            pre_total + home_place,
+        ]
+    )
+    reorder = (jnp.arange(total, dtype=jnp.int32)[:, None] == place[None, :]).astype(jnp.bfloat16)
+    mine_placed = jnp.dot(reorder, mine.astype(jnp.bfloat16), preferred_element_type=jnp.float32)
+    rank = jnp.dot(
+        mine_placed.astype(jnp.bfloat16)[None, :], earlier, preferred_element_type=jnp.float32
+    )
+    slots = homes * capacity
+    slot_ids = jnp.arange(1, slots + 1, dtype=jnp.float32)
+    gather = ((rank == slot_ids[:, None]) & (mine_placed[None, :] > 0.0)).astype(jnp.bfloat16)
+    scatter = gather.T
+    select = jnp.dot(gather, reorder, preferred_element_type=jnp.float32).astype(jnp.bfloat16)
+
+    shared_hidden = [
+        lax.dot_general(
+            tokens, shared_in[i], (((1,), (1,)), ((), ())), preferred_element_type=jnp.float32
+        )
+        for i in range(2)
+    ]
+    shared_act = (jax.nn.silu(shared_hidden[0]) * shared_hidden[1]).astype(jnp.bfloat16)
+    shared_act = jnp.dot(reorder, shared_act, preferred_element_type=jnp.float32).astype(
+        jnp.bfloat16
+    )
+    shared_act_other = swap(shared_act, "dp", 1)
+    expert_rows = jnp.dot(select, tokens, preferred_element_type=jnp.float32).astype(jnp.bfloat16)
+    scores = jax.nn.sigmoid(
+        lax.dot_general(
+            tokens, router_rel, (((1,), (1,)), ((), ())), preferred_element_type=jnp.float32
+        )
+    )
+    token_weight = ROUTE_SCALE * scores[:, 0] / jnp.sum(scores * chosen, axis=1)
+    slot_weight = jnp.sum(select.astype(jnp.float32) * token_weight[None, :], axis=1)
+    gate_proj = jnp.dot(expert_rows, gate_weight[0], preferred_element_type=jnp.float32)
+    up_proj = jnp.dot(expert_rows, up_weight[0], preferred_element_type=jnp.float32)
+    expert_act = (jax.nn.silu(gate_proj) * up_proj * slot_weight[:, None]).astype(jnp.bfloat16)
+    expert_act_other = swap(expert_act, "dp", 1)
+    width = gate_weight.shape[2]
+    down_own = lax.dynamic_slice_in_dim(down_weight[0], my_group * width, width, 0)
+    down_other = lax.dynamic_slice_in_dim(down_weight[0], (1 - my_group) * width, width, 0)
+    routed_cols = (
+        jnp.dot(expert_act, down_own, preferred_element_type=jnp.float32)
+        + jnp.dot(expert_act_other, down_other, preferred_element_type=jnp.float32)
+    ).astype(jnp.bfloat16)
+    cols = (
+        jnp.dot(scatter, routed_cols, preferred_element_type=jnp.float32)
+        + jnp.dot(shared_act, shared_down_own, preferred_element_type=jnp.float32)
+        + jnp.dot(shared_act_other, shared_down_other, preferred_element_type=jnp.float32)
+    )
+    col_width = cols.shape[1]
+    home_blocks = jnp.concatenate(
+        [
+            cols[:pre_total].reshape(homes, pre_rows, col_width),
+            fold_row(cols[pre_total:].reshape(homes, 1, col_width)),
+        ],
+        axis=2,
+    ).astype(jnp.bfloat16)
+    kept, sent = home_blocks[: homes // 2], home_blocks[homes // 2 :]
+    pair_sum = (kept.astype(jnp.float32) + swap(sent, "expert", 1).astype(jnp.float32)).astype(
+        jnp.bfloat16
+    )
+    halves = [
+        [g * members + 2 * i + b for g in range(groups) for i in range(members // 2)]
+        for b in range(2)
+    ]
+    home_got = lax.all_to_all(
+        pair_sum, both, split_axis=0, concat_axis=0, axis_index_groups=halves, tiled=True
+    )
+    home_sum = jnp.sum(
+        home_got.reshape((groups, members // 2) + home_got.shape[1:]).astype(jnp.float32), axis=1
+    )
+    pre_moe = jnp.concatenate([home_sum[g, :, :col_width] for g in range(groups)], axis=1)
+    dec_moe = unfold_row(home_sum[:, :, col_width:]).reshape(1, D)
+    pre_out = (pre_hidden.astype(jnp.float32) + pre_moe).astype(jnp.bfloat16)
+    dec_out = (dec_hidden.astype(jnp.float32) + dec_moe).astype(jnp.bfloat16)
+    return (pre_out, dec_out)
+
+
+def fits(mesh, heads, ff):
+    groups, members = mesh.shape["dp"], mesh.shape["expert"]
+    return (
+        groups == 2
+        and members % (2 * OUTER) == 0
+        and (heads // groups) % OUTER == 0
+        and ff % (groups * members) == 0
+    )
+
+
 def solution(mesh):
     in_specs = (
         P(("dp", "expert"), None, None),
@@ -229,4 +646,11 @@
         P("expert", "dp"),
     )
     out_specs = (P(("dp", "expert"), None), P(("dp", "expert"), None))
-    return jax.shard_map(shards, mesh=mesh, in_specs=in_specs, out_specs=out_specs, check_vma=False)
+
+    def layer(*args):
+        plan = token_shards if fits(mesh, args[9].shape[0], args[17].shape[1]) else shards
+        return jax.shard_map(
+            plan, mesh=mesh, in_specs=in_specs, out_specs=out_specs, check_vma=False
+        )(*args)
+
+    return layer

time: 271 us -> 192 us (0.71)
  waiting for transfers between devices: 126 us -> 18 us
  local copies, waits for them, and re-layouts: 28 us -> 60.2 us
  blocking collectives: 43.3 us -> 22 us
  starting transfers between devices: 23 us -> 38.5 us
  between operations: 15.6 us -> 2.77 us
  other arithmetic: 6.51 us -> 19.2 us
    all_gather x5 -> x0, waiting for transfers between devices: 94.8 us -> none  [the longest x1 52.3 us: shards(): lax.all_gather(out_weight, 'expert', axis=1, tiled=True)]
    all_gather x4 -> x0, blocking collectives: 28.7 us -> none  [the longest x1 11.4 us: shards(): routed_piece = lax.all_gather(expert_act, 'dp', axis=1, tiled=True)]
    ppermute x0 -> x19, starting transfers between devices: none -> 25.2 us  [the longest x17 21.6 us: swap(): return lax.ppermute(value, axis, [(i, i ^ bit) for i in range(size)])]
    unnamed x36 -> x84, local copies, waits for them, and re-layouts: 5.17 us -> 28.9 us
    all_to_all x4 -> x3, waiting for transfers between devices: 28 us -> 4.62 us  [the longest x1 2.96 us: token_shards(): lax.all_to_all(shared_cols, 'expert', split_axis=0, concat_axis=0, tiled=...]
    all_to_all x1, blocking collectives: 6.84 us -> 22 us  [token_shards(): lax.all_to_all(pair_sum, both, split_axis=0, concat_axis=0, axis_index_gr...]
    ppermute x0 -> x19, waiting for transfers between devices: none -> 13.4 us  [the longest x17 13.4 us: swap(): return lax.ppermute(value, axis, [(i, i ^ bit) for i in range(size)])]
    slice x3 -> x17, local copies, waits for them, and re-layouts: 2.13 us -> 12.3 us  [the longest x1 3.2 us: token_shards(): rows_all[:, :D]]
  transfers between devices with their start and end apart: 10 -> 22, of which waited for: 6 -> 10; matrix products, arithmetic and copies ran while one was open for 24% -> 50% of each run, Pallas kernels for 0% -> 0%
where the time goes in v1:
time: 192 us; the launch traced here: 190 us
  local copies, waits for them, and re-layouts  60.2 us (31%)
  starting transfers between devices  38.5 us (20%)
  matrix products  29.4 us (15%)
  blocking collectives  22 us (11%)
  other arithmetic  19.2 us (10%)
  waiting for transfers between devices  18 us (9%)
  between operations  2.77 us (1%)
    unnamed x84, local copies, waits for them, and re-layouts  28.9 us
    all_to_all x1, blocking collectives, token_shards(): lax.all_to_all(pair_sum, both, split_axis=0, concat_axis=0, axis_index_gr...  22 us
    ppermute x17, starting transfers between devices, swap(): return lax.ppermute(value, axis, [(i, i ^ bit) for i in range(size)])  21.6 us
    ppermute x17, waiting for transfers between devices, swap(): return lax.ppermute(value, axis, [(i, i ^ bit) for i in range(size)])  13.4 us
    all_to_all x1, starting transfers between devices, token_shards(): lax.all_to_all(att_blocks, both, split_axis=0, concat_axis=0, axis_index_...  6.05 us
    another operation x3, local copies, waits for them, and re-layouts, token_shards(): jnp.stack([shared_gate.T.reshape(members, units, depth), shared_up.T.resh...  4.4 us
    unnamed x4, other arithmetic  3.93 us
  transfers between devices with their start and end apart: 22, of which 10 were waited for; matrix products, arithmetic and copies ran while one was open for 50% of the time, Pallas kernels for 0%

profile of v1, /device:TPU:0, one launch (start us, length us, event | category | flops | bytes accessed | tf_op | source)
XLA Modules:
  0.0 190.1 jit_solution(8503555963601909390)
XLA Ops:
  5.6 3.0 %collective-permute-start = (bf16[1,16,2816]{2,1,0:T(8,128)(2,1)}, bf16[1,16,2816]{2,1,0:T(8,128)(2,1)}, u32[]{:S(2)}, u32[]{:S(2)}) collective-permute-start(bf16[1,16,2816]{2,1,0:T(8,128)(2,1)} %get-tuple-element.16), channel_id=1, source_target_pairs={{0,4},{1,5},{2,6},{3,7},{4,0},{5,1},{6,2},{7,3},{8,12},{9,13},{10,... | collective-permute-start | bytes 270344 | tf_op jit(solution)/shard_map/ppermute | solution.py:222
  8.6 2.6 %collective-permute-start.1 = (bf16[1,16,2816]{2,1,0:T(8,128)(2,1)}, bf16[1,16,2816]{2,1,0:T(8,128)(2,1)S(1)}, u32[]{:S(2)}, u32[]{:S(2)}) collective-permute-start(bf16[1,16,2816]{2,1,0:T(8,128)(2,1)} %get-tuple-element.15), channel_id=1, source_target_pairs={{0,8},{1,9},{2,10},{3,11},{4,12},{5,13},{6,14},{7,15},{8,0},{9,1},... | collective-permute-start | bytes 270344 | tf_op jit(solution)/shard_map/ppermute | solution.py:222
  19.9 6.1 %all-to-all-start = ((bf16[8,16,1088]{2,1,0:T(8,128)(2,1)}), bf16[8,16,1088]{2,1,0:T(8,128)(2,1)S(1)}, u32[]{:S(2)}, u32[]{:S(2)}) async-start(bf16[8,16,1088]{2,1,0:T(8,128)(2,1)} %pad_maximum_fusion.6), calls=%async_computation | async-start | bytes 589824 | tf_op jit(solution)/shard_map/all_to_all | solution.py:425
  27.6 2.1 %collective-permute-start.15 = (bf16[44,1024]{1,0:T(8,128)(2,1)}, bf16[44,1024]{1,0:T(8,128)(2,1)}, u32[]{:S(2)}, u32[]{:S(2)}) collective-permute-start(bf16[44,1024]{1,0:T(8,128)(2,1)} %get-tuple-element.24), channel_id=1, source_target_pairs={{0,0},{1,2},{2,4},{3,6},{4,8},{5,10},{6,12},{7,14},{8,1},{9,3},{10... | collective-permute-start | bytes 270344 | tf_op jit(solution)/shard_map/ppermute | solution.py:394
  41.4 4.0 %collective-permute-start.3 = (bf16[4,16,2816]{2,1,0:T(8,128)(2,1)}, bf16[4,16,2816]{2,1,0:T(8,128)(2,1)}, u32[]{:S(2)}, u32[]{:S(2)}) collective-permute-start(bf16[4,16,2816]{2,1,0:T(8,128)(2,1)} %pad_maximum_fusion.5), channel_id=1, source_target_pairs={{0,2},{1,3},{2,0},{3,1},{4,6},{5,7},{6,4},{7,5},{8,10},{9,11},{10,... | collective-permute-start | bytes 1081352 | tf_op jit(solution)/shard_map/ppermute | solution.py:222
  49.1 3.5 %all-to-all-start.2 = ((bf16[16,2,44,128]{3,1,2,0:T(2,128)(2,1)}), bf16[16,2,44,128]{3,1,2,0:T(2,128)(2,1)S(1)}, u32[]{:S(2)}, u32[]{:S(2)}) async-start(bf16[16,2,44,128]{3,1,2,0:T(2,128)(2,1)} %copy.75), calls=%async_computation.2 | async-start | bytes 720896 | tf_op jit(solution)/shard_map/all_to_all | solution.py:389
  52.6 1.8 collective-permute-done.3
  54.4 1.9 constant_dynamic-update-slice_fusion
  61.3 3.0 %all-to-all-done.2 = bf16[16,2,44,128]{3,1,2,0:T(2,128)(2,1)S(1)} async-done(((bf16[16,2,44,128]{3,1,2,0:T(2,128)(2,1)}), bf16[16,2,44,128]{3,1,2,0:T(2,128)(2,1)S(1)}, u32[]{:S(2)}, u32[]{:S(2)}) %all-to-all-start.2) | async-done | bytes 360480 | tf_op jit(solution)/shard_map/all_to_all | solution.py:389
  77.9 3.7 %all-to-all-start.1 = ((bf16[8,16,2176]{2,1,0:T(8,128)(2,1)}), bf16[8,16,2176]{2,1,0:T(8,128)(2,1)S(1)}, u32[]{:S(2)}, u32[]{:S(2)}) async-start(bf16[8,16,2176]{2,1,0:T(8,128)(2,1)} %pad_maximum_fusion.2), calls=%async_computation.1 | async-start | bytes 1114112 | tf_op jit(solution)/shard_map/all_to_all | solution.py:460
  102.1 2.4 %collective-permute-start.9 = (bf16[16,2176]{1,0:T(8,128)(2,1)S(1)}, bf16[16,2176]{1,0:T(8,128)(2,1)S(1)}, u32[]{:S(2)}, u32[]{:S(2)}) collective-permute-start(bf16[16,2176]{1,0:T(8,128)(2,1)S(1)} %get-tuple-element.45), channel_id=1, source_target_pairs={{0,8},{1,9},{2,10},{3,11},{4,12},{5,13},{6,14},{7,15},{8,0},{9,1},... | collective-permute-start | bytes 208904 | tf_op jit(solution)/shard_map/ppermute | solution.py:222
  104.5 1.9 %collective-permute-start.10 = (bf16[16,2176]{1,0:T(8,128)(2,1)S(1)}, bf16[16,2176]{1,0:T(8,128)(2,1)S(1)}, u32[]{:S(2)}, u32[]{:S(2)}) collective-permute-start(bf16[16,2176]{1,0:T(8,128)(2,1)S(1)} %get-tuple-element.45), channel_id=1, source_target_pairs={{0,12},{1,13},{2,14},{3,15},{4,8},{5,9},{6,10},{7,11},{8,4},{9,5},... | collective-permute-start | bytes 208904 | tf_op jit(solution)/shard_map/ppermute | solution.py:222
  107.7 3.0 %collective-permute-done.10 = bf16[16,2176]{1,0:T(8,128)(2,1)S(1)} collective-permute-done((bf16[16,2176]{1,0:T(8,128)(2,1)S(1)}, bf16[16,2176]{1,0:T(8,128)(2,1)S(1)}, u32[]{:S(2)}, u32[]{:S(2)}) %collective-permute-start.10) | collective-permute-done | bytes 69664 | tf_op jit(solution)/shard_map/ppermute | solution.py:222
  113.5 3.8 %collective-permute-done.11 = bf16[32,2176]{1,0:T(8,128)(2,1)S(1)} collective-permute-done((bf16[32,2176]{1,0:T(8,128)(2,1)S(1)}, bf16[32,2176]{1,0:T(8,128)(2,1)S(1)}, u32[]{:S(2)}, u32[]{:S(2)}) %collective-permute-start.11) | collective-permute-done | bytes 139296 | tf_op jit(solution)/shard_map/ppermute | solution.py:222
  118.7 1.8 collective-permute-done.8
  130.2 2.3 %constant_dynamic-update-slice_fusion.35 = bf16[512,2176]{1,0:T(8,128)(2,1)} fusion(bf16[512,2176]{1,0:T(8,128)(2,1)} %get-tuple-element.20, bf16[256,2176]{1,0:T(8,128)(2,1)} %collective-permute-done.13), kind=kLoop, calls=%fused_computation.152 | loop fusion | bytes 2228224 | tf_op jit(solution)/shard_map/concatenate | solution.py:489
  133.4 3.2 %slice.302 = bf16[512,2048]{1,0:T(8,128)(2,1)} slice(bf16[512,2176]{1,0:T(8,128)(2,1)} %constant_dynamic-update-slice_fusion.35), slice={[0:512], [0:2048]} | slice | bytes 4194304 | tf_op jit(solution)/shard_map/slice | solution.py:505
  136.7 2.5 %multiply_reduce_fusion.1 = (f32[544]{0:T(1024)S(1)}, f32[544,16]{0,1:T(8,128)S(1)}) fusion(f32[544,16]{0,1:T(8,128)S(1)} %convert_reduce_fusion.2, bf16[2,8,16,128]{3,2,1,0:T(8,128)(2,1)S(1)} %bitcast.162, bf16[32,2048]{1,0:T(8,128)(2,1)S(1)} %reshape_reshape.18, bf16[512,2048]{1,0:T(8,128)(2,1)} %slice.302), kind=kOutput, calls=%fused_computation.177 | convolution fusion | flops 40151008 | bytes 2365568 | tf_op jit(solution)/shard_map/dot_general | solution.py:564
  147.4 2.8 %fusion.38 = bf16[544,44]{0,1:T(8,128)(2,1)S(1)} fusion(s32[544]{0:T(1024)S(1)} %pad_add_fusion, f32[544,44]{0,1:T(8,128)} %fusion.131, bf16[44,2048]{1,0:T(8,128)(2,1)} %bitcast.154, bf16[32,2048]{1,0:T(8,128)(2,1)S(1)} %copy-done.12, bf16[512,2048]{1,0:T(8,128)(2,1)} %slice.302), kind=kOutput, calls=%fused_computation.40 | convolution fusion | flops 129004160 | bytes 2554240 | tf_op jit(solution)/shard_map/dot_general | solution.py:558
  152.5 2.7 %fusion.81 = f32[544,1024]{1,0:T(8,128)} fusion(bf16[544,44]{0,1:T(8,128)(2,1)S(1)} %fusion.38, bf16[44,1024]{1,0:T(8,128)(2,1)} %collective-permute-done.15, bf16[44,1024]{1,0:T(8,128)(2,1)} %collective-permute-done.16, pred[]{:T(512)S(6)} %eq.92), kind=kOutput, calls=%fused_computation.111 | convolution fusion | flops 49065984 | bytes 2456321 | tf_op jit(solution)/shard_map/dot_general | solution.py:583
  155.6 3.5 %fusion.30 = f32[544,1024]{1,0:T(8,128)} fusion(f32[224,1024]{1,0:T(8,128)} %fusion.6, bf16[224,704]{1,0:T(8,128)(2,1)} %collective-permute-done.14, bf16[1,1408,1024]{2,1,0:T(8,128)(2,1)S(1)} %copy-done, s32[]{:T(128)S(6)} %select_n.104, f32[544]{0:T(1024)S(1)} %fusion.50, f32[224]{0:T(256)S(1)} %copy-done.21, pred[544]{0:T(1024)(128)(4,1)S(1)} %broadcast_compare_fusion), kind=kOutput, calls=%fused_computation.26 | convolution fusion | flops 573224960 | bytes 4909060 | tf_op jit(solution)/shard_map/dot_general | solution.py:582
  159.1 2.8 %add_convert_fusion = bf16[544,1024]{1,0:T(8,128)(2,1)S(1)} fusion(f32[544,1024]{1,0:T(8,128)} %fusion.30, f32[544,1024]{1,0:T(8,128)} %fusion.81, bf16[544,44]{0,1:T(8,128)(2,1)S(1)} %collective-permute-done.17, bf16[44,1024]{1,0:T(8,128)(2,1)} %collective-permute-done.16, bf16[44,1024]{1,0:T(8,128)(2,1)} %collective-permute-done.15, pred[]{:T(512)S(6)} %eq.92), kind=kOutput, calls=%fused_computation.7 | convolution fusion | flops 50737152 | bytes 5798657 | tf_op jit(solution)/shard_map/dot_general | solution.py:584
  164.5 2.0 %collective-permute-done.18 = bf16[16,16,1088]{2,1,0:T(8,128)(2,1)S(1)} collective-permute-done((bf16[16,16,1088]{2,1,0:T(8,128)(2,1)S(1)}, bf16[16,16,1088]{2,1,0:T(8,128)(2,1)S(1)}, u32[]{:S(2)}, u32[]{:S(2)}) %collective-permute-start.18) | collective-permute-done | bytes 557088 | tf_op jit(solution)/shard_map/ppermute | solution.py:222
  166.6 22.0 %all_to_all.20 = bf16[16,16,1088]{2,1,0:T(8,128)(2,1)S(1)} all-to-all(bf16[16,16,1088]{2,1,0:T(8,128)(2,1)S(1)} %add_convert_fusion.1), channel_id=1, replica_groups={{0,2,4,6,8,10,12,14,16,18,20,22,24,26,28,30},{1,3,5,7,9,11,13,15,17,19,..., dimensions={0} | all-to-all | bytes 1114112 | tf_op jit(solution)/shard_map/all_to_all | solution.py:602
  (230 shorter events, 99.0 us)
Async XLA Ops:
  0.6 150.3 %copy-start = (bf16[1,1408,1024]{2,1,0:T(8,128)(2,1)S(1)}, bf16[1,1408,1024]{2,1,0:T(8,128)(2,1)}, u32[]{:S(2)}) copy-start(bf16[1,1408,1024]{2,1,0:T(8,128)(2,1)} %param.39) | copy-start | bytes 8650756
  5.6 34.1 %collective-permute-start = (bf16[1,16,2816]{2,1,0:T(8,128)(2,1)}, bf16[1,16,2816]{2,1,0:T(8,128)(2,1)}, u32[]{:S(2)}, u32[]{:S(2)}) collective-permute-start(bf16[1,16,2816]{2,1,0:T(8,128)(2,1)} %get-tuple-element.16), channel_id=1, source_target_pairs={{0,4},{1,5},{2,6},{3,7},{4,0},{5,1},{6,2},{7,3},{8,12},{9,13},{10,... | collective-permute-start | bytes 270344 | tf_op jit(solution)/shard_map/ppermute | solution.py:222
  8.6 31.1 %collective-permute-start.1 = (bf16[1,16,2816]{2,1,0:T(8,128)(2,1)}, bf16[1,16,2816]{2,1,0:T(8,128)(2,1)S(1)}, u32[]{:S(2)}, u32[]{:S(2)}) collective-permute-start(bf16[1,16,2816]{2,1,0:T(8,128)(2,1)} %get-tuple-element.15), channel_id=1, source_target_pairs={{0,8},{1,9},{2,10},{3,11},{4,12},{5,13},{6,14},{7,15},{8,0},{9,1},... | collective-permute-start | bytes 270344 | tf_op jit(solution)/shard_map/ppermute | solution.py:222
  11.2 28.5 %collective-permute-start.2 = (bf16[1,16,2816]{2,1,0:T(8,128)(2,1)}, bf16[1,16,2816]{2,1,0:T(8,128)(2,1)S(1)}, u32[]{:S(2)}, u32[]{:S(2)}) collective-permute-start(bf16[1,16,2816]{2,1,0:T(8,128)(2,1)} %get-tuple-element.14), channel_id=1, source_target_pairs={{0,12},{1,13},{2,14},{3,15},{4,8},{5,9},{6,10},{7,11},{8,4},{9,5},... | collective-permute-start | bytes 270344 | tf_op jit(solution)/shard_map/ppermute | solution.py:222
  19.9 28.4 %all-to-all-start = ((bf16[8,16,1088]{2,1,0:T(8,128)(2,1)}), bf16[8,16,1088]{2,1,0:T(8,128)(2,1)S(1)}, u32[]{:S(2)}, u32[]{:S(2)}) async-start(bf16[8,16,1088]{2,1,0:T(8,128)(2,1)} %pad_maximum_fusion.6), calls=%async_computation | async-start | bytes 589824 | tf_op jit(solution)/shard_map/all_to_all | solution.py:425
  27.6 124.8 %collective-permute-start.15 = (bf16[44,1024]{1,0:T(8,128)(2,1)}, bf16[44,1024]{1,0:T(8,128)(2,1)}, u32[]{:S(2)}, u32[]{:S(2)}) collective-permute-start(bf16[44,1024]{1,0:T(8,128)(2,1)} %get-tuple-element.24), channel_id=1, source_target_pairs={{0,0},{1,2},{2,4},{3,6},{4,8},{5,10},{6,12},{7,14},{8,1},{9,3},{10... | collective-permute-start | bytes 270344 | tf_op jit(solution)/shard_map/ppermute | solution.py:394
  29.8 122.7 %collective-permute-start.16 = (bf16[44,1024]{1,0:T(8,128)(2,1)}, bf16[44,1024]{1,0:T(8,128)(2,1)}, u32[]{:S(2)}, u32[]{:S(2)}) collective-permute-start(bf16[44,1024]{1,0:T(8,128)(2,1)} %get-tuple-element.23), channel_id=1, source_target_pairs={{0,1},{1,3},{2,5},{3,7},{4,9},{5,11},{6,13},{7,15},{8,0},{9,2},{10... | collective-permute-start | bytes 270344 | tf_op jit(solution)/shard_map/ppermute | solution.py:399
  41.4 13.0 %collective-permute-start.3 = (bf16[4,16,2816]{2,1,0:T(8,128)(2,1)}, bf16[4,16,2816]{2,1,0:T(8,128)(2,1)}, u32[]{:S(2)}, u32[]{:S(2)}) collective-permute-start(bf16[4,16,2816]{2,1,0:T(8,128)(2,1)} %pad_maximum_fusion.5), channel_id=1, source_target_pairs={{0,2},{1,3},{2,0},{3,1},{4,6},{5,7},{6,4},{7,5},{8,10},{9,11},{10,... | collective-permute-start | bytes 1081352 | tf_op jit(solution)/shard_map/ppermute | solution.py:222
  49.1 15.2 %all-to-all-start.2 = ((bf16[16,2,44,128]{3,1,2,0:T(2,128)(2,1)}), bf16[16,2,44,128]{3,1,2,0:T(2,128)(2,1)S(1)}, u32[]{:S(2)}, u32[]{:S(2)}) async-start(bf16[16,2,44,128]{3,1,2,0:T(2,128)(2,1)} %copy.75), calls=%async_computation.2 | async-start | bytes 720896 | tf_op jit(solution)/shard_map/all_to_all | solution.py:389
  56.3 10.0 %collective-permute-start.4 = (bf16[8,16,2816]{2,1,0:T(8,128)(2,1)}, bf16[8,16,2816]{2,1,0:T(8,128)(2,1)}, u32[]{:S(2)}, u32[]{:S(2)}) collective-permute-start(bf16[8,16,2816]{2,1,0:T(8,128)(2,1)} %get-tuple-element.12), channel_id=1, source_target_pairs={{0,1},{1,0},{2,3},{3,2},{4,5},{5,4},{6,7},{7,6},{8,9},{9,8},{10,11... | collective-permute-start | bytes 2162696 | tf_op jit(solution)/shard_map/ppermute | solution.py:222
  74.0 24.5 %copy-start.16 = (bf16[1,2048]{1,0:T(2,128)(2,1)S(1)}, bf16[1,2048]{1,0:T(2,128)(2,1)}, u32[]{:S(2)}) copy-start(bf16[1,2048]{1,0:T(2,128)(2,1)} %param.28) | copy-start | bytes 12292
  75.5 6.1 %collective-permute-start.5 = (bf16[16,16,128]{2,1,0:T(8,128)(2,1)}, bf16[16,16,128]{2,1,0:T(8,128)(2,1)}, u32[]{:S(2)}, u32[]{:S(2)}) collective-permute-start(bf16[16,16,128]{2,1,0:T(8,128)(2,1)} %get-tuple-element.9), channel_id=1, source_target_pairs={{0,16},{16,0},{1,17},{17,1},{2,18},{18,2},{3,19},{19,3},{4,20},{20... | collective-permute-start | bytes 196616 | tf_op jit(solution)/shard_map/ppermute | solution.py:222
  77.9 19.6 %all-to-all-start.1 = ((bf16[8,16,2176]{2,1,0:T(8,128)(2,1)}), bf16[8,16,2176]{2,1,0:T(8,128)(2,1)S(1)}, u32[]{:S(2)}, u32[]{:S(2)}) async-start(bf16[8,16,2176]{2,1,0:T(8,128)(2,1)} %pad_maximum_fusion.2), calls=%async_computation.1 | async-start | bytes 1114112 | tf_op jit(solution)/shard_map/all_to_all | solution.py:460
  100.7 5.7 %collective-permute-start.6 = (bf16[16,2176]{1,0:T(8,128)(2,1)S(1)}, bf16[16,2176]{1,0:T(8,128)(2,1)S(1)}, u32[]{:S(2)}, u32[]{:S(2)}) collective-permute-start(bf16[16,2176]{1,0:T(8,128)(2,1)S(1)} %get-tuple-element.45), channel_id=1, source_target_pairs={{0,4},{1,5},{2,6},{3,7},{4,0},{5,1},{6,2},{7,3},{8,12},{9,13},{10,... | collective-permute-start | bytes 208904 | tf_op jit(solution)/shard_map/ppermute | solution.py:222
  102.1 5.5 %collective-permute-start.9 = (bf16[16,2176]{1,0:T(8,128)(2,1)S(1)}, bf16[16,2176]{1,0:T(8,128)(2,1)S(1)}, u32[]{:S(2)}, u32[]{:S(2)}) collective-permute-start(bf16[16,2176]{1,0:T(8,128)(2,1)S(1)} %get-tuple-element.45), channel_id=1, source_target_pairs={{0,8},{1,9},{2,10},{3,11},{4,12},{5,13},{6,14},{7,15},{8,0},{9,1},... | collective-permute-start | bytes 208904 | tf_op jit(solution)/shard_map/ppermute | solution.py:222
  104.5 6.1 %collective-permute-start.10 = (bf16[16,2176]{1,0:T(8,128)(2,1)S(1)}, bf16[16,2176]{1,0:T(8,128)(2,1)S(1)}, u32[]{:S(2)}, u32[]{:S(2)}) collective-permute-start(bf16[16,2176]{1,0:T(8,128)(2,1)S(1)} %get-tuple-element.45), channel_id=1, source_target_pairs={{0,12},{1,13},{2,14},{3,15},{4,8},{5,9},{6,10},{7,11},{8,4},{9,5},... | collective-permute-start | bytes 208904 | tf_op jit(solution)/shard_map/ppermute | solution.py:222
  106.4 6.4 %collective-permute-start.7 = (bf16[32,2176]{1,0:T(8,128)(2,1)S(1)}, bf16[32,2176]{1,0:T(8,128)(2,1)S(1)}, u32[]{:S(2)}, u32[]{:S(2)}) collective-permute-start(bf16[32,2176]{1,0:T(8,128)(2,1)S(1)} %pad_maximum_fusion.11), channel_id=1, source_target_pairs={{0,2},{1,3},{2,0},{3,1},{4,6},{5,7},{6,4},{7,5},{8,10},{9,11},{10,... | collective-permute-start | bytes 417800 | tf_op jit(solution)/shard_map/ppermute | solution.py:222
  110.6 6.6 %collective-permute-start.11 = (bf16[32,2176]{1,0:T(8,128)(2,1)S(1)}, bf16[32,2176]{1,0:T(8,128)(2,1)S(1)}, u32[]{:S(2)}, u32[]{:S(2)}) collective-permute-start(bf16[32,2176]{1,0:T(8,128)(2,1)S(1)} %pad_maximum_fusion.12), channel_id=1, source_target_pairs={{0,16},{16,0},{1,17},{17,1},{2,18},{18,2},{3,19},{19,3},{4,20},{20... | collective-permute-start | bytes 417800 | tf_op jit(solution)/shard_map/ppermute | solution.py:222
  112.9 7.7 %collective-permute-start.8 = (bf16[64,2176]{1,0:T(8,128)(2,1)S(1)}, bf16[64,2176]{1,0:T(8,128)(2,1)S(1)}, u32[]{:S(2)}, u32[]{:S(2)}) collective-permute-start(bf16[64,2176]{1,0:T(8,128)(2,1)S(1)} %pad_maximum_fusion.7), channel_id=1, source_target_pairs={{0,16},{16,0},{1,17},{17,1},{2,18},{18,2},{3,19},{19,3},{4,20},{20... | collective-permute-start | bytes 835592 | tf_op jit(solution)/shard_map/ppermute | solution.py:222
  117.3 6.6 %collective-permute-start.12 = (bf16[64,2176]{1,0:T(8,128)(2,1)S(1)}, bf16[64,2176]{1,0:T(8,128)(2,1)S(1)}, u32[]{:S(2)}, u32[]{:S(2)}) collective-permute-start(bf16[64,2176]{1,0:T(8,128)(2,1)S(1)} %pad_maximum_fusion.8), channel_id=1, source_target_pairs={{0,2},{1,3},{2,0},{3,1},{4,6},{5,7},{6,4},{7,5},{8,10},{9,11},{10,... | collective-permute-start | bytes 835592 | tf_op jit(solution)/shard_map/ppermute | solution.py:222
  124.8 5.3 %collective-permute-start.13 = (bf16[256,2176]{1,0:T(8,128)(2,1)}, bf16[256,2176]{1,0:T(8,128)(2,1)}, u32[]{:S(2)}, u32[]{:S(2)}) collective-permute-start(bf16[256,2176]{1,0:T(8,128)(2,1)} %get-tuple-element.19), channel_id=1, source_target_pairs={{0,1},{1,0},{2,3},{3,2},{4,5},{5,4},{6,7},{7,6},{8,9},{9,8},{10,11... | collective-permute-start | bytes 3342344 | tf_op jit(solution)/shard_map/ppermute | solution.py:222
  144.6 11.0 %collective-permute-start.14 = (bf16[224,704]{1,0:T(8,128)(2,1)S(1)}, bf16[224,704]{1,0:T(8,128)(2,1)}, u32[]{:S(2)}, u32[]{:S(2)}) collective-permute-start(bf16[224,704]{1,0:T(8,128)(2,1)S(1)} %fusion.26), channel_id=1, source_target_pairs={{0,16},{16,0},{1,17},{17,1},{2,18},{18,2},{3,19},{19,3},{4,20},{20... | collective-permute-start | bytes 946184 | tf_op jit(solution)/shard_map/ppermute | solution.py:222
  150.1 9.0 %collective-permute-start.17 = (bf16[544,44]{0,1:T(8,128)(2,1)S(1)}, bf16[544,44]{0,1:T(8,128)(2,1)S(1)}, u32[]{:S(2)}, u32[]{:S(2)}) collective-permute-start(bf16[544,44]{0,1:T(8,128)(2,1)S(1)} %fusion.38), channel_id=1, source_target_pairs={{0,16},{16,0},{1,17},{17,1},{2,18},{18,2},{3,19},{19,3},{4,20},{20... | collective-permute-start | bytes 143624 | tf_op jit(solution)/shard_map/ppermute | solution.py:222
  164.4 2.1 %collective-permute-start.18 = (bf16[16,16,1088]{2,1,0:T(8,128)(2,1)S(1)}, bf16[16,16,1088]{2,1,0:T(8,128)(2,1)S(1)}, u32[]{:S(2)}, u32[]{:S(2)}) collective-permute-start(bf16[16,16,1088]{2,1,0:T(8,128)(2,1)S(1)} %pad_maximum_fusion.1), channel_id=1, source_target_pairs={{0,1},{1,0},{2,3},{3,2},{4,5},{5,4},{6,7},{7,6},{8,9},{9,8},{10,11... | collective-permute-start | bytes 1671176 | tf_op jit(solution)/shard_map/ppermute | solution.py:222
  (26 other events, 226.4 us)

commit v2 on v0

--- a/solution.py
+++ b/solution.py
@@ -3,6 +3,8 @@
 import jax
 import jax.numpy as jnp
 from jax import lax
+from jax.experimental import pallas as pl
+from jax.experimental.pallas import tpu as pltpu
 from jax.sharding import PartitionSpec as P
 
 D = 2048
@@ -205,6 +207,690 @@
     return (final[:pre_rows], final[pre_rows:])
 
 
+OUTER = 4
+TILE = 16
+LANES = 128
+ROWS_CONTRACT = (((1,), (1,)), ((), ()))
+
+
+def fold_row(row):
+    return row.reshape(row.shape[:-2] + (TILE, row.shape[-1] // TILE))
+
+
+def swap(value, axis, bit):
+    size = lax.axis_size(axis)
+    return lax.ppermute(value, axis, [(i, i ^ bit) for i in range(size)])
+
+
+def call(kernel, out_shapes, args, scratch=(), scalars=0, flops=0, vmem=10):
+    specs = [pl.BlockSpec(memory_space=pltpu.SMEM)] * scalars + [
+        pl.BlockSpec(memory_space=pltpu.VMEM)
+    ] * (len(args) - scalars)
+    moved = sum(a.size * a.dtype.itemsize for a in args)
+    single = not isinstance(out_shapes, (list, tuple))
+    return pl.pallas_call(
+        kernel,
+        out_shape=out_shapes,
+        in_specs=specs,
+        out_specs=pl.BlockSpec(memory_space=pltpu.VMEM)
+        if single
+        else [pl.BlockSpec(memory_space=pltpu.VMEM)] * len(out_shapes),
+        scratch_shapes=list(scratch),
+        compiler_params=pltpu.CompilerParams(vmem_limit_bytes=vmem * 1024 * 1024),
+        cost_estimate=pl.CostEstimate(flops=flops, bytes_accessed=moved, transcendentals=0),
+    )(*args)
+
+
+def low(shape):
+    return jax.ShapeDtypeStruct(shape, jnp.bfloat16)
+
+
+def pack_kernel(place_ref, out_ref, uv_ref, router_ref, routes_ref, *rest):
+    block_refs, (side_ref,) = rest[:OUTER], rest[OUTER:]
+    me = place_ref[0]
+    outer = me // place_ref[2]
+    heads = out_ref.shape[0] // OUTER
+    tiles = heads * uv_ref.shape[1] // TILE
+    side_ref[...] = jnp.zeros_like(side_ref)
+    for part in range(TILE):
+        side_ref[part : part + 1, :LANES] = router_ref[
+            :, part * LANES : (part + 1) * LANES
+        ].astype(jnp.float32)
+    choices, rows = routes_ref.shape
+    side_ref[:choices, LANES : LANES + rows] = routes_ref[...].astype(jnp.float32)
+    side = side_ref[...].astype(jnp.bfloat16)
+    for step in range(OUTER):
+        target = outer ^ step
+        block = block_refs[step]
+        block[0, :, :D] = out_ref[pl.ds(target * heads, heads)].reshape(TILE, D)
+        uv = uv_ref[pl.ds(target * heads, heads)].reshape(tiles * TILE, LANES)
+        for tile in range(tiles):
+            at = D + tile * LANES
+            block[0, :, at : at + LANES] = uv[tile * TILE : (tile + 1) * TILE]
+        block[0, :, D + tiles * LANES :] = side
+
+
+def spread_kernel(units, place_ref, gate_ref, up_ref, *block_refs):
+    me = place_ref[0]
+    inner = block_refs[0].shape[0]
+    padded = block_refs[0].shape[1] // 2
+    for step in range(OUTER):
+        block_refs[step][...] = jnp.zeros_like(block_refs[step])
+    for member in range(inner * OUTER):
+        offset = member ^ me
+        step, near = offset // inner, offset % inner
+        rows = slice(member * units, (member + 1) * units)
+        for outer in range(OUTER):
+
+            @pl.when(step == outer)
+            def _():
+                block_refs[outer][near, :units] = gate_ref[rows]
+                block_refs[outer][near, padded : padded + units] = up_ref[rows]
+
+
+def small_kernel(place_ref, kept_ref, far_ref, *rest):
+    router_refs, (small_ref, fold_ref) = rest[:-2], rest[-2:]
+    me = place_ref[0]
+    members = kept_ref.shape[0] + far_ref.shape[0]
+    small_ref[...] = jnp.zeros_like(small_ref)
+    half = LANES // 2
+    padded = kept_ref.shape[1] // 2
+    for member in range(members):
+        ref, i = (kept_ref, member) if member < members // 2 else (far_ref, member - members // 2)
+        holder = me ^ chain_offset(member, members)
+        lanes = pl.ds(pl.multiple_of(holder * LANES, LANES), LANES)
+        small_ref[:padded, lanes] = ref[i, :padded]
+        small_ref[half : half + padded, lanes] = ref[i, padded:]
+    row = 0
+    for ref in router_refs:
+        count = ref.shape[0] * TILE
+        fold_ref[row : row + count, :] = ref[...].reshape(count, LANES).astype(jnp.float32)
+        row += count
+    for part in range(TILE):
+        small_ref[LANES - members :, part * LANES : (part + 1) * LANES] = fold_ref[
+            pl.ds(part, members, stride=TILE), :
+        ].astype(jnp.bfloat16)
+
+
+def attend_kernel(
+    length_ref, query_ref, latent_ref, dec_query_ref, dec_latent_ref, cache_ref, sink_ref,
+    out_ref, rows_ref, dec_ref, fold_ref,
+):
+    span, heads, _ = query_ref.shape
+    scale_qk = (QK_NOPE + ROPE) ** (-0.5)
+    square = (heads, heads)
+    diagonal = lax.broadcasted_iota(jnp.int32, square, 0) == lax.broadcasted_iota(
+        jnp.int32, square, 1
+    )
+    sinks = jnp.sum(
+        jnp.where(diagonal, jnp.broadcast_to(sink_ref[...], square), 0.0), axis=1, keepdims=True
+    )
+    latent = latent_ref[...]
+    query = query_ref[...].reshape(span * heads, query_ref.shape[2])
+    scores = (
+        lax.dot_general(query, latent, ROWS_CONTRACT, preferred_element_type=jnp.float32) * scale_qk
+    )
+    token = lax.broadcasted_iota(jnp.int32, scores.shape, 0) // heads
+    allowed = lax.broadcasted_iota(jnp.int32, scores.shape, 1) <= token
+    masked = jnp.where(allowed, scores, NEG_FILL)
+    sink_rows = jnp.broadcast_to(sinks[None], (span, heads, 1)).reshape(span * heads, 1)
+    top = jnp.maximum(jnp.max(masked, axis=1, keepdims=True), sink_rows)
+    terms = jnp.where(allowed, jnp.exp(masked - top), 0.0)
+    total = jnp.sum(terms, axis=1, keepdims=True) + jnp.exp(sink_rows - top)
+    numer = jnp.dot(
+        terms.astype(jnp.bfloat16), latent[:, :LATENT], preferred_element_type=jnp.float32
+    )
+    attended = numer / total
+    per_block = heads // out_ref.shape[0]
+    parts = LATENT // LANES
+    for part in range(parts):
+        rows_ref[part] = attended[:, part * LANES : (part + 1) * LANES]
+        for head in range(heads):
+            at = (head % per_block) * LATENT + part * LANES
+            out_ref[head // per_block, :, at : at + LANES] = rows_ref[
+                part, pl.ds(head, span, stride=heads), :
+            ].astype(jnp.bfloat16)
+
+    window = cache_ref.shape[2]
+    length = length_ref[0]
+    slot = lax.broadcasted_iota(jnp.int32, (heads, window), 1)
+    position = length - 1 - lax.rem(length - 1 - slot + window, window)
+    usable = (position >= 0) & (position > length - window)
+    dec_query = dec_query_ref[0]
+    dec_latent = dec_latent_ref[...]
+    cache = cache_ref[0]
+    cache_scores = (
+        jnp.dot(dec_query, cache, preferred_element_type=jnp.float32) * scale_qk
+    )
+    own = (
+        jnp.sum(
+            dec_query.astype(jnp.float32) * dec_latent.astype(jnp.float32), axis=1, keepdims=True
+        )
+        * scale_qk
+    )
+    cache_masked = jnp.where(usable, cache_scores, NEG_FILL)
+    dec_top = jnp.maximum(
+        jnp.maximum(jnp.max(cache_masked, axis=1, keepdims=True), own), sinks
+    )
+    cache_exp = jnp.where(usable, jnp.exp(cache_masked - dec_top), 0.0)
+    own_exp = jnp.exp(own - dec_top)
+    dec_numer = lax.dot_general(
+        cache_exp.astype(jnp.bfloat16),
+        cache[:LATENT, :],
+        ROWS_CONTRACT,
+        preferred_element_type=jnp.float32,
+    )
+    dec_numer = dec_numer + own_exp.astype(jnp.bfloat16).astype(jnp.float32) * dec_latent[
+        :, :LATENT
+    ].astype(jnp.float32)
+    dec_total = jnp.sum(cache_exp, axis=1, keepdims=True) + own_exp + jnp.exp(sinks - dec_top)
+    dec_attended = dec_numer / dec_total
+    blocks = out_ref.shape[0]
+    fold_ref[...] = jnp.zeros_like(fold_ref)
+    for part in range(parts):
+        dec_ref[part] = dec_attended[:, part * LANES : (part + 1) * LANES]
+        for head in range(per_block):
+            fold_ref[pl.ds(head * parts + part, blocks, stride=TILE), :] = dec_ref[
+                part, pl.ds(head, blocks, stride=per_block), :
+            ]
+    out_ref[:, :, per_block * LATENT :] = (
+        fold_ref[...].astype(jnp.bfloat16).reshape(blocks, TILE, LANES)
+    )
+
+
+def project_kernel(place_ref, att_ref, *rest):
+    piece_refs, (out_ref, rows_ref, fold_ref, uv_ref) = rest[:-4], rest[-4:]
+    pieces = [(ref, i) for ref in piece_refs for i in range(ref.shape[0])]
+    me = place_ref[0]
+    blocks, span, width = att_ref.shape
+    width -= LANES
+    members = len(pieces)
+    heads = width // LATENT
+    latent_rows = LATENT // members
+    tiles = latent_rows // TILE
+    value_rows = TILE // heads
+    rows_ref[: blocks * span, :] = att_ref[:, :, :width].reshape(blocks * span, width)
+    fold_ref[...] = att_ref[:, :, width:].reshape(blocks * TILE, LANES).astype(jnp.float32)
+    dec_rows = jnp.concatenate(
+        [fold_ref[pl.ds(i, blocks, stride=TILE), :] for i in range(width // LANES)], axis=1
+    )
+    dec_rows = jnp.concatenate([dec_rows, jnp.zeros((TILE - blocks, width), jnp.float32)], axis=0)
+    rows_ref[blocks * span :, :] = dec_rows.astype(jnp.bfloat16)
+    for step in range(members):
+        holder = me ^ chain_offset(step, members)
+        for head in range(heads):
+            for tile in range(tiles):
+                at = D + (head * tiles + tile) * LANES
+                start = pl.multiple_of(head * LATENT + holder * latent_rows + tile * TILE, TILE)
+                ref, i = pieces[step]
+                uv_ref[pl.ds(start, TILE), :] = ref[i, :, at : at + LANES]
+    value = lax.broadcasted_iota(jnp.int32, (LANES, members * TILE), 0)
+    column = lax.broadcasted_iota(jnp.int32, (LANES, members * TILE), 1)
+    step = column // TILE
+    holder = chain_offset(step, members) ^ me
+    wanted = holder * value_rows + column % value_rows
+    column_head = (column % TILE) // value_rows
+    spread = []
+    for head in range(heads):
+        order = jnp.where((value == wanted) & (column_head == head), 1.0, 0.0).astype(jnp.bfloat16)
+        spread.append(
+            jnp.dot(
+                uv_ref[head * LATENT : (head + 1) * LATENT, :],
+                order,
+                preferred_element_type=jnp.float32,
+            ).astype(jnp.bfloat16)
+        )
+    head_values = jnp.dot(
+        rows_ref[...], jnp.concatenate(spread, axis=0), preferred_element_type=jnp.float32
+    ).astype(jnp.bfloat16)
+    out_rows = jnp.concatenate([ref[i, :, :D] for ref, i in pieces], axis=0)
+    partial_rows = jnp.dot(head_values, out_rows, preferred_element_type=jnp.float32)
+    split = blocks * span
+    out_ref[:, :, :D] = partial_rows[:split].astype(jnp.bfloat16).reshape(blocks, span, D)
+    for part in range(TILE):
+        fold_ref[pl.ds(part, blocks, stride=TILE), :] = partial_rows[
+            split : split + blocks, part * LANES : (part + 1) * LANES
+        ]
+    out_ref[:, :, D:] = fold_ref[...].astype(jnp.bfloat16).reshape(blocks, TILE, LANES)
+
+
+def chain_offset(step, members):
+    inner = members // OUTER
+    offset = (step % OUTER) * inner
+    rest = step // OUTER
+    bit = inner // 2
+    while bit:
+        offset = offset + (rest % 2) * bit
+        rest = rest // 2
+        bit //= 2
+    return offset
+
+
+def norm_kernel(partial_ref, resid_ref, gain_ref, hidden_ref, normed_ref):
+    summed = partial_ref[0].astype(jnp.float32)
+    for i in range(1, partial_ref.shape[0]):
+        summed = summed + partial_ref[i].astype(jnp.float32)
+    hidden = (resid_ref[...].astype(jnp.float32) + summed).astype(jnp.bfloat16)
+    hidden_ref[...] = hidden
+    hidden = hidden.astype(jnp.float32)
+    gain = gain_ref[...].astype(jnp.float32)
+    pre, dec = hidden[:, :D], hidden[:, D:]
+    pre_mean = jnp.sum(pre * pre, axis=1, keepdims=True) / D
+    dec_mean = jnp.sum(jnp.sum(dec * dec, axis=1, keepdims=True), axis=0, keepdims=True) / D
+    normed_ref[:, :D] = (pre * lax.rsqrt(pre_mean + NORM_EPS) * gain[:1, :D]).astype(jnp.bfloat16)
+    normed_ref[:, D:] = (dec * lax.rsqrt(dec_mean + NORM_EPS) * gain[:, D:]).astype(jnp.bfloat16)
+
+
+def expert_kernel(
+    units, small_ref, select_ref, chosen_ref, reorder_ref, gate_ref, up_ref, *rest
+):
+    piece_refs, (act_ref, shared_ref, fold_ref, pre_ref, dec_ref) = rest[:-5], rest[-5:]
+    pre_total = pre_ref.shape[0]
+    homes = pre_total // TILE
+    row = 0
+    for ref in piece_refs:
+        count = ref.shape[0]
+        pre_ref[row : row + count, :] = ref[:, :D]
+        fold_ref[row : row + count, :] = ref[:, D:].astype(jnp.float32)
+        row += count
+    for part in range(TILE):
+        dec_ref[:, part * LANES : (part + 1) * LANES] = fold_ref[
+            pl.ds(part, homes, stride=TILE), :
+        ].astype(jnp.bfloat16)
+    pre = pre_ref[...]
+    dec = dec_ref[...]
+    small = small_ref[...]
+    first = jnp.concatenate(
+        [
+            lax.dot_general(pre, small, ROWS_CONTRACT, preferred_element_type=jnp.float32),
+            lax.dot_general(dec, small, ROWS_CONTRACT, preferred_element_type=jnp.float32),
+        ],
+        axis=0,
+    )
+    half = LANES // 2
+    members = len(piece_refs)
+    gate_part = first[:, :units]
+    up_part = first[:, half : half + units]
+    shared_act = (gate_part / (1.0 + jnp.exp(-gate_part)) * up_part).astype(jnp.bfloat16)
+    shared_act = jnp.dot(
+        reorder_ref[...], shared_act, preferred_element_type=jnp.float32
+    ).astype(jnp.bfloat16)
+    total = shared_act.shape[0]
+    shared_ref[...] = jnp.zeros_like(shared_ref)
+    shared_ref[:, :units] = shared_act[: total // 2]
+    shared_ref[:, half : half + units] = shared_act[total // 2 :]
+    logits = first[:, LANES - members :]
+    scores = 1.0 / (1.0 + jnp.exp(-logits))
+    token_weight = (
+        ROUTE_SCALE * scores[:, :1] / jnp.sum(scores * chosen_ref[:, LANES - members :], axis=1, keepdims=True)
+    )
+    high = token_weight.astype(jnp.bfloat16)
+    rest = token_weight - high.astype(jnp.float32)
+    middle = rest.astype(jnp.bfloat16)
+    rest = (rest - middle.astype(jnp.float32)).astype(jnp.bfloat16)
+    select = select_ref[...]
+    weights = jnp.dot(
+        select, jnp.concatenate([high, middle, rest], axis=1), preferred_element_type=jnp.float32
+    )
+    slot_weight = jnp.sum(weights, axis=1, keepdims=True)
+    expert_rows = (
+        jnp.dot(select[:, :pre_total], pre, preferred_element_type=jnp.float32)
+        + jnp.dot(select[:, pre_total:], dec, preferred_element_type=jnp.float32)
+    ).astype(jnp.bfloat16)
+    gate = lax.dot_general(
+        expert_rows, gate_ref[0], ROWS_CONTRACT, preferred_element_type=jnp.float32
+    )
+    up = lax.dot_general(expert_rows, up_ref[0], ROWS_CONTRACT, preferred_element_type=jnp.float32)
+    act_ref[...] = (gate / (1.0 + jnp.exp(-gate)) * up * slot_weight).astype(jnp.bfloat16)
+
+
+def down_kernel(
+    place_ref, act_ref, act_other_ref, shared_ref, shared_other_ref, down_ref,
+    shared_down_ref, shared_down_other_ref, scatter_ref, kept_ref, sent_ref, fold_ref,
+):
+    group = place_ref[1]
+    width = act_ref.shape[1]
+    columns = down_ref.shape[2]
+    own = down_ref[0, pl.ds(pl.multiple_of(group * width, TILE), width), :]
+    other = down_ref[0, pl.ds(pl.multiple_of((1 - group) * width, TILE), width), :]
+    routed = (
+        jnp.dot(act_ref[...], own, preferred_element_type=jnp.float32)
+        + jnp.dot(act_other_ref[...], other, preferred_element_type=jnp.float32)
+    ).astype(jnp.bfloat16)
+    units = shared_down_ref.shape[0]
+
+    def down(at):
+        both = jnp.concatenate([shared_ref[:, at : at + units], shared_other_ref[:, at : at + units]], axis=1)
+        return jnp.dot(both, jnp.concatenate([shared_down_ref[...], shared_down_other_ref[...]], axis=0), preferred_element_type=jnp.float32)
+
+    total = (
+        jnp.dot(scatter_ref[...], routed, preferred_element_type=jnp.float32)
+        + jnp.concatenate([down(0), down(LANES // 2)], axis=0)
+    )
+    half = kept_ref.shape[0]
+    homes = 2 * half
+    split = homes * TILE
+    kept_ref[:, :, :columns] = (
+        total[: split // 2].astype(jnp.bfloat16).reshape(half, TILE, columns)
+    )
+    sent_ref[:, :, :columns] = (
+        total[split // 2 : split].astype(jnp.bfloat16).reshape(half, TILE, columns)
+    )
+    fold_ref[...] = jnp.zeros_like(fold_ref)
+    for part in range(columns // LANES):
+        fold_ref[pl.ds(part, homes, stride=TILE), :] = total[
+            split:, part * LANES : (part + 1) * LANES
+        ]
+    folded = fold_ref[...].astype(jnp.bfloat16)
+    kept_ref[:, :, columns:] = folded[: split // 2].reshape(half, TILE, LANES)
+    sent_ref[:, :, columns:] = folded[split // 2 :].reshape(half, TILE, LANES)
+
+
+def finish_kernel(got_ref, hidden_ref, pre_ref, dec_ref):
+    sources, _, width = got_ref.shape
+    columns = width - LANES
+    groups = D // columns
+    each = sources // groups
+    for group in range(groups):
+        summed = got_ref[group * each].astype(jnp.float32)
+        for i in range(1, each):
+            summed = summed + got_ref[group * each + i].astype(jnp.float32)
+        at = group * columns
+        pre_ref[:, at : at + columns] = (
+            hidden_ref[:, at : at + columns].astype(jnp.float32) + summed[:, :columns]
+        ).astype(jnp.bfloat16)
+        parts = columns // LANES
+        for part in range(parts):
+            row = group * parts + part
+            dec_ref[:, row * LANES : (row + 1) * LANES] = (
+                hidden_ref[row : row + 1, D:].astype(jnp.float32)
+                + summed[part : part + 1, columns:]
+            ).astype(jnp.bfloat16)
+
+
+def token_shards(
+    pre_query,
+    pre_latent,
+    pre_resid,
+    dec_query,
+    dec_latent,
+    dec_resid,
+    cache_lengths,
+    latent_cache,
+    sink_logits,
+    uv_weight,
+    out_weight,
+    norm_gain,
+    router,
+    routes,
+    gate_weight,
+    up_weight,
+    down_weight,
+    shared_gate,
+    shared_up,
+    shared_down,
+):
+    groups = lax.axis_size("dp")
+    members = lax.axis_size("expert")
+    inner = members // OUTER
+    homes = groups * members
+    me = lax.axis_index("expert")
+    my_group = lax.axis_index("dp")
+    place_ids = jnp.stack([me, my_group, jnp.int32(inner)]).astype(jnp.int32)
+    pre_rows = pre_query.shape[0]
+    rows_dev = pre_rows + 1
+    capacity = max(2, (rows_dev * TOPK + members - 1) // members)
+
+    heads_dev, latent_rows, value_dim = uv_weight.shape
+    heads_outer = heads_dev // OUTER
+    uv_tiles = heads_outer * latent_rows // TILE
+    block_width = D + uv_tiles * value_dim + 2 * LANES
+    blocks = call(
+        pack_kernel,
+        [low((1, TILE, block_width))] * OUTER,
+        [place_ids, out_weight, uv_weight, router.T, routes.T],
+        scratch=[pltpu.VMEM((TILE, 2 * LANES), jnp.float32)],
+        scalars=1,
+    )
+    pair_bit = inner // 2
+    near = [blocks[0]] + [swap(blocks[i], "expert", i * inner) for i in range(1, OUTER)]
+    own_pair = swap(blocks[0], "expert", pair_bit)
+    line = jnp.concatenate(near, axis=0)
+    far_pair = swap(line[1:], "expert", pair_bit)
+    pieces = [line, own_pair, far_pair]
+    pieces = pieces + [swap(piece, "expert", 1) for piece in pieces]
+    chain = [chain_offset(step, members) for step in range(members)]
+    holders = me ^ jnp.array(chain, jnp.int32)
+    side_at = D + uv_tiles * value_dim
+    router_blocks = [piece[:, :, side_at : side_at + LANES] for piece in pieces]
+    routes_plane = jnp.concatenate(
+        [piece[:, :TOPK, side_at + LANES : side_at + LANES + rows_dev] for piece in pieces], axis=0
+    )
+    routes_other = swap(routes_plane, "dp", 1)
+
+    pre_query, blocks = lax.optimization_barrier((pre_query, blocks))
+    peers = groups * OUTER
+    heads_block = heads_outer * LATENT
+    att_blocks = call(
+        attend_kernel,
+        low((peers, pre_rows, heads_block + LANES)),
+        [
+            cache_lengths, pre_query, pre_latent, dec_query, dec_latent,
+            latent_cache.swapaxes(1, 2),
+            sink_logits.reshape(1, -1),
+        ],
+        scratch=[
+            pltpu.VMEM((LATENT // LANES, pre_rows * pre_query.shape[1], LANES), jnp.float32),
+            pltpu.VMEM((LATENT // LANES, pre_query.shape[1], LANES), jnp.float32),
+            pltpu.VMEM((peers * TILE, LANES), jnp.float32),
+        ],
+        scalars=1,
+        flops=100_000_000,
+    )
+    lines = [
+        [g * members + o * inner + i for g in range(groups) for o in range(OUTER)]
+        for i in range(inner)
+    ]
+    both = ("dp", "expert")
+    att_got = lax.all_to_all(
+        att_blocks, both, split_axis=0, concat_axis=0, axis_index_groups=lines, tiled=True
+    )
+    partial_blocks = call(
+        project_kernel,
+        low((peers, pre_rows, D + LANES)),
+        [place_ids, att_got, *pieces],
+        scratch=[
+            pltpu.VMEM((peers * pre_rows + TILE, heads_block), jnp.bfloat16),
+            pltpu.VMEM((peers * TILE, LANES), jnp.float32),
+            pltpu.VMEM((heads_block, value_dim), jnp.bfloat16),
+        ],
+        scalars=1,
+        flops=300_000_000,
+    )
+
+    units = shared_gate.shape[1] // members
+    padded = -(-units // TILE) * TILE
+    depth = shared_gate.shape[0]
+    shared_gate, shared_up, line = lax.optimization_barrier((shared_gate, shared_up, line))
+    spread = call(
+        partial(spread_kernel, units),
+        [low((inner, 2 * padded, depth))] * OUTER,
+        [place_ids, shared_gate.T, shared_up.T],
+        scalars=1,
+    )
+    shared_got = [spread[0]] + [swap(spread[i], "expert", i * inner) for i in range(1, OUTER)]
+    kept = jnp.concatenate([block[:pair_bit] for block in shared_got], axis=0)
+    sent = jnp.concatenate([block[pair_bit:] for block in shared_got], axis=0)
+    far = swap(sent, "expert", pair_bit)
+    shared_kept = jnp.concatenate([kept[::pair_bit], far[::pair_bit]], axis=0)
+    shared_sent = jnp.concatenate([kept[1::pair_bit], far[1::pair_bit]], axis=0)
+    shared_far = swap(shared_sent, "expert", 1)
+    small = call(
+        small_kernel,
+        low((LANES, D)),
+        [place_ids, shared_kept, shared_far, *router_blocks],
+        scratch=[pltpu.VMEM((members * TILE, LANES), jnp.float32)],
+        scalars=1,
+    )
+    partial_got = lax.all_to_all(
+        partial_blocks, both, split_axis=0, concat_axis=0, axis_index_groups=lines, tiled=True
+    )
+    shared_down, att_blocks = lax.optimization_barrier((shared_down, att_blocks))
+    half = members // 2
+    lower = me < half
+    first, second = shared_down[:units], shared_down[units:]
+    down_a = lax.ppermute(
+        jnp.where(lower, first, second),
+        "expert",
+        [(i, 2 * i if i < half else 2 * (i - half) + 1) for i in range(members)],
+    )
+    down_b = lax.ppermute(
+        jnp.where(lower, second, first),
+        "expert",
+        [(i, 2 * i + 1 if i < half else 2 * (i - half)) for i in range(members)],
+    )
+    mine_first = (me % 2) == my_group
+    shared_down_own = jnp.where(mine_first, down_a, down_b)
+    shared_down_other = jnp.where(mine_first, down_b, down_a)
+
+    middle = OUTER // 2
+    pair_bit = inner // 2
+    tags_a = [(0, step * inner) for step in range(middle)]
+    tags_b = [(0, step * inner) for step in range(middle, OUTER)]
+    tags = []
+    for last in range(2):
+        for which, group_bit, member_bit in (
+            (tags_a, 0, 0), (tags_b, 0, 0), (tags_a, 0, 1), (tags_b, 1, 0),
+            (tags_a, 1, 0), (tags_b, 0, 1), (tags_a, 1, 1), (tags_b, 1, 1),
+        ):
+            tags += [(g ^ group_bit, m ^ (member_bit * pair_bit) ^ last) for g, m in which]
+    pre_total = homes * pre_rows
+    total = pre_total + homes
+
+    positions = [g * members + chain.index(m) for g, m in tags]
+    routes_all = jnp.concatenate([routes_plane, routes_other], axis=0)
+    routes_all = jnp.stack([routes_all[p] for p in positions], axis=0)
+    token_routes = jnp.concatenate(
+        [
+            routes_all[:, :, :pre_rows].transpose(0, 2, 1).reshape(pre_total, TOPK),
+            routes_all[:, :, pre_rows],
+        ],
+        axis=0,
+    ).astype(jnp.int32)
+    lane_expert = jnp.concatenate([jnp.full((LANES - members,), -1, jnp.int32), holders])
+    chosen = jnp.sum(
+        (token_routes[:, :, None] == lane_expert[None, None, :]).astype(jnp.float32), axis=1
+    )
+    mine = jnp.sum((token_routes == me).astype(jnp.float32), axis=1)
+    earlier = (
+        jnp.arange(total, dtype=jnp.int32)[:, None] <= jnp.arange(total, dtype=jnp.int32)[None, :]
+    ).astype(jnp.bfloat16)
+    home_group = jnp.array([g for g, _ in tags], jnp.int32) ^ my_group
+    home_member = jnp.array([m for _, m in tags], jnp.int32) ^ me
+    home_place = (
+        ((home_member ^ me) % 2) * (homes // 2) + home_group * (members // 2) + home_member // 2
+    )
+    place = jnp.concatenate(
+        [
+            (home_place[:, None] * pre_rows + jnp.arange(pre_rows)[None, :]).reshape(-1),
+            pre_total + home_place,
+        ]
+    )
+    reorder = (jnp.arange(total, dtype=jnp.int32)[:, None] == place[None, :]).astype(jnp.bfloat16)
+    mine_placed = jnp.dot(reorder, mine.astype(jnp.bfloat16), preferred_element_type=jnp.float32)
+    rank = jnp.dot(
+        mine_placed.astype(jnp.bfloat16)[None, :], earlier, preferred_element_type=jnp.float32
+    )
+    slots = homes * capacity
+    slot_ids = jnp.arange(1, slots + 1, dtype=jnp.float32)
+    gather = ((rank == slot_ids[:, None]) & (mine_placed[None, :] > 0.0)).astype(jnp.bfloat16)
+    scatter = gather.T
+    select = jnp.dot(gather, reorder, preferred_element_type=jnp.float32).astype(jnp.bfloat16)
+
+    (
+        partial_got, select, scatter, reorder, chosen, small, shared_down_own, shared_down_other
+    ) = lax.optimization_barrier(
+        (
+            partial_got, select, scatter, reorder, chosen, small, shared_down_own,
+            shared_down_other,
+        )
+    )
+    resid = jnp.concatenate([pre_resid, fold_row(dec_resid)], axis=1)
+    gain = jnp.concatenate(
+        [jnp.broadcast_to(norm_gain[None], (TILE, D)), norm_gain.reshape(TILE, LANES)], axis=1
+    )
+    hidden, normed = call(
+        norm_kernel, [low(resid.shape)] * 2, [partial_got, resid, gain], flops=1_000_000
+    )
+
+    line = [normed] + [swap(normed, "expert", step * inner) for step in range(1, OUTER)]
+    middle = OUTER // 2
+    row_pieces = []
+    for part in (line[:middle], line[middle:]):
+        row_pieces.append(jnp.concatenate(part, axis=0))
+    piece_a, piece_b = row_pieces
+    a_pair, b_group = swap(piece_a, "expert", pair_bit), swap(piece_b, "dp", 1)
+    a_group, b_pair = swap(piece_a, "dp", 1), swap(piece_b, "expert", pair_bit)
+    a_both, b_both = swap(a_pair, "dp", 1), swap(b_group, "expert", pair_bit)
+    row_pieces = [piece_a, piece_b, a_pair, b_group, a_group, b_pair, a_both, b_both]
+    row_pieces = row_pieces + [swap(piece, "expert", 1) for piece in row_pieces]
+
+    width = gate_weight.shape[2]
+    expert_act, shared_act = call(
+        partial(expert_kernel, units),
+        [low((slots, width)), low((total // 2, LANES))],
+        [
+            small, select, chosen, reorder, gate_weight.swapaxes(1, 2), up_weight.swapaxes(1, 2),
+            *row_pieces,
+        ],
+        scratch=[
+            pltpu.VMEM((pre_total, LANES), jnp.float32),
+            pltpu.VMEM((pre_total, D), jnp.bfloat16),
+            pltpu.VMEM((homes, D), jnp.bfloat16),
+        ],
+        flops=3_000_000_000,
+        vmem=20,
+    )
+    expert_act_other = swap(expert_act, "dp", 1)
+    shared_act_other = swap(shared_act, "dp", 1)
+    col_width = down_weight.shape[2]
+    kept, sent = call(
+        down_kernel,
+        [low((homes // 2, TILE, col_width + LANES))] * 2,
+        [
+            place_ids, expert_act, expert_act_other, shared_act, shared_act_other, down_weight,
+            shared_down_own, shared_down_other, scatter,
+        ],
+        scratch=[pltpu.VMEM((pre_total, LANES), jnp.float32)],
+        scalars=1,
+        flops=1_000_000_000,
+        vmem=20,
+    )
+    pair_sum = (kept.astype(jnp.float32) + swap(sent, "expert", 1).astype(jnp.float32)).astype(
+        jnp.bfloat16
+    )
+    halves = [
+        [g * members + 2 * i + b for g in range(groups) for i in range(members // 2)]
+        for b in range(2)
+    ]
+    home_got = lax.all_to_all(
+        pair_sum, both, split_axis=0, concat_axis=0, axis_index_groups=halves, tiled=True
+    )
+    return tuple(
+        call(finish_kernel, [low(pre_resid.shape), low(dec_resid.shape)], [home_got, hidden])
+    )
+
+
+def fits(mesh, heads, ff):
+    groups, members = mesh.shape["dp"], mesh.shape["expert"]
+    return (
+        groups == 2
+        and members % (2 * OUTER) == 0
+        and (heads // groups) % OUTER == 0
+        and ff % (groups * members) == 0
+    )
+
+
 def solution(mesh):
     in_specs = (
         P(("dp", "expert"), None, None),
@@ -229,4 +915,11 @@
         P("expert", "dp"),
     )
     out_specs = (P(("dp", "expert"), None), P(("dp", "expert"), None))
-    return jax.shard_map(shards, mesh=mesh, in_specs=in_specs, out_specs=out_specs, check_vma=False)
+
+    def layer(*args):
+        plan = token_shards if fits(mesh, args[9].shape[0], args[17].shape[1]) else shards
+        return jax.shard_map(
+            plan, mesh=mesh, in_specs=in_specs, out_specs=out_specs, check_vma=False
+        )(*args)
+
+    return layer

time: 271 us -> 157 us (0.58)
  waiting for transfers between devices: 126 us -> 36.8 us
  matrix products: 27.4 us -> 2.52 us
  blocking collectives: 43.3 us -> 21.5 us
  starting transfers between devices: 23 us -> 43.6 us
  Pallas kernels: 0 us -> 15 us
  between operations: 15.6 us -> 1.91 us
    all_gather x5 -> x0, waiting for transfers between devices: 94.8 us -> none  [the longest x1 52.3 us: shards(): lax.all_gather(out_weight, 'expert', axis=1, tiled=True)]
    ppermute x0 -> x36, waiting for transfers between devices: none -> 34.5 us  [the longest x34 34.5 us: swap(): return lax.ppermute(value, axis, [(i, i ^ bit) for i in range(size)])]
    ppermute x0 -> x36, starting transfers between devices: none -> 33.6 us  [the longest x34 32.9 us: swap(): return lax.ppermute(value, axis, [(i, i ^ bit) for i in range(size)])]
    all_gather x4 -> x0, blocking collectives: 28.7 us -> none  [the longest x1 11.4 us: shards(): routed_piece = lax.all_gather(expert_act, 'dp', axis=1, tiled=True)]
    all_to_all x4 -> x2, waiting for transfers between devices: 28 us -> 2.26 us  [the longest x1 2.26 us: token_shards(): lax.all_to_all(partial_blocks, both, split_axis=0, concat_axis=0, axis_in...]
    dot_general x14 -> x3, matrix products: 27.4 us -> 2.52 us  [the longest x1 1.27 us: token_shards(): jnp.dot(gather, reorder, preferred_element_type=jnp.float32)]
    unnamed x36 -> x93, local copies, waits for them, and re-layouts: 5.17 us -> 25.5 us
    pallas_call x0 -> x9, Pallas kernels: none -> 15 us  [call(): pl.pallas_call(kernel, out_shape=out_shapes, in_specs=specs, out_specs=pl...]
  transfers between devices with their start and end apart: 10 -> 38, of which waited for: 6 -> 13; matrix products, arithmetic and copies ran while one was open for 24% -> 12% of each run, Pallas kernels for 0% -> 4%
where the time goes in v2:
time: 157 us; the launch traced here: 156 us
  starting transfers between devices  43.6 us (28%)
  waiting for transfers between devices  36.8 us (23%)
  local copies, waits for them, and re-layouts  30.4 us (19%)
  blocking collectives  21.5 us (14%)
  Pallas kernels  15 us (10%)
  other arithmetic  4.21 us (3%)
  matrix products  2.52 us (2%)
  between operations  1.91 us (1%)
    ppermute x34, waiting for transfers between devices, swap(): return lax.ppermute(value, axis, [(i, i ^ bit) for i in range(size)])  34.5 us
    ppermute x34, starting transfers between devices, swap(): return lax.ppermute(value, axis, [(i, i ^ bit) for i in range(size)])  32.9 us
    unnamed x93, local copies, waits for them, and re-layouts  25.5 us
    all_to_all x1, blocking collectives, token_shards(): lax.all_to_all(pair_sum, both, split_axis=0, concat_axis=0, axis_index_gr...  21.5 us
    pallas_call x9, Pallas kernels, call(): pl.pallas_call(kernel, out_shape=out_shapes, in_specs=specs, out_specs=pl...  15 us
    all_to_all x1, starting transfers between devices, token_shards(): lax.all_to_all(att_blocks, both, split_axis=0, concat_axis=0, axis_index_...  5.97 us
    all_to_all x1, starting transfers between devices, token_shards(): lax.all_to_all(partial_blocks, both, split_axis=0, concat_axis=0, axis_in...  4.06 us
  transfers between devices with their start and end apart: 38, of which 13 were waited for; matrix products, arithmetic and copies ran while one was open for 12% of the time, Pallas kernels for 4%

profile of v2, /device:TPU:0, one launch (start us, length us, event | category | flops | bytes accessed | tf_op | source)
XLA Modules:
  0.0 155.9 jit_solution(14337654420965630634)
XLA Ops:
  4.5 3.1 %collective-permute-start = (bf16[1,16,2816]{2,1,0:T(8,128)(2,1)S(1)}, bf16[1,16,2816]{2,1,0:T(8,128)(2,1)S(1)}, u32[]{:S(2)}, u32[]{:S(2)}) collective-permute-start(bf16[1,16,2816]{2,1,0:T(8,128)(2,1)S(1)} %get-tuple-element.29), channel_id=1, source_target_pairs={{0,4},{1,5},{2,6},{3,7},{4,0},{5,1},{6,2},{7,3},{8,12},{9,13},{10,... | collective-permute-start | bytes 270344 | tf_op jit(solution)/shard_map/ppermute | solution.py:222
  7.6 2.6 %collective-permute-start.1 = (bf16[1,16,2816]{2,1,0:T(8,128)(2,1)S(1)}, bf16[1,16,2816]{2,1,0:T(8,128)(2,1)S(1)}, u32[]{:S(2)}, u32[]{:S(2)}) collective-permute-start(bf16[1,16,2816]{2,1,0:T(8,128)(2,1)S(1)} %get-tuple-element.30), channel_id=1, source_target_pairs={{0,8},{1,9},{2,10},{3,11},{4,12},{5,13},{6,14},{7,15},{8,0},{9,1},... | collective-permute-start | bytes 270344 | tf_op jit(solution)/shard_map/ppermute | solution.py:222
  17.6 1.9 %shard_map.231 = bf16[8,16,1152]{2,1,0:T(8,128)(2,1)} custom-call(s32[1]{0:T(128)S(6)} %copy.57.length_ref, bf16[16,16,576]{2,1,0:T(8,128)(2,1)S(1)} %copy-done.2, bf16[16,576]{1,0:T(8,128)(2,1)S(1)} %copy-done.13, bf16[1,16,576]{2,1,0:T(8,128)(2,1)S(1)} %copy-done.14, bf16[1,576]{1,0:T(2,128)(2,1)S(1)} %copy-done.23, bf16[1,576,1024]{2,1,0:T(8,128)(2,1)S(1)} %bitcast.19, ...), custom_call_target="tpu_custom_call" | custom-call | flops 100000000 | bytes 1512644 | tf_op jit(solution)/shard_map/pallas_call | solution.py:231
  19.5 6.0 %all-to-all-start = ((bf16[8,16,1152]{2,1,0:T(8,128)(2,1)}), bf16[8,16,1152]{2,1,0:T(8,128)(2,1)S(1)}, u32[]{:S(2)}, u32[]{:S(2)}) async-start(bf16[8,16,1152]{2,1,0:T(8,128)(2,1)} %shard_map.231), calls=%async_computation | async-start | bytes 589824 | tf_op jit(solution)/shard_map/all_to_all | solution.py:695
  28.7 2.5 %collective-permute-start.5 = (bf16[4,16,2816]{2,1,0:T(8,128)(2,1)S(1)}, bf16[4,16,2816]{2,1,0:T(8,128)(2,1)S(1)}, u32[]{:S(2)}, u32[]{:S(2)}) collective-permute-start(bf16[4,16,2816]{2,1,0:T(8,128)(2,1)S(1)} %constant_dynamic-update-slice_fusion.rest_0_), channel_id=1, source_target_pairs={{0,1},{1,0},{2,3},{3,2},{4,5},{5,4},{6,7},{7,6},{8,9},{9,8},{10,11... | collective-permute-start | bytes 1081352 | tf_op jit(solution)/shard_map/ppermute | solution.py:222
  31.3 2.4 %collective-permute-start.4 = (bf16[3,16,2816]{2,1,0:T(8,128)(2,1)S(1)}, bf16[3,16,2816]{2,1,0:T(8,128)(2,1)S(1)}, u32[]{:S(2)}, u32[]{:S(2)}) collective-permute-start(bf16[3,16,2816]{2,1,0:T(8,128)(2,1)S(1)} %pad_maximum_fusion), channel_id=1, source_target_pairs={{0,2},{1,3},{2,0},{3,1},{4,6},{5,7},{6,4},{7,5},{8,10},{9,11},{10,... | collective-permute-start | bytes 811016 | tf_op jit(solution)/shard_map/ppermute | solution.py:222
  34.8 2.9 %collective-permute-start.9 = (bf16[4,96,128]{2,1,0:T(8,128)(2,1)S(1)}, bf16[4,96,128]{2,1,0:T(8,128)(2,1)S(1)}, u32[]{:S(2)}, u32[]{:S(2)}) collective-permute-start(bf16[4,96,128]{2,1,0:T(8,128)(2,1)S(1)} %get-tuple-element.36), channel_id=1, source_target_pairs={{0,4},{1,5},{2,6},{3,7},{4,0},{5,1},{6,2},{7,3},{8,12},{9,13},{10,... | collective-permute-start | bytes 294920 | tf_op jit(solution)/shard_map/ppermute | solution.py:222
  39.6 1.9 %collective-permute-start.11 = (bf16[4,96,128]{2,1,0:T(8,128)(2,1)S(1)}, bf16[4,96,128]{2,1,0:T(8,128)(2,1)S(1)}, u32[]{:S(2)}, u32[]{:S(2)}) collective-permute-start(bf16[4,96,128]{2,1,0:T(8,128)(2,1)S(1)} %get-tuple-element.38), channel_id=1, source_target_pairs={{0,12},{1,13},{2,14},{3,15},{4,8},{5,9},{6,10},{7,11},{8,4},{9,5},... | collective-permute-start | bytes 294920 | tf_op jit(solution)/shard_map/ppermute | solution.py:222
  42.1 6.3 %collective-permute-done.10 = bf16[4,96,128]{2,1,0:T(8,128)(2,1)S(1)} collective-permute-done((bf16[4,96,128]{2,1,0:T(8,128)(2,1)S(1)}, bf16[4,96,128]{2,1,0:T(8,128)(2,1)S(1)}, u32[]{:S(2)}, u32[]{:S(2)}) %collective-permute-start.10) | collective-permute-done | bytes 98336 | tf_op jit(solution)/shard_map/ppermute | solution.py:222
  50.8 4.6 %collective-permute-done.12 = bf16[8,96,128]{2,1,0:T(8,128)(2,1)S(1)} collective-permute-done((bf16[8,96,128]{2,1,0:T(8,128)(2,1)S(1)}, bf16[8,96,128]{2,1,0:T(8,128)(2,1)S(1)}, u32[]{:S(2)}, u32[]{:S(2)}) %collective-permute-start.12) | collective-permute-done | bytes 196640 | tf_op jit(solution)/shard_map/ppermute | solution.py:222
  62.4 2.3 %shard_map.232 = bf16[8,16,2176]{2,1,0:T(8,128)(2,1)} custom-call(s32[3]{0:T(128)S(1)} %copy-done.16, bf16[8,16,1152]{2,1,0:T(8,128)(2,1)S(1)} %all-to-all-done.att_ref, bf16[4,16,2816]{2,1,0:T(8,128)(2,1)S(1)} %constant_dynamic-update-slice_fusion.rest_0_, bf16[1,16,2816]{2,1,0:T(8,128)(2,1)S(1)} %copy-done.9, ...), custom_call_target="tpu_custom_call" | custom-call | flops 300000000 | bytes 1736716 | tf_op jit(solution)/shard_map/pallas_call | solution.py:231
  64.7 4.1 %all-to-all-start.1 = ((bf16[8,16,2176]{2,1,0:T(8,128)(2,1)}), bf16[8,16,2176]{2,1,0:T(8,128)(2,1)S(1)}, u32[]{:S(2)}, u32[]{:S(2)}) async-start(bf16[8,16,2176]{2,1,0:T(8,128)(2,1)} %shard_map.232), calls=%async_computation.1 | async-start | bytes 1114112 | tf_op jit(solution)/shard_map/all_to_all | solution.py:735
  83.0 2.3 %all-to-all-done.1.partial_ref = bf16[8,16,2176]{2,1,0:T(8,128)(2,1)S(1)} async-done(((bf16[8,16,2176]{2,1,0:T(8,128)(2,1)}), bf16[8,16,2176]{2,1,0:T(8,128)(2,1)S(1)}, u32[]{:S(2)}, u32[]{:S(2)}) %all-to-all-start.1) | async-done | bytes 557088 | tf_op jit(solution)/shard_map/all_to_all | solution.py:735
  87.1 2.8 %collective-permute-start.16 = (bf16[16,2176]{1,0:T(8,128)(2,1)S(1)}, bf16[16,2176]{1,0:T(8,128)(2,1)S(1)}, u32[]{:S(2)}, u32[]{:S(2)}) collective-permute-start(bf16[16,2176]{1,0:T(8,128)(2,1)S(1)} %get-tuple-element.45), channel_id=1, source_target_pairs={{0,4},{1,5},{2,6},{3,7},{4,0},{5,1},{6,2},{7,3},{8,12},{9,13},{10,... | collective-permute-start | bytes 208904 | tf_op jit(solution)/shard_map/ppermute | solution.py:222
  89.9 3.0 %collective-permute-done.16 = bf16[16,2176]{1,0:T(8,128)(2,1)S(1)} collective-permute-done((bf16[16,2176]{1,0:T(8,128)(2,1)S(1)}, bf16[16,2176]{1,0:T(8,128)(2,1)S(1)}, u32[]{:S(2)}, u32[]{:S(2)}) %collective-permute-start.16) | collective-permute-done | bytes 69664 | tf_op jit(solution)/shard_map/ppermute | solution.py:222
  97.2 2.3 %collective-permute-done.21.rest_4_ = bf16[32,2176]{1,0:T(8,128)(2,1)S(1)} collective-permute-done((bf16[32,2176]{1,0:T(8,128)(2,1)S(1)}, bf16[32,2176]{1,0:T(8,128)(2,1)S(1)}, u32[]{:S(2)}, u32[]{:S(2)}) %collective-permute-start.21) | collective-permute-done | bytes 139296 | tf_op jit(solution)/shard_map/ppermute | solution.py:222
  99.5 2.1 %collective-permute-start.23 = (bf16[32,2176]{1,0:T(8,128)(2,1)S(1)}, bf16[32,2176]{1,0:T(8,128)(2,1)S(1)}, u32[]{:S(2)}, u32[]{:S(2)}) collective-permute-start(bf16[32,2176]{1,0:T(8,128)(2,1)S(1)} %collective-permute-done.19.rest_2_), channel_id=1, source_target_pairs={{0,16},{16,0},{1,17},{17,1},{2,18},{18,2},{3,19},{19,3},{4,20},{20... | collective-permute-start | bytes 417800 | tf_op jit(solution)/shard_map/ppermute | solution.py:222
  103.0 2.6 %collective-permute-done.23.rest_6_ = bf16[32,2176]{1,0:T(8,128)(2,1)S(1)} collective-permute-done((bf16[32,2176]{1,0:T(8,128)(2,1)S(1)}, bf16[32,2176]{1,0:T(8,128)(2,1)S(1)}, u32[]{:S(2)}, u32[]{:S(2)}) %collective-permute-start.23) | collective-permute-done | bytes 139296 | tf_op jit(solution)/shard_map/ppermute | solution.py:222
  108.6 1.8 %copy-done.25 = bf16[1,2048,704]{1,2,0:T(8,128)(2,1)S(1)} copy-done((bf16[1,2048,704]{1,2,0:T(8,128)(2,1)S(1)}, bf16[1,2048,704]{1,2,0:T(8,128)(2,1)}, u32[]{:S(2)}) %copy-start.25) | copy-done | bytes 2883608
  112.3 5.5 %shard_map.236 = (bf16[224,704]{1,0:T(8,128)(2,1)S(1)}, bf16[272,128]{1,0:T(8,128)(2,1)S(1)}) custom-call(bf16[128,2048]{1,0:T(8,128)(2,1)S(1)} %shard_map.234.small_ref, bf16[224,544]{1,0:T(8,128)(2,1)S(1)} %fusion.4.select_ref, f32[544,128]{1,0:T(8,128)S(1)} %convert_reduce_fusion.chosen_ref, bf16[544,544]{1,0:T(8,128)(2,1)S(1)} %fusion.reorder_ref, ...), custom_call_target="tpu_custom_call" | custom-call | flops 3000000000 | bytes 9633792 | tf_op jit(solution)/shard_map/pallas_call | solution.py:231
  119.8 9.6 %collective-permute-done.34.shared_other_ref = bf16[272,128]{1,0:T(8,128)(2,1)S(1)} collective-permute-done((bf16[272,128]{1,0:T(8,128)(2,1)S(1)}, bf16[272,128]{1,0:T(8,128)(2,1)S(1)}, u32[]{:S(2)}, u32[]{:S(2)}) %collective-permute-start.34) | collective-permute-done | bytes 69664 | tf_op jit(solution)/shard_map/ppermute | solution.py:222
  129.4 2.0 %shard_map.237 = (bf16[16,16,1152]{2,1,0:T(8,128)(2,1)S(1)}, bf16[16,16,1152]{2,1,0:T(8,128)(2,1)S(1)}) custom-call(s32[3]{0:T(128)S(1)} %copy-done.18, bf16[224,704]{1,0:T(8,128)(2,1)S(1)} %get-tuple-element.46.act_ref, bf16[224,704]{1,0:T(8,128)(2,1)S(1)} %collective-permute-done.33.act_other_ref, bf16[272,128]{1,0:T(8,128)(2,1)S(1)} %get-tuple-element.47.shared_ref, ...), custom_call_target="tpu_custom_call" | custom-call | flops 1000000000 | bytes 4077580 | tf_op jit(solution)/shard_map/pallas_call | solution.py:231
  131.5 2.0 %collective-permute-done.35 = bf16[16,16,1152]{2,1,0:T(8,128)(2,1)S(1)} collective-permute-done((bf16[16,16,1152]{2,1,0:T(8,128)(2,1)S(1)}, bf16[16,16,1152]{2,1,0:T(8,128)(2,1)S(1)}, u32[]{:S(2)}, u32[]{:S(2)}) %collective-permute-start.35) | collective-permute-done | bytes 589856 | tf_op jit(solution)/shard_map/ppermute | solution.py:222
  133.7 21.5 %all_to_all.15.got_ref = bf16[16,16,1152]{2,1,0:T(8,128)(2,1)S(1)} all-to-all(bf16[16,16,1152]{2,1,0:T(8,128)(2,1)S(1)} %add_convert_fusion), channel_id=1, replica_groups={{0,2,4,6,8,10,12,14,16,18,20,22,24,26,28,30},{1,3,5,7,9,11,13,15,17,19,..., dimensions={0} | all-to-all | bytes 1179648 | tf_op jit(solution)/shard_map/all_to_all | solution.py:876
  (209 shorter events, 56.2 us)
Async XLA Ops:
  4.5 22.9 %collective-permute-start = (bf16[1,16,2816]{2,1,0:T(8,128)(2,1)S(1)}, bf16[1,16,2816]{2,1,0:T(8,128)(2,1)S(1)}, u32[]{:S(2)}, u32[]{:S(2)}) collective-permute-start(bf16[1,16,2816]{2,1,0:T(8,128)(2,1)S(1)} %get-tuple-element.29), channel_id=1, source_target_pairs={{0,4},{1,5},{2,6},{3,7},{4,0},{5,1},{6,2},{7,3},{8,12},{9,13},{10,... | collective-permute-start | bytes 270344 | tf_op jit(solution)/shard_map/ppermute | solution.py:222
  7.6 20.5 %collective-permute-start.1 = (bf16[1,16,2816]{2,1,0:T(8,128)(2,1)S(1)}, bf16[1,16,2816]{2,1,0:T(8,128)(2,1)S(1)}, u32[]{:S(2)}, u32[]{:S(2)}) collective-permute-start(bf16[1,16,2816]{2,1,0:T(8,128)(2,1)S(1)} %get-tuple-element.30), channel_id=1, source_target_pairs={{0,8},{1,9},{2,10},{3,11},{4,12},{5,13},{6,14},{7,15},{8,0},{9,1},... | collective-permute-start | bytes 270344 | tf_op jit(solution)/shard_map/ppermute | solution.py:222
  10.2 17.9 %collective-permute-start.2 = (bf16[1,16,2816]{2,1,0:T(8,128)(2,1)S(1)}, bf16[1,16,2816]{2,1,0:T(8,128)(2,1)S(1)}, u32[]{:S(2)}, u32[]{:S(2)}) collective-permute-start(bf16[1,16,2816]{2,1,0:T(8,128)(2,1)S(1)} %get-tuple-element.31), channel_id=1, source_target_pairs={{0,12},{1,13},{2,14},{3,15},{4,8},{5,9},{6,10},{7,11},{8,4},{9,5},... | collective-permute-start | bytes 270344 | tf_op jit(solution)/shard_map/ppermute | solution.py:222
  10.2 24.6 %collective-permute-start.3 = (bf16[1,16,2816]{2,1,0:T(8,128)(2,1)S(1)}, bf16[1,16,2816]{2,1,0:T(8,128)(2,1)S(1)}, u32[]{:S(2)}, u32[]{:S(2)}) collective-permute-start(bf16[1,16,2816]{2,1,0:T(8,128)(2,1)S(1)} %get-tuple-element.28), channel_id=1, source_target_pairs={{0,2},{1,3},{2,0},{3,1},{4,6},{5,7},{6,4},{7,5},{8,10},{9,11},{10,... | collective-permute-start | bytes 270344 | tf_op jit(solution)/shard_map/ppermute | solution.py:222
  19.5 40.5 %all-to-all-start = ((bf16[8,16,1152]{2,1,0:T(8,128)(2,1)}), bf16[8,16,1152]{2,1,0:T(8,128)(2,1)S(1)}, u32[]{:S(2)}, u32[]{:S(2)}) async-start(bf16[8,16,1152]{2,1,0:T(8,128)(2,1)} %shard_map.231), calls=%async_computation | async-start | bytes 589824 | tf_op jit(solution)/shard_map/all_to_all | solution.py:695
  25.5 12.8 %collective-permute-start.15 = (bf16[44,1024]{1,0:T(8,128)(2,1)S(1)}, bf16[44,1024]{1,0:T(8,128)(2,1)S(1)}, u32[]{:S(2)}, u32[]{:S(2)}) collective-permute-start(bf16[44,1024]{1,0:T(8,128)(2,1)S(1)} %get-tuple-element.64), channel_id=1, source_target_pairs={{0,1},{1,3},{2,5},{3,7},{4,9},{5,11},{6,13},{7,15},{8,0},{9,2},{10... | collective-permute-start | bytes 270344 | tf_op jit(solution)/shard_map/ppermute | solution.py:747
  27.4 11.0 %collective-permute-start.14 = (bf16[44,1024]{1,0:T(8,128)(2,1)S(1)}, bf16[44,1024]{1,0:T(8,128)(2,1)S(1)}, u32[]{:S(2)}, u32[]{:S(2)}) collective-permute-start(bf16[44,1024]{1,0:T(8,128)(2,1)S(1)} %get-tuple-element.65), channel_id=1, source_target_pairs={{0,0},{1,2},{2,4},{3,6},{4,8},{5,10},{6,12},{7,14},{8,1},{9,3},{10... | collective-permute-start | bytes 270344 | tf_op jit(solution)/shard_map/ppermute | solution.py:742
  28.7 27.4 %collective-permute-start.5 = (bf16[4,16,2816]{2,1,0:T(8,128)(2,1)S(1)}, bf16[4,16,2816]{2,1,0:T(8,128)(2,1)S(1)}, u32[]{:S(2)}, u32[]{:S(2)}) collective-permute-start(bf16[4,16,2816]{2,1,0:T(8,128)(2,1)S(1)} %constant_dynamic-update-slice_fusion.rest_0_), channel_id=1, source_target_pairs={{0,1},{1,0},{2,3},{3,2},{4,5},{5,4},{6,7},{7,6},{8,9},{9,8},{10,11... | collective-permute-start | bytes 1081352 | tf_op jit(solution)/shard_map/ppermute | solution.py:222
  31.3 17.7 %collective-permute-start.4 = (bf16[3,16,2816]{2,1,0:T(8,128)(2,1)S(1)}, bf16[3,16,2816]{2,1,0:T(8,128)(2,1)S(1)}, u32[]{:S(2)}, u32[]{:S(2)}) collective-permute-start(bf16[3,16,2816]{2,1,0:T(8,128)(2,1)S(1)} %pad_maximum_fusion), channel_id=1, source_target_pairs={{0,2},{1,3},{2,0},{3,1},{4,6},{5,7},{6,4},{7,5},{8,10},{9,11},{10,... | collective-permute-start | bytes 811016 | tf_op jit(solution)/shard_map/ppermute | solution.py:222
  34.8 7.3 %collective-permute-start.9 = (bf16[4,96,128]{2,1,0:T(8,128)(2,1)S(1)}, bf16[4,96,128]{2,1,0:T(8,128)(2,1)S(1)}, u32[]{:S(2)}, u32[]{:S(2)}) collective-permute-start(bf16[4,96,128]{2,1,0:T(8,128)(2,1)S(1)} %get-tuple-element.36), channel_id=1, source_target_pairs={{0,4},{1,5},{2,6},{3,7},{4,0},{5,1},{6,2},{7,3},{8,12},{9,13},{10,... | collective-permute-start | bytes 294920 | tf_op jit(solution)/shard_map/ppermute | solution.py:222
  38.4 10.0 %collective-permute-start.10 = (bf16[4,96,128]{2,1,0:T(8,128)(2,1)S(1)}, bf16[4,96,128]{2,1,0:T(8,128)(2,1)S(1)}, u32[]{:S(2)}, u32[]{:S(2)}) collective-permute-start(bf16[4,96,128]{2,1,0:T(8,128)(2,1)S(1)} %get-tuple-element.37), channel_id=1, source_target_pairs={{0,8},{1,9},{2,10},{3,11},{4,12},{5,13},{6,14},{7,15},{8,0},{9,1},... | collective-permute-start | bytes 294920 | tf_op jit(solution)/shard_map/ppermute | solution.py:222
  39.6 8.8 %collective-permute-start.11 = (bf16[4,96,128]{2,1,0:T(8,128)(2,1)S(1)}, bf16[4,96,128]{2,1,0:T(8,128)(2,1)S(1)}, u32[]{:S(2)}, u32[]{:S(2)}) collective-permute-start(bf16[4,96,128]{2,1,0:T(8,128)(2,1)S(1)} %get-tuple-element.38), channel_id=1, source_target_pairs={{0,12},{1,13},{2,14},{3,15},{4,8},{5,9},{6,10},{7,11},{8,4},{9,5},... | collective-permute-start | bytes 294920 | tf_op jit(solution)/shard_map/ppermute | solution.py:222
  48.4 6.9 %collective-permute-start.12 = (bf16[8,96,128]{2,1,0:T(8,128)(2,1)S(1)}, bf16[8,96,128]{2,1,0:T(8,128)(2,1)S(1)}, u32[]{:S(2)}, u32[]{:S(2)}) collective-permute-start(bf16[8,96,128]{2,1,0:T(8,128)(2,1)S(1)} %pad_maximum_fusion.2), channel_id=1, source_target_pairs={{0,2},{1,3},{2,0},{3,1},{4,6},{5,7},{6,4},{7,5},{8,10},{9,11},{10,... | collective-permute-start | bytes 589832 | tf_op jit(solution)/shard_map/ppermute | solution.py:222
  49.6 8.3 %collective-permute-start.7 = (bf16[3,16,2816]{2,1,0:T(8,128)(2,1)S(1)}, bf16[3,16,2816]{2,1,0:T(8,128)(2,1)S(1)}, u32[]{:S(2)}, u32[]{:S(2)}) collective-permute-start(bf16[3,16,2816]{2,1,0:T(8,128)(2,1)S(1)} %collective-permute-done.4.rest_2_), channel_id=1, source_target_pairs={{0,1},{1,0},{2,3},{3,2},{4,5},{5,4},{6,7},{7,6},{8,9},{9,8},{10,11... | collective-permute-start | bytes 811016 | tf_op jit(solution)/shard_map/ppermute | solution.py:222
  56.1 12.7 %collective-permute-start.13 = (bf16[8,96,128]{2,1,0:T(8,128)(2,1)}, bf16[8,96,128]{2,1,0:T(8,128)(2,1)S(1)}, u32[]{:S(2)}, u32[]{:S(2)}) collective-permute-start(bf16[8,96,128]{2,1,0:T(8,128)(2,1)} %pad_maximum_fusion.4), channel_id=1, source_target_pairs={{0,1},{1,0},{2,3},{3,2},{4,5},{5,4},{6,7},{7,6},{8,9},{9,8},{10,11... | collective-permute-start | bytes 589832 | tf_op jit(solution)/shard_map/ppermute | solution.py:222
  58.5 14.5 %collective-permute-start.8 = (bf16[16,6,17]{2,1,0:T(8,128)(2,1)}, bf16[16,6,17]{2,1,0:T(8,128)(2,1)}, u32[]{:S(2)}, u32[]{:S(2)}) collective-permute-start(bf16[16,6,17]{2,1,0:T(8,128)(2,1)} %constant_dynamic-update-slice_fusion.4), channel_id=1, source_target_pairs={{0,16},{16,0},{1,17},{17,1},{2,18},{18,2},{3,19},{19,3},{4,20},{20... | collective-permute-start | bytes 9800 | tf_op jit(solution)/shard_map/ppermute | solution.py:222
  64.7 20.5 %all-to-all-start.1 = ((bf16[8,16,2176]{2,1,0:T(8,128)(2,1)}), bf16[8,16,2176]{2,1,0:T(8,128)(2,1)S(1)}, u32[]{:S(2)}, u32[]{:S(2)}) async-start(bf16[8,16,2176]{2,1,0:T(8,128)(2,1)} %shard_map.232), calls=%async_computation.1 | async-start | bytes 1114112 | tf_op jit(solution)/shard_map/all_to_all | solution.py:735
  85.4 8.4 %collective-permute-start.18 = (bf16[16,2176]{1,0:T(8,128)(2,1)S(1)}, bf16[16,2176]{1,0:T(8,128)(2,1)S(1)}, u32[]{:S(2)}, u32[]{:S(2)}) collective-permute-start(bf16[16,2176]{1,0:T(8,128)(2,1)S(1)} %get-tuple-element.45), channel_id=1, source_target_pairs={{0,12},{1,13},{2,14},{3,15},{4,8},{5,9},{6,10},{7,11},{8,4},{9,5},... | collective-permute-start | bytes 208904 | tf_op jit(solution)/shard_map/ppermute | solution.py:222
  87.1 6.8 %collective-permute-start.17 = (bf16[16,2176]{1,0:T(8,128)(2,1)S(1)}, bf16[16,2176]{1,0:T(8,128)(2,1)S(1)}, u32[]{:S(2)}, u32[]{:S(2)}) collective-permute-start(bf16[16,2176]{1,0:T(8,128)(2,1)S(1)} %get-tuple-element.45), channel_id=1, source_target_pairs={{0,8},{1,9},{2,10},{3,11},{4,12},{5,13},{6,14},{7,15},{8,0},{9,1},... | collective-permute-start | bytes 208904 | tf_op jit(solution)/shard_map/ppermute | solution.py:222
  93.9 8.1 %collective-permute-start.20 = (bf16[32,2176]{1,0:T(8,128)(2,1)S(1)}, bf16[32,2176]{1,0:T(8,128)(2,1)S(1)}, u32[]{:S(2)}, u32[]{:S(2)}) collective-permute-start(bf16[32,2176]{1,0:T(8,128)(2,1)S(1)} %constant_dynamic-update-slice_fusion.26.rest_1_), channel_id=1, source_target_pairs={{0,16},{16,0},{1,17},{17,1},{2,18},{18,2},{3,19},{19,3},{4,20},{20... | collective-permute-start | bytes 417800 | tf_op jit(solution)/shard_map/ppermute | solution.py:222
  95.5 6.9 %collective-permute-start.26 = (bf16[32,2176]{1,0:T(8,128)(2,1)S(1)}, bf16[32,2176]{1,0:T(8,128)(2,1)S(1)}, u32[]{:S(2)}, u32[]{:S(2)}) collective-permute-start(bf16[32,2176]{1,0:T(8,128)(2,1)S(1)} %constant_dynamic-update-slice_fusion.26.rest_1_), channel_id=1, source_target_pairs={{0,1},{1,0},{2,3},{3,2},{4,5},{5,4},{6,7},{7,6},{8,9},{9,8},{10,11... | collective-permute-start | bytes 417800 | tf_op jit(solution)/shard_map/ppermute | solution.py:222
  95.6 6.9 %collective-permute-start.22 = (bf16[32,2176]{1,0:T(8,128)(2,1)S(1)}, bf16[32,2176]{1,0:T(8,128)(2,1)S(1)}, u32[]{:S(2)}, u32[]{:S(2)}) collective-permute-start(bf16[32,2176]{1,0:T(8,128)(2,1)S(1)} %constant_dynamic-update-slice_fusion.26.rest_1_), channel_id=1, source_target_pairs={{0,2},{1,3},{2,0},{3,1},{4,6},{5,7},{6,4},{7,5},{8,10},{9,11},{10,... | collective-permute-start | bytes 417800 | tf_op jit(solution)/shard_map/ppermute | solution.py:222
  117.7 11.7 %collective-permute-start.33 = (bf16[224,704]{1,0:T(8,128)(2,1)S(1)}, bf16[224,704]{1,0:T(8,128)(2,1)S(1)}, u32[]{:S(2)}, u32[]{:S(2)}) collective-permute-start(bf16[224,704]{1,0:T(8,128)(2,1)S(1)} %get-tuple-element.46.act_ref), channel_id=1, source_target_pairs={{0,16},{16,0},{1,17},{17,1},{2,18},{18,2},{3,19},{19,3},{4,20},{20... | collective-permute-start | bytes 946184 | tf_op jit(solution)/shard_map/ppermute | solution.py:222
  118.2 11.2 %collective-permute-start.34 = (bf16[272,128]{1,0:T(8,128)(2,1)S(1)}, bf16[272,128]{1,0:T(8,128)(2,1)S(1)}, u32[]{:S(2)}, u32[]{:S(2)}) collective-permute-start(bf16[272,128]{1,0:T(8,128)(2,1)S(1)} %get-tuple-element.47.shared_ref), channel_id=1, source_target_pairs={{0,16},{16,0},{1,17},{17,1},{2,18},{18,2},{3,19},{19,3},{4,20},{20... | collective-permute-start | bytes 208904 | tf_op jit(solution)/shard_map/ppermute | solution.py:222
  (50 other events, 278.2 us)

commit v3 on v2

--- a/solution.py
+++ b/solution.py
@@ -222,22 +222,57 @@
     return lax.ppermute(value, axis, [(i, i ^ bit) for i in range(size)])
 
 
-def call(kernel, out_shapes, args, scratch=(), scalars=0, flops=0, vmem=10):
-    specs = [pl.BlockSpec(memory_space=pltpu.SMEM)] * scalars + [
-        pl.BlockSpec(memory_space=pltpu.VMEM)
-    ] * (len(args) - scalars)
-    moved = sum(a.size * a.dtype.itemsize for a in args)
+def call(kernel, out_shapes, args, scratch=(), scalars=0, flops=0, vmem=10, moved=(), late=(), rows=None):
+    specs = []
+    for i in range(len(args)):
+        if i < scalars:
+            specs.append(pl.BlockSpec(memory_space=pltpu.SMEM))
+        elif i in moved:
+            specs.append(pl.BlockSpec(memory_space=pl.ANY))
+        else:
+            specs.append(pl.BlockSpec(memory_space=pltpu.VMEM))
+    scratch = list(scratch)
+    body = kernel
+    if moved:
+        rows = dict(rows or {})
+        shapes = {i: args[i].shape for i in moved}
+        for i, (_, count) in rows.items():
+            shapes[i] = (shapes[i][0], count) + shapes[i][2:]
+        buffers = [pltpu.VMEM(shapes[i], args[i].dtype) for i in moved]
+        scratch = scratch + buffers + [pltpu.SemaphoreType.DMA((len(moved),))]
+
+        def body(*refs):
+            rest, held, sem = refs[: -len(moved) - 1], refs[-len(moved) - 1 : -1], refs[-1]
+            sources = {i: refs[i] for i in moved}
+            for i, (start, count) in rows.items():
+                sources[i] = refs[i].at[:, pl.ds(start, count)]
+            copies = [
+                pltpu.make_async_copy(sources[i], held[j], sem.at[j]) for j, i in enumerate(moved)
+            ]
+            for copy in copies:
+                copy.start()
+            for i, copy in zip(moved, copies):
+                if i not in late:
+                    copy.wait()
+            inputs = [held[moved.index(i)] if i in moved else refs[i] for i in range(len(args))]
+            if late:
+                waits = [copies[moved.index(i)].wait for i in late]
+                kernel(*inputs, *rest[len(args) :], waits=waits)
+            else:
+                kernel(*inputs, *rest[len(args) :])
+
+    moved_bytes = sum(a.size * a.dtype.itemsize for a in args)
     single = not isinstance(out_shapes, (list, tuple))
     return pl.pallas_call(
-        kernel,
+        body,
         out_shape=out_shapes,
         in_specs=specs,
         out_specs=pl.BlockSpec(memory_space=pltpu.VMEM)
         if single
         else [pl.BlockSpec(memory_space=pltpu.VMEM)] * len(out_shapes),
-        scratch_shapes=list(scratch),
+        scratch_shapes=scratch,
         compiler_params=pltpu.CompilerParams(vmem_limit_bytes=vmem * 1024 * 1024),
-        cost_estimate=pl.CostEstimate(flops=flops, bytes_accessed=moved, transcendentals=0),
+        cost_estimate=pl.CostEstimate(flops=flops, bytes_accessed=moved_bytes, transcendentals=0),
     )(*args)
 
 
@@ -270,8 +305,13 @@
         block[0, :, D + tiles * LANES :] = side
 
 
-def spread_kernel(units, place_ref, gate_ref, up_ref, *block_refs):
+def spread_kernel(units, place_ref, gate_ref, up_ref, down_ref, *out_refs):
+    block_refs, (down_a_ref, down_b_ref) = out_refs[:-2], out_refs[-2:]
     me = place_ref[0]
+    lower = me < block_refs[0].shape[0] * OUTER // 2
+    first, second = down_ref[:units], down_ref[units:]
+    down_a_ref[...] = jnp.where(lower, first, second)
+    down_b_ref[...] = jnp.where(lower, second, first)
     inner = block_refs[0].shape[0]
     padded = block_refs[0].shape[1] // 2
     for step in range(OUTER):
@@ -288,8 +328,7 @@
                 block_refs[outer][near, padded : padded + units] = up_ref[rows]
 
 
-def small_kernel(place_ref, kept_ref, far_ref, *rest):
-    router_refs, (small_ref, fold_ref) = rest[:-2], rest[-2:]
+def small_kernel(place_ref, kept_ref, far_ref, router_ref, small_ref, fold_ref):
     me = place_ref[0]
     members = kept_ref.shape[0] + far_ref.shape[0]
     small_ref[...] = jnp.zeros_like(small_ref)
@@ -301,11 +340,7 @@
         lanes = pl.ds(pl.multiple_of(holder * LANES, LANES), LANES)
         small_ref[:padded, lanes] = ref[i, :padded]
         small_ref[half : half + padded, lanes] = ref[i, padded:]
-    row = 0
-    for ref in router_refs:
-        count = ref.shape[0] * TILE
-        fold_ref[row : row + count, :] = ref[...].reshape(count, LANES).astype(jnp.float32)
-        row += count
+    fold_ref[...] = router_ref[...].reshape(members * TILE, LANES).astype(jnp.float32)
     for part in range(TILE):
         small_ref[LANES - members :, part * LANES : (part + 1) * LANES] = fold_ref[
             pl.ds(part, members, stride=TILE), :
@@ -399,8 +434,11 @@
 
 
 def project_kernel(place_ref, att_ref, *rest):
-    piece_refs, (out_ref, rows_ref, fold_ref, uv_ref) = rest[:-4], rest[-4:]
+    piece_refs, (out_ref, router_ref, routes_ref, rows_ref, fold_ref, uv_ref) = rest[:-6], rest[-6:]
     pieces = [(ref, i) for ref in piece_refs for i in range(ref.shape[0])]
+    for step, (ref, i) in enumerate(pieces):
+        router_ref[step] = ref[i, :, -2 * LANES : -LANES]
+        routes_ref[step] = ref[i, :, -LANES:]
     me = place_ref[0]
     blocks, span, width = att_ref.shape
     width -= LANES
@@ -466,6 +504,80 @@
     return offset
 
 
+def route_kernel(
+    place_ref, plane_ref, other_ref, select_ref, scatter_ref, chosen_ref
+):
+    me, group = place_ref[0], place_ref[1]
+    members = plane_ref.shape[0]
+    homes = 2 * members
+    total = chosen_ref.shape[0]
+    pre_total = homes * TILE
+    slots = select_ref.shape[0]
+
+    def home_of(token):
+        return jnp.where(token < pre_total, token // TILE, token - pre_total)
+
+    def row_of(token):
+        return jnp.where(token < pre_total, token % TILE, TILE)
+
+    def place_of(token):
+        place = home_place(home_of(token), me, group, members)
+        return jnp.where(token < pre_total, place * TILE + token % TILE, pre_total + place)
+
+    def iota(shape, axis):
+        return lax.broadcasted_iota(jnp.int32, shape, axis)
+
+    token = iota((total, homes), 0)
+    home = home_of(token)
+    held = ((home // (members // 2)) % 2) * members + (home // members) * (members // 2) + home % (
+        members // 2
+    )
+    pick = jnp.where(held == iota((total, homes), 1), 1.0, 0.0).astype(jnp.bfloat16)
+    own_row = iota((total, LANES), 1) == row_of(iota((total, LANES), 0))
+    lane = iota((total, LANES), 1)
+    lane_expert = jnp.where(
+        lane >= LANES - members,
+        chain_offset(lane - jnp.where(lane >= LANES - members, LANES - members, 0), members) ^ me,
+        -1,
+    ).astype(jnp.float32)
+    chosen = jnp.zeros((total, LANES), jnp.float32)
+    mine = jnp.zeros((total, LANES), jnp.float32)
+    for k in range(TOPK):
+        table = jnp.concatenate([plane_ref[:, k, :], other_ref[:, k, :]], axis=0)
+        spread = jnp.dot(pick, table, preferred_element_type=jnp.float32)
+        expert = jnp.sum(jnp.where(own_row, spread, 0.0), axis=1, keepdims=True)
+        chosen = chosen + jnp.where(expert == lane_expert, 1.0, 0.0)
+        mine = mine + jnp.where(own_row & (spread == me.astype(jnp.float32)), 1.0, 0.0)
+    chosen_ref[...] = chosen.astype(jnp.bfloat16)
+    mine_row = lax.dot_general(
+        jnp.ones((8, LANES), jnp.bfloat16),
+        mine.astype(jnp.bfloat16),
+        ROWS_CONTRACT,
+        preferred_element_type=jnp.float32,
+    )
+    square = (total, total)
+    place_row = place_of(iota((8, total), 1))[:1]
+    place_column = place_of(iota((total, LANES), 0))[:, :1]
+    earlier = jnp.where(place_column <= place_row, 1.0, 0.0).astype(jnp.bfloat16)
+    rank_row = jnp.dot(
+        mine_row.astype(jnp.bfloat16), earlier, preferred_element_type=jnp.float32
+    )[:1]
+    slot = (iota((slots, total), 0) + 1).astype(jnp.float32)
+    select = jnp.where((slot == rank_row) & (mine_row[:1] > 0.0), 1.0, 0.0).astype(jnp.bfloat16)
+    same = jnp.where(iota(square, 0) == iota(square, 1), 1.0, 0.0).astype(jnp.bfloat16)
+    select_ref[...] = select
+    scatter_ref[...] = lax.dot_general(
+        same, select, ROWS_CONTRACT, preferred_element_type=jnp.float32
+    ).astype(jnp.bfloat16)
+
+
+def home_place(index, me, group, members):
+    half = members // 2
+    last, home_group = index // members, (index // half) % 2
+    member = chain_offset(index % half + last * half, members) ^ me
+    return last * members + (home_group ^ group) * half + member // 2
+
+
 def norm_kernel(partial_ref, resid_ref, gain_ref, hidden_ref, normed_ref):
     summed = partial_ref[0].astype(jnp.float32)
     for i in range(1, partial_ref.shape[0]):
@@ -481,10 +593,9 @@
     normed_ref[:, D:] = (dec * lax.rsqrt(dec_mean + NORM_EPS) * gain[:, D:]).astype(jnp.bfloat16)
 
 
-def expert_kernel(
-    units, small_ref, select_ref, chosen_ref, reorder_ref, gate_ref, up_ref, *rest
-):
-    piece_refs, (act_ref, shared_ref, fold_ref, pre_ref, dec_ref) = rest[:-5], rest[-5:]
+def expert_kernel(units, small_ref, select_ref, chosen_ref, gate_ref, up_ref, *rest):
+    piece_refs, outs = rest[:-7], rest[-7:]
+    act_ref, shared_ref, rows_ref, weight_ref, fold_ref, pre_ref, dec_ref = outs
     pre_total = pre_ref.shape[0]
     homes = pre_total // TILE
     row = 0
@@ -512,17 +623,19 @@
     gate_part = first[:, :units]
     up_part = first[:, half : half + units]
     shared_act = (gate_part / (1.0 + jnp.exp(-gate_part)) * up_part).astype(jnp.bfloat16)
-    shared_act = jnp.dot(
-        reorder_ref[...], shared_act, preferred_element_type=jnp.float32
-    ).astype(jnp.bfloat16)
-    total = shared_act.shape[0]
     shared_ref[...] = jnp.zeros_like(shared_ref)
-    shared_ref[:, :units] = shared_act[: total // 2]
-    shared_ref[:, half : half + units] = shared_act[total // 2 :]
+    split = pre_total // 2
+    middle = pre_total + homes // 2
+    shared_ref[:split, :units] = shared_act[:split]
+    shared_ref[:split, half : half + units] = shared_act[split:pre_total]
+    shared_ref[split:, :units] = shared_act[pre_total:middle]
+    shared_ref[split:, half : half + units] = shared_act[middle:]
     logits = first[:, LANES - members :]
     scores = 1.0 / (1.0 + jnp.exp(-logits))
     token_weight = (
-        ROUTE_SCALE * scores[:, :1] / jnp.sum(scores * chosen_ref[:, LANES - members :], axis=1, keepdims=True)
+        ROUTE_SCALE
+        * scores[:, :1]
+        / jnp.sum(scores * chosen_ref[:, LANES - members :], axis=1, keepdims=True)
     )
     high = token_weight.astype(jnp.bfloat16)
     rest = token_weight - high.astype(jnp.float32)
@@ -532,58 +645,86 @@
     weights = jnp.dot(
         select, jnp.concatenate([high, middle, rest], axis=1), preferred_element_type=jnp.float32
     )
-    slot_weight = jnp.sum(weights, axis=1, keepdims=True)
-    expert_rows = (
+    weight_ref[...] = jnp.broadcast_to(jnp.sum(weights, axis=1, keepdims=True), weight_ref.shape)
+    rows_ref[...] = (
         jnp.dot(select[:, :pre_total], pre, preferred_element_type=jnp.float32)
         + jnp.dot(select[:, pre_total:], dec, preferred_element_type=jnp.float32)
     ).astype(jnp.bfloat16)
+    hidden_kernel(0, rows_ref, weight_ref, gate_ref, up_ref, act_ref)
+
+
+def hidden_kernel(start, rows_ref, weight_ref, gate_ref, up_ref, act_ref):
+    rows = rows_ref[...]
+    count = act_ref.shape[1]
     gate = lax.dot_general(
-        expert_rows, gate_ref[0], ROWS_CONTRACT, preferred_element_type=jnp.float32
-    )
-    up = lax.dot_general(expert_rows, up_ref[0], ROWS_CONTRACT, preferred_element_type=jnp.float32)
-    act_ref[...] = (gate / (1.0 + jnp.exp(-gate)) * up * slot_weight).astype(jnp.bfloat16)
+        rows, gate_ref[0, start : start + count], ROWS_CONTRACT, preferred_element_type=jnp.float32
+    )
+    up = lax.dot_general(
+        rows, up_ref[0, start : start + count], ROWS_CONTRACT, preferred_element_type=jnp.float32
+    )
+    act_ref[...] = (gate / (1.0 + jnp.exp(-gate)) * up * weight_ref[:, :1]).astype(jnp.bfloat16)
 
 
 def down_kernel(
-    place_ref, act_ref, act_other_ref, shared_ref, shared_other_ref, down_ref,
-    shared_down_ref, shared_down_other_ref, scatter_ref, kept_ref, sent_ref, fold_ref,
+    place_ref, act_a_ref, act_b_ref, other_a_ref, other_b_ref, shared_ref, shared_other_ref,
+    down_ref, down_a_ref, down_b_ref, scatter_ref, kept_ref, sent_ref, fold_ref,
 ):
-    group = place_ref[1]
-    width = act_ref.shape[1]
+    me, group = place_ref[0], place_ref[1]
     columns = down_ref.shape[2]
-    own = down_ref[0, pl.ds(pl.multiple_of(group * width, TILE), width), :]
-    other = down_ref[0, pl.ds(pl.multiple_of((1 - group) * width, TILE), width), :]
-    routed = (
-        jnp.dot(act_ref[...], own, preferred_element_type=jnp.float32)
-        + jnp.dot(act_other_ref[...], other, preferred_element_type=jnp.float32)
-    ).astype(jnp.bfloat16)
-    units = shared_down_ref.shape[0]
-
-    def down(at):
-        both = jnp.concatenate([shared_ref[:, at : at + units], shared_other_ref[:, at : at + units]], axis=1)
-        return jnp.dot(both, jnp.concatenate([shared_down_ref[...], shared_down_other_ref[...]], axis=0), preferred_element_type=jnp.float32)
-
-    total = (
-        jnp.dot(scatter_ref[...], routed, preferred_element_type=jnp.float32)
-        + jnp.concatenate([down(0), down(LANES // 2)], axis=0)
-    )
+    units = down_a_ref.shape[0]
+    width = down_ref.shape[1] // 2
+    routed = jnp.zeros((act_a_ref.shape[0], columns), jnp.float32)
+    for refs, which in (((act_a_ref, act_b_ref), group), ((other_a_ref, other_b_ref), 1 - group)):
+        row = which * width
+        for ref in refs:
+            rows = down_ref[0, pl.ds(pl.multiple_of(row, TILE), ref.shape[1]), :]
+            routed = routed + jnp.dot(ref[...], rows, preferred_element_type=jnp.float32)
+            row = row + ref.shape[1]
+    routed = routed.astype(jnp.bfloat16)
+    mine_first = lax.rem(me, 2) == group
+    own_down = jnp.where(mine_first, down_a_ref[...], down_b_ref[...])
+    other_down = jnp.where(mine_first, down_b_ref[...], down_a_ref[...])
+    both_down = jnp.concatenate([own_down, other_down], axis=0)
     half = kept_ref.shape[0]
     homes = 2 * half
     split = homes * TILE
-    kept_ref[:, :, :columns] = (
-        total[: split // 2].astype(jnp.bfloat16).reshape(half, TILE, columns)
-    )
-    sent_ref[:, :, :columns] = (
-        total[split // 2 : split].astype(jnp.bfloat16).reshape(half, TILE, columns)
+    other = shared_other_ref[...]
+    middle, decs = split // 4, other[split // 2 :].astype(jnp.float32)
+    eighth = homes // 4
+    other = jnp.concatenate(
+        [
+            other[middle : 2 * middle],
+            other[:middle],
+            jnp.concatenate([decs[eighth:], decs[:eighth]], axis=0).astype(jnp.bfloat16),
+        ],
+        axis=0,
+    )
+    shared = shared_ref[...]
+
+    def down(at):
+        acts = jnp.concatenate([shared[:, at : at + units], other[:, at : at + units]], axis=1)
+        return jnp.dot(acts, both_down, preferred_element_type=jnp.float32)
+
+    low_half, high_half = down(0), down(LANES // 2)
+    total = jnp.dot(scatter_ref[...], routed, preferred_element_type=jnp.float32) + jnp.concatenate(
+        [
+            low_half[: split // 2], high_half[: split // 2], low_half[split // 2 :],
+            high_half[split // 2 :],
+        ],
+        axis=0,
     )
     fold_ref[...] = jnp.zeros_like(fold_ref)
     for part in range(columns // LANES):
         fold_ref[pl.ds(part, homes, stride=TILE), :] = total[
             split:, part * LANES : (part + 1) * LANES
         ]
-    folded = fold_ref[...].astype(jnp.bfloat16)
-    kept_ref[:, :, columns:] = folded[: split // 2].reshape(half, TILE, LANES)
-    sent_ref[:, :, columns:] = folded[split // 2 :].reshape(half, TILE, LANES)
+    for home in range(homes):
+        place = home_place(home, me, group, half)
+        ref = kept_ref if home < half else sent_ref
+        at = place if home < half else place - half
+        rows = slice(home * TILE, (home + 1) * TILE)
+        ref[at, :, :columns] = total[rows].astype(jnp.bfloat16)
+        ref[at, :, columns:] = fold_ref[rows].astype(jnp.bfloat16)
 
 
 def finish_kernel(got_ref, hidden_ref, pre_ref, dec_ref):
@@ -651,22 +792,28 @@
         [place_ids, out_weight, uv_weight, router.T, routes.T],
         scratch=[pltpu.VMEM((TILE, 2 * LANES), jnp.float32)],
         scalars=1,
+        moved=(1, 2, 3, 4),
+        vmem=60,
     )
     pair_bit = inner // 2
     near = [blocks[0]] + [swap(blocks[i], "expert", i * inner) for i in range(1, OUTER)]
     own_pair = swap(blocks[0], "expert", pair_bit)
     line = jnp.concatenate(near, axis=0)
-    far_pair = swap(line[1:], "expert", pair_bit)
+    far_in, own_pair = lax.optimization_barrier((line[1:], own_pair))
+    far_pair = swap(far_in, "expert", pair_bit)
+    units = shared_gate.shape[1] // members
+    padded = -(-units // TILE) * TILE
+    depth = shared_gate.shape[0]
+    line, line_gate = lax.optimization_barrier((line, shared_gate))
+    *spread, down_a, down_b = call(
+        partial(spread_kernel, units),
+        [low((inner, 2 * padded, depth))] * OUTER + [low((units, shared_down.shape[1]))] * 2,
+        [place_ids, line_gate.T, shared_up.T, shared_down],
+        scalars=1,
+    )
+    far_pair, *spread = lax.optimization_barrier((far_pair, *spread))
     pieces = [line, own_pair, far_pair]
     pieces = pieces + [swap(piece, "expert", 1) for piece in pieces]
-    chain = [chain_offset(step, members) for step in range(members)]
-    holders = me ^ jnp.array(chain, jnp.int32)
-    side_at = D + uv_tiles * value_dim
-    router_blocks = [piece[:, :, side_at : side_at + LANES] for piece in pieces]
-    routes_plane = jnp.concatenate(
-        [piece[:, :TOPK, side_at + LANES : side_at + LANES + rows_dev] for piece in pieces], axis=0
-    )
-    routes_other = swap(routes_plane, "dp", 1)
 
     pre_query, blocks = lax.optimization_barrier((pre_query, blocks))
     peers = groups * OUTER
@@ -686,6 +833,8 @@
         ],
         scalars=1,
         flops=100_000_000,
+        moved=(1, 2, 3, 4, 5),
+        vmem=60,
     )
     lines = [
         [g * members + o * inner + i for g in range(groups) for o in range(OUTER)]
@@ -695,9 +844,9 @@
     att_got = lax.all_to_all(
         att_blocks, both, split_axis=0, concat_axis=0, axis_index_groups=lines, tiled=True
     )
-    partial_blocks = call(
+    partial_blocks, router_blocks, routes_plane = call(
         project_kernel,
-        low((peers, pre_rows, D + LANES)),
+        [low((peers, pre_rows, D + LANES))] + [low((members, TILE, LANES))] * 2,
         [place_ids, att_got, *pieces],
         scratch=[
             pltpu.VMEM((peers * pre_rows + TILE, heads_block), jnp.bfloat16),
@@ -706,121 +855,49 @@
         ],
         scalars=1,
         flops=300_000_000,
-    )
-
-    units = shared_gate.shape[1] // members
-    padded = -(-units // TILE) * TILE
-    depth = shared_gate.shape[0]
-    shared_gate, shared_up, line = lax.optimization_barrier((shared_gate, shared_up, line))
-    spread = call(
-        partial(spread_kernel, units),
-        [low((inner, 2 * padded, depth))] * OUTER,
-        [place_ids, shared_gate.T, shared_up.T],
-        scalars=1,
-    )
+        moved=tuple(range(2, 2 + len(pieces))),
+    )
+    routes_other = swap(routes_plane, "dp", 1)
+
     shared_got = [spread[0]] + [swap(spread[i], "expert", i * inner) for i in range(1, OUTER)]
+    _, *shared_got = lax.optimization_barrier((partial_blocks, *shared_got))
     kept = jnp.concatenate([block[:pair_bit] for block in shared_got], axis=0)
     sent = jnp.concatenate([block[pair_bit:] for block in shared_got], axis=0)
     far = swap(sent, "expert", pair_bit)
+    pre_total = homes * pre_rows
+    total = pre_total + homes
+    slots = homes * capacity
+    select, scatter, chosen = call(
+        route_kernel,
+        [low((slots, total)), low((total, slots)), low((total, LANES))],
+        [place_ids, routes_plane, routes_other],
+        scalars=1,
+        vmem=16,
+    )
+    far, select = lax.optimization_barrier((far, select))
     shared_kept = jnp.concatenate([kept[::pair_bit], far[::pair_bit]], axis=0)
     shared_sent = jnp.concatenate([kept[1::pair_bit], far[1::pair_bit]], axis=0)
     shared_far = swap(shared_sent, "expert", 1)
     small = call(
         small_kernel,
         low((LANES, D)),
-        [place_ids, shared_kept, shared_far, *router_blocks],
+        [place_ids, shared_kept, shared_far, router_blocks],
         scratch=[pltpu.VMEM((members * TILE, LANES), jnp.float32)],
         scalars=1,
     )
     partial_got = lax.all_to_all(
         partial_blocks, both, split_axis=0, concat_axis=0, axis_index_groups=lines, tiled=True
     )
-    shared_down, att_blocks = lax.optimization_barrier((shared_down, att_blocks))
-    half = members // 2
-    lower = me < half
-    first, second = shared_down[:units], shared_down[units:]
-    down_a = lax.ppermute(
-        jnp.where(lower, first, second),
-        "expert",
-        [(i, 2 * i if i < half else 2 * (i - half) + 1) for i in range(members)],
-    )
-    down_b = lax.ppermute(
-        jnp.where(lower, second, first),
-        "expert",
-        [(i, 2 * i + 1 if i < half else 2 * (i - half)) for i in range(members)],
-    )
-    mine_first = (me % 2) == my_group
-    shared_down_own = jnp.where(mine_first, down_a, down_b)
-    shared_down_other = jnp.where(mine_first, down_b, down_a)
-
     middle = OUTER // 2
-    pair_bit = inner // 2
-    tags_a = [(0, step * inner) for step in range(middle)]
-    tags_b = [(0, step * inner) for step in range(middle, OUTER)]
-    tags = []
-    for last in range(2):
-        for which, group_bit, member_bit in (
-            (tags_a, 0, 0), (tags_b, 0, 0), (tags_a, 0, 1), (tags_b, 1, 0),
-            (tags_a, 1, 0), (tags_b, 0, 1), (tags_a, 1, 1), (tags_b, 1, 1),
-        ):
-            tags += [(g ^ group_bit, m ^ (member_bit * pair_bit) ^ last) for g, m in which]
-    pre_total = homes * pre_rows
-    total = pre_total + homes
-
-    positions = [g * members + chain.index(m) for g, m in tags]
-    routes_all = jnp.concatenate([routes_plane, routes_other], axis=0)
-    routes_all = jnp.stack([routes_all[p] for p in positions], axis=0)
-    token_routes = jnp.concatenate(
-        [
-            routes_all[:, :, :pre_rows].transpose(0, 2, 1).reshape(pre_total, TOPK),
-            routes_all[:, :, pre_rows],
-        ],
-        axis=0,
-    ).astype(jnp.int32)
-    lane_expert = jnp.concatenate([jnp.full((LANES - members,), -1, jnp.int32), holders])
-    chosen = jnp.sum(
-        (token_routes[:, :, None] == lane_expert[None, None, :]).astype(jnp.float32), axis=1
-    )
-    mine = jnp.sum((token_routes == me).astype(jnp.float32), axis=1)
-    earlier = (
-        jnp.arange(total, dtype=jnp.int32)[:, None] <= jnp.arange(total, dtype=jnp.int32)[None, :]
-    ).astype(jnp.bfloat16)
-    home_group = jnp.array([g for g, _ in tags], jnp.int32) ^ my_group
-    home_member = jnp.array([m for _, m in tags], jnp.int32) ^ me
-    home_place = (
-        ((home_member ^ me) % 2) * (homes // 2) + home_group * (members // 2) + home_member // 2
-    )
-    place = jnp.concatenate(
-        [
-            (home_place[:, None] * pre_rows + jnp.arange(pre_rows)[None, :]).reshape(-1),
-            pre_total + home_place,
-        ]
-    )
-    reorder = (jnp.arange(total, dtype=jnp.int32)[:, None] == place[None, :]).astype(jnp.bfloat16)
-    mine_placed = jnp.dot(reorder, mine.astype(jnp.bfloat16), preferred_element_type=jnp.float32)
-    rank = jnp.dot(
-        mine_placed.astype(jnp.bfloat16)[None, :], earlier, preferred_element_type=jnp.float32
-    )
-    slots = homes * capacity
-    slot_ids = jnp.arange(1, slots + 1, dtype=jnp.float32)
-    gather = ((rank == slot_ids[:, None]) & (mine_placed[None, :] > 0.0)).astype(jnp.bfloat16)
-    scatter = gather.T
-    select = jnp.dot(gather, reorder, preferred_element_type=jnp.float32).astype(jnp.bfloat16)
-
-    (
-        partial_got, select, scatter, reorder, chosen, small, shared_down_own, shared_down_other
-    ) = lax.optimization_barrier(
-        (
-            partial_got, select, scatter, reorder, chosen, small, shared_down_own,
-            shared_down_other,
-        )
+    partial_got, select, scatter, chosen, small = lax.optimization_barrier(
+        (partial_got, select, scatter, chosen, small)
     )
     resid = jnp.concatenate([pre_resid, fold_row(dec_resid)], axis=1)
     gain = jnp.concatenate(
         [jnp.broadcast_to(norm_gain[None], (TILE, D)), norm_gain.reshape(TILE, LANES)], axis=1
     )
     hidden, normed = call(
-        norm_kernel, [low(resid.shape)] * 2, [partial_got, resid, gain], flops=1_000_000
+        norm_kernel, [low(resid.shape)] * 2, [partial_got, resid, gain], flops=20_000_000_000
     )
 
     line = [normed] + [swap(normed, "expert", step * inner) for step in range(1, OUTER)]
@@ -832,34 +909,56 @@
     a_pair, b_group = swap(piece_a, "expert", pair_bit), swap(piece_b, "dp", 1)
     a_group, b_pair = swap(piece_a, "dp", 1), swap(piece_b, "expert", pair_bit)
     a_both, b_both = swap(a_pair, "dp", 1), swap(b_group, "expert", pair_bit)
-    row_pieces = [piece_a, piece_b, a_pair, b_group, a_group, b_pair, a_both, b_both]
+    row_pieces = [piece_a, piece_b, a_pair, b_pair, a_group, b_group, a_both, b_both]
     row_pieces = row_pieces + [swap(piece, "expert", 1) for piece in row_pieces]
 
     width = gate_weight.shape[2]
-    expert_act, shared_act = call(
+    first_width = -(-width // (2 * LANES)) * LANES
+    gate_rows, up_rows = gate_weight.swapaxes(1, 2), up_weight.swapaxes(1, 2)
+    act_a, shared_act, expert_rows, slot_weight = call(
         partial(expert_kernel, units),
-        [low((slots, width)), low((total // 2, LANES))],
         [
-            small, select, chosen, reorder, gate_weight.swapaxes(1, 2), up_weight.swapaxes(1, 2),
-            *row_pieces,
+            low((slots, first_width)), low((total // 2, LANES)), low((slots, D)),
+            jax.ShapeDtypeStruct((slots, LANES), jnp.float32),
         ],
+        [small, select, chosen, gate_rows, up_rows, *row_pieces],
         scratch=[
             pltpu.VMEM((pre_total, LANES), jnp.float32),
             pltpu.VMEM((pre_total, D), jnp.bfloat16),
             pltpu.VMEM((homes, D), jnp.bfloat16),
         ],
-        flops=3_000_000_000,
+        flops=2_000_000_000,
         vmem=20,
     )
-    expert_act_other = swap(expert_act, "dp", 1)
+    act_a_other = swap(act_a, "dp", 1)
+    act_b = call(
+        partial(hidden_kernel, first_width),
+        low((slots, width - first_width)),
+        [expert_rows, slot_weight, gate_rows, up_rows],
+        flops=1_000_000_000,
+        vmem=12,
+    )
+    act_b_other = swap(act_b, "dp", 1)
     shared_act_other = swap(shared_act, "dp", 1)
+    act_a, down_a, down_b = lax.optimization_barrier((act_a, down_a, down_b))
+    half = members // 2
+    down_a = lax.ppermute(
+        down_a,
+        "expert",
+        [(i, 2 * i if i < half else 2 * (i - half) + 1) for i in range(members)],
+    )
+    down_b = lax.ppermute(
+        down_b,
+        "expert",
+        [(i, 2 * i + 1 if i < half else 2 * (i - half)) for i in range(members)],
+    )
     col_width = down_weight.shape[2]
     kept, sent = call(
         down_kernel,
         [low((homes // 2, TILE, col_width + LANES))] * 2,
         [
-            place_ids, expert_act, expert_act_other, shared_act, shared_act_other, down_weight,
-            shared_down_own, shared_down_other, scatter,
+            place_ids, act_a, act_b, act_a_other, act_b_other, shared_act, shared_act_other,
+            down_weight, down_a, down_b, scatter,
         ],
         scratch=[pltpu.VMEM((pre_total, LANES), jnp.float32)],
         scalars=1,

time: 157 us -> 127 us (0.81)
  local copies, waits for them, and re-layouts: 30.4 us -> 0.16 us
  Pallas kernels: 15 us -> 23.5 us
  waiting for transfers between devices: 36.8 us -> 32.4 us
  other arithmetic: 4.21 us -> 1 us
  matrix products: 2.52 us -> 0 us
  blocking collectives: 21.5 us -> 23.3 us
    unnamed x93 -> x24, local copies, waits for them, and re-layouts: 25.5 us -> 0.07 us
    pallas_call x9 -> x11, Pallas kernels: 15 us -> 23.5 us  [call(): pl.pallas_call(body, out_shape=out_shapes, in_specs=specs, out_specs=pl.B...]
    ppermute x34 -> x35, waiting for transfers between devices: 34.5 us -> 27.6 us  [swap(): return lax.ppermute(value, axis, [(i, i ^ bit) for i in range(size)])]
    slice x8 -> x0, local copies, waits for them, and re-layouts: 2.62 us -> none  [the longest x6 2.39 us: token_shards(): router_blocks = [piece[:, :, side_at:side_at + LANES] for piece in pieces]]
    ppermute x34 -> x35, starting transfers between devices: 32.9 us -> 30.3 us  [swap(): return lax.ppermute(value, axis, [(i, i ^ bit) for i in range(size)])]
    all_to_all x1, waiting for transfers between devices: 2.26 us -> 4.81 us  [token_shards(): lax.all_to_all(partial_blocks, both, split_axis=0, concat_axis=0, axis_in...]
    dot_general x3 -> x0, matrix products: 2.52 us -> none  [the longest x1 1.27 us: token_shards(): jnp.dot(gather, reorder, preferred_element_type=jnp.float32)]
    ppermute x2, starting transfers between devices: 0.72 us -> 2.6 us  [the longest x1 1.95 us: token_shards(): lax.ppermute(down_b, 'expert', [(i, 2 * i + 1 if i < half else 2 * (i - h...]
  transfers between devices with their start and end apart: 38 -> 39, of which waited for: 13 -> 13; matrix products, arithmetic and copies ran while one was open for 12% -> 0% of each run, Pallas kernels for 4% -> 10%
where the time goes in v3:
time: 127 us; the launch traced here: 126 us
  starting transfers between devices  44.3 us (35%)
  waiting for transfers between devices  32.4 us (26%)
  Pallas kernels  23.5 us (19%)
  blocking collectives  23.3 us (18%)
  between operations  1.74 us (1%)
    ppermute x35, starting transfers between devices, swap(): return lax.ppermute(value, axis, [(i, i ^ bit) for i in range(size)])  30.3 us
    ppermute x35, waiting for transfers between devices, swap(): return lax.ppermute(value, axis, [(i, i ^ bit) for i in range(size)])  27.6 us
    pallas_call x11, Pallas kernels, call(): pl.pallas_call(body, out_shape=out_shapes, in_specs=specs, out_specs=pl.B...  23.5 us
    all_to_all x1, blocking collectives, token_shards(): lax.all_to_all(pair_sum, both, split_axis=0, concat_axis=0, axis_index_gr...  23.3 us
    all_to_all x1, starting transfers between devices, token_shards(): lax.all_to_all(att_blocks, both, split_axis=0, concat_axis=0, axis_index_...  5.98 us
    all_to_all x1, starting transfers between devices, token_shards(): lax.all_to_all(partial_blocks, both, split_axis=0, concat_axis=0, axis_in...  5.42 us
    all_to_all x1, waiting for transfers between devices, token_shards(): lax.all_to_all(partial_blocks, both, split_axis=0, concat_axis=0, axis_in...  4.81 us
  transfers between devices with their start and end apart: 39, of which 13 were waited for; matrix products, arithmetic and copies ran while one was open for 0% of the time, Pallas kernels for 10%

profile of v3, /device:TPU:0, one launch (start us, length us, event | category | flops | bytes accessed | tf_op | source)
XLA Modules:
  0.0 126.4 jit_solution(5161758242659853608)
XLA Ops:
  1.2 2.4 %shard_map.203 = (bf16[1,16,2816]{2,1,0:T(8,128)(2,1)}, bf16[1,16,2816]{2,1,0:T(8,128)(2,1)}, bf16[1,16,2816]{2,1,0:T(8,128)(2,1)}, bf16[1,16,2816]{2,1,0:T(8,128)(2,1)}) custom-call(s32[3]{0:T(128)} %pad_add_fusion.refs_0_.place_ref, bf16[8,8,2048]{2,1,0:T(8,128)(2,1)} %refs_1_.1, bf16[8,32,128]{2,1,0:T(8,128)(2,1)} %refs_2_.2, bf16[1,2048]{1,0:T(2,128)(2,1)} %bitcast.21, ...), custom_call_target="tpu_custom_call" | custom-call | bytes 332196 | tf_op jit(solution)/shard_map/pallas_call | solution.py:266
  3.7 3.1 %collective-permute-start = (bf16[1,16,2816]{2,1,0:T(8,128)(2,1)}, bf16[1,16,2816]{2,1,0:T(8,128)(2,1)S(1)}, u32[]{:S(2)}, u32[]{:S(2)}) collective-permute-start(bf16[1,16,2816]{2,1,0:T(8,128)(2,1)} %get-tuple-element.51), channel_id=1, source_target_pairs={{0,4},{1,5},{2,6},{3,7},{4,0},{5,1},{6,2},{7,3},{8,12},{9,13},{10,... | collective-permute-start | bytes 270344 | tf_op jit(solution)/shard_map/ppermute | solution.py:222
  6.8 2.6 %collective-permute-start.1 = (bf16[1,16,2816]{2,1,0:T(8,128)(2,1)}, bf16[1,16,2816]{2,1,0:T(8,128)(2,1)S(1)}, u32[]{:S(2)}, u32[]{:S(2)}) collective-permute-start(bf16[1,16,2816]{2,1,0:T(8,128)(2,1)} %get-tuple-element.52), channel_id=1, source_target_pairs={{0,8},{1,9},{2,10},{3,11},{4,12},{5,13},{6,14},{7,15},{8,0},{9,1},... | collective-permute-start | bytes 270344 | tf_op jit(solution)/shard_map/ppermute | solution.py:222
  11.7 4.1 %shard_map.204 = bf16[8,16,1152]{2,1,0:T(8,128)(2,1)} custom-call(s32[1]{0:T(128)S(6)} %copy.24.refs_0_, bf16[16,16,576]{2,1,0:T(8,128)(2,1)} %refs_1_.2, bf16[16,576]{1,0:T(8,128)(2,1)} %refs_2_.3, bf16[1,16,576]{2,1,0:T(8,128)(2,1)} %refs_3_.1, bf16[1,576]{1,0:T(2,128)(2,1)} %refs_4_.1, bf16[1,576,1024]{2,1,0:T(8,128)(2,1)} %bitcast.18, f32[1,16]{1,0:T(1,128)} %bitcast.23), custom_call_target="tpu_custom_call" | custom-call | flops 100000000 | bytes 1512644 | tf_op jit(solution)/shard_map/pallas_call | solution.py:266
  15.9 6.0 %all-to-all-start = ((bf16[8,16,1152]{2,1,0:T(8,128)(2,1)}), bf16[8,16,1152]{2,1,0:T(8,128)(2,1)S(1)}, u32[]{:S(2)}, u32[]{:S(2)}) async-start(bf16[8,16,1152]{2,1,0:T(8,128)(2,1)} %shard_map.204), calls=%async_computation | async-start | bytes 589824 | tf_op jit(solution)/shard_map/all_to_all | solution.py:844
  23.8 5.0 %collective-permute-done.4.refs_4_ = bf16[3,16,2816]{2,1,0:T(8,128)(2,1)S(1)} collective-permute-done((bf16[3,16,2816]{2,1,0:T(8,128)(2,1)S(1)}, bf16[3,16,2816]{2,1,0:T(8,128)(2,1)S(1)}, u32[]{:S(2)}, u32[]{:S(2)}) %collective-permute-start.4) | collective-permute-done | bytes 270368 | tf_op jit(solution)/shard_map/ppermute | solution.py:222
  31.0 2.4 %collective-permute-start.9 = (bf16[4,96,128]{2,1,0:T(8,128)(2,1)S(1)}, bf16[4,96,128]{2,1,0:T(8,128)(2,1)S(1)}, u32[]{:S(2)}, u32[]{:S(2)}) collective-permute-start(bf16[4,96,128]{2,1,0:T(8,128)(2,1)S(1)} %get-tuple-element.67), channel_id=1, source_target_pairs={{0,8},{1,9},{2,10},{3,11},{4,12},{5,13},{6,14},{7,15},{8,0},{9,1},... | collective-permute-start | bytes 294920 | tf_op jit(solution)/shard_map/ppermute | solution.py:222
  34.1 3.0 %shard_map.206 = (bf16[8,16,2176]{2,1,0:T(8,128)(2,1)}, bf16[16,16,128]{2,1,0:T(8,128)(2,1)S(1)}, bf16[16,16,128]{2,1,0:T(8,128)(2,1)S(1)}) custom-call(s32[3]{0:T(128)S(1)} %copy-done.6, bf16[8,16,1152]{2,1,0:T(8,128)(2,1)S(1)} %all-to-all-done.refs_1_, bf16[4,16,2816]{2,1,0:T(8,128)(2,1)S(1)} %pad_maximum_fusion.refs_2_, ...), custom_call_target="tpu_custom_call" | custom-call | flops 300000000 | bytes 1736716 | tf_op jit(solution)/shard_map/pallas_call | solution.py:266
  37.1 5.4 %all-to-all-start.1 = ((bf16[8,16,2176]{2,1,0:T(8,128)(2,1)}), bf16[8,16,2176]{2,1,0:T(8,128)(2,1)S(1)}, u32[]{:S(2)}, u32[]{:S(2)}) async-start(bf16[8,16,2176]{2,1,0:T(8,128)(2,1)} %get-tuple-element.64), calls=%async_computation.1 | async-start | bytes 1114112 | tf_op jit(solution)/shard_map/all_to_all | solution.py:888
  42.5 2.1 %collective-permute-start.12 = (bf16[16,16,128]{2,1,0:T(8,128)(2,1)S(1)}, bf16[16,16,128]{2,1,0:T(8,128)(2,1)S(1)}, u32[]{:S(2)}, u32[]{:S(2)}) collective-permute-start(bf16[16,16,128]{2,1,0:T(8,128)(2,1)S(1)} %get-tuple-element.73.plane_ref), channel_id=1, source_target_pairs={{0,16},{16,0},{1,17},{17,1},{2,18},{18,2},{3,19},{19,3},{4,20},{20... | collective-permute-start | bytes 196616 | tf_op jit(solution)/shard_map/ppermute | solution.py:222
  45.3 2.7 %collective-permute-done.12.other_ref = bf16[16,16,128]{2,1,0:T(8,128)(2,1)S(1)} collective-permute-done((bf16[16,16,128]{2,1,0:T(8,128)(2,1)S(1)}, bf16[16,16,128]{2,1,0:T(8,128)(2,1)S(1)}, u32[]{:S(2)}, u32[]{:S(2)}) %collective-permute-start.12) | collective-permute-done | bytes 65568 | tf_op jit(solution)/shard_map/ppermute | solution.py:222
  48.0 2.8 %shard_map.207 = (bf16[224,544]{1,0:T(8,128)(2,1)S(1)}, bf16[544,224]{1,0:T(8,128)(2,1)S(1)}, bf16[544,128]{1,0:T(8,128)(2,1)S(1)}) custom-call(s32[3]{0:T(128)S(1)} %copy-done.6, bf16[16,16,128]{2,1,0:T(8,128)(2,1)S(1)} %get-tuple-element.73.plane_ref, bf16[16,16,128]{2,1,0:T(8,128)(2,1)S(1)} %collective-permute-done.12.other_ref), custom_call_target="tpu_custom_call" | custom-call | bytes 131084 | tf_op jit(solution)/shard_map/pallas_call | solution.py:266
  53.1 4.8 %all-to-all-done.1.partial_ref = bf16[8,16,2176]{2,1,0:T(8,128)(2,1)S(1)} async-done(((bf16[8,16,2176]{2,1,0:T(8,128)(2,1)}), bf16[8,16,2176]{2,1,0:T(8,128)(2,1)S(1)}, u32[]{:S(2)}, u32[]{:S(2)}) %all-to-all-start.1) | async-done | bytes 557088 | tf_op jit(solution)/shard_map/all_to_all | solution.py:888
  58.1 2.1 %collective-permute-start.16 = (bf16[16,2176]{1,0:T(8,128)(2,1)S(1)}, bf16[16,2176]{1,0:T(8,128)(2,1)S(1)}, u32[]{:S(2)}, u32[]{:S(2)}) collective-permute-start(bf16[16,2176]{1,0:T(8,128)(2,1)S(1)} %get-tuple-element.84), channel_id=1, source_target_pairs={{0,12},{1,13},{2,14},{3,15},{4,8},{5,9},{6,10},{7,11},{8,4},{9,5},... | collective-permute-start | bytes 208904 | tf_op jit(solution)/shard_map/ppermute | solution.py:222
  60.2 2.4 %collective-permute-start.14 = (bf16[16,2176]{1,0:T(8,128)(2,1)S(1)}, bf16[16,2176]{1,0:T(8,128)(2,1)S(1)}, u32[]{:S(2)}, u32[]{:S(2)}) collective-permute-start(bf16[16,2176]{1,0:T(8,128)(2,1)S(1)} %get-tuple-element.84), channel_id=1, source_target_pairs={{0,4},{1,5},{2,6},{3,7},{4,0},{5,1},{6,2},{7,3},{8,12},{9,13},{10,... | collective-permute-start | bytes 208904 | tf_op jit(solution)/shard_map/ppermute | solution.py:222
  62.6 2.9 %collective-permute-done.14 = bf16[16,2176]{1,0:T(8,128)(2,1)S(1)} collective-permute-done((bf16[16,2176]{1,0:T(8,128)(2,1)S(1)}, bf16[16,2176]{1,0:T(8,128)(2,1)S(1)}, u32[]{:S(2)}, u32[]{:S(2)}) %collective-permute-start.14) | collective-permute-done | bytes 69664 | tf_op jit(solution)/shard_map/ppermute | solution.py:222
  69.7 2.3 %collective-permute-done.19.rest_4_ = bf16[32,2176]{1,0:T(8,128)(2,1)S(1)} collective-permute-done((bf16[32,2176]{1,0:T(8,128)(2,1)S(1)}, bf16[32,2176]{1,0:T(8,128)(2,1)S(1)}, u32[]{:S(2)}, u32[]{:S(2)}) %collective-permute-start.19) | collective-permute-done | bytes 139296 | tf_op jit(solution)/shard_map/ppermute | solution.py:222
  75.7 2.4 %collective-permute-done.21.rest_6_ = bf16[32,2176]{1,0:T(8,128)(2,1)S(1)} collective-permute-done((bf16[32,2176]{1,0:T(8,128)(2,1)S(1)}, bf16[32,2176]{1,0:T(8,128)(2,1)S(1)}, u32[]{:S(2)}, u32[]{:S(2)}) %collective-permute-start.21) | collective-permute-done | bytes 139296 | tf_op jit(solution)/shard_map/ppermute | solution.py:222
  81.2 5.0 %shard_map.210 = (bf16[224,384]{1,0:T(8,128)(2,1)S(1)}, bf16[272,128]{1,0:T(8,128)(2,1)S(1)}, bf16[224,2048]{1,0:T(8,128)(2,1)S(1)}, f32[224,128]{1,0:T(8,128)S(1)}) custom-call(bf16[128,2048]{1,0:T(8,128)(2,1)S(1)} %shard_map.208.small_ref, bf16[224,544]{1,0:T(8,128)(2,1)S(1)} %get-tuple-element.81.select_ref, ...), custom_call_target="tpu_custom_call" | custom-call | flops 2000000000 | bytes 8902656 | tf_op jit(solution)/shard_map/pallas_call | solution.py:266
  90.2 1.9 %collective-permute-start.35 = (bf16[44,1024]{1,0:T(8,128)(2,1)S(1)}, bf16[44,1024]{1,0:T(8,128)(2,1)S(1)}, u32[]{:S(2)}, u32[]{:S(2)}) collective-permute-start(bf16[44,1024]{1,0:T(8,128)(2,1)S(1)} %get-tuple-element.93), channel_id=1, source_target_pairs={{0,1},{1,3},{2,5},{3,7},{4,9},{5,11},{6,13},{7,15},{8,0},{9,2},{10... | collective-permute-start | bytes 270344 | tf_op jit(solution)/shard_map/ppermute | solution.py:950
  92.9 4.8 %collective-permute-done.33.shared_other_ref = bf16[272,128]{1,0:T(8,128)(2,1)S(1)} collective-permute-done((bf16[272,128]{1,0:T(8,128)(2,1)S(1)}, bf16[272,128]{1,0:T(8,128)(2,1)S(1)}, u32[]{:S(2)}, u32[]{:S(2)}) %collective-permute-start.33) | collective-permute-done | bytes 69664 | tf_op jit(solution)/shard_map/ppermute | solution.py:222
  97.8 2.4 %shard_map.212 = (bf16[16,16,1152]{2,1,0:T(8,128)(2,1)S(1)}, bf16[16,16,1152]{2,1,0:T(8,128)(2,1)S(1)}) custom-call(s32[3]{0:T(128)S(1)} %copy-done.6, bf16[224,384]{1,0:T(8,128)(2,1)S(1)} %get-tuple-element.88.act_a_ref, bf16[224,320]{1,0:T(8,128)(2,1)S(1)} %shard_map.211.act_b_ref, bf16[224,384]{1,0:T(8,128)(2,1)S(1)} %collective-permute-done.31.other_a_ref, ...), custom_call_target="tpu_custom_call" | custom-call | flops 1000000000 | bytes 4077580 | tf_op jit(solution)/shard_map/pallas_call | solution.py:266
  100.3 1.9 %collective-permute-done.36 = bf16[16,16,1152]{2,1,0:T(8,128)(2,1)S(1)} collective-permute-done((bf16[16,16,1152]{2,1,0:T(8,128)(2,1)S(1)}, bf16[16,16,1152]{2,1,0:T(8,128)(2,1)S(1)}, u32[]{:S(2)}, u32[]{:S(2)}) %collective-permute-start.36) | collective-permute-done | bytes 589856 | tf_op jit(solution)/shard_map/ppermute | solution.py:222
  102.4 23.3 %all_to_all.15.got_ref = bf16[16,16,1152]{2,1,0:T(8,128)(2,1)S(1)} all-to-all(bf16[16,16,1152]{2,1,0:T(8,128)(2,1)S(1)} %add_convert_fusion), channel_id=1, replica_groups={{0,2,4,6,8,10,12,14,16,18,20,22,24,26,28,30},{1,3,5,7,9,11,13,15,17,19,..., dimensions={0} | all-to-all | bytes 1179648 | tf_op jit(solution)/shard_map/all_to_all | solution.py:975
  (107 shorter events, 27.1 us)
Async XLA Ops:
  3.7 18.2 %collective-permute-start = (bf16[1,16,2816]{2,1,0:T(8,128)(2,1)}, bf16[1,16,2816]{2,1,0:T(8,128)(2,1)S(1)}, u32[]{:S(2)}, u32[]{:S(2)}) collective-permute-start(bf16[1,16,2816]{2,1,0:T(8,128)(2,1)} %get-tuple-element.51), channel_id=1, source_target_pairs={{0,4},{1,5},{2,6},{3,7},{4,0},{5,1},{6,2},{7,3},{8,12},{9,13},{10,... | collective-permute-start | bytes 270344 | tf_op jit(solution)/shard_map/ppermute | solution.py:222
  6.8 15.1 %collective-permute-start.1 = (bf16[1,16,2816]{2,1,0:T(8,128)(2,1)}, bf16[1,16,2816]{2,1,0:T(8,128)(2,1)S(1)}, u32[]{:S(2)}, u32[]{:S(2)}) collective-permute-start(bf16[1,16,2816]{2,1,0:T(8,128)(2,1)} %get-tuple-element.52), channel_id=1, source_target_pairs={{0,8},{1,9},{2,10},{3,11},{4,12},{5,13},{6,14},{7,15},{8,0},{9,1},... | collective-permute-start | bytes 270344 | tf_op jit(solution)/shard_map/ppermute | solution.py:222
  9.3 12.5 %collective-permute-start.2 = (bf16[1,16,2816]{2,1,0:T(8,128)(2,1)}, bf16[1,16,2816]{2,1,0:T(8,128)(2,1)S(1)}, u32[]{:S(2)}, u32[]{:S(2)}) collective-permute-start(bf16[1,16,2816]{2,1,0:T(8,128)(2,1)} %get-tuple-element.53), channel_id=1, source_target_pairs={{0,12},{1,13},{2,14},{3,15},{4,8},{5,9},{6,10},{7,11},{8,4},{9,5},... | collective-permute-start | bytes 270344 | tf_op jit(solution)/shard_map/ppermute | solution.py:222
  9.3 12.6 %collective-permute-start.3 = (bf16[1,16,2816]{2,1,0:T(8,128)(2,1)}, bf16[1,16,2816]{2,1,0:T(8,128)(2,1)S(1)}, u32[]{:S(2)}, u32[]{:S(2)}) collective-permute-start(bf16[1,16,2816]{2,1,0:T(8,128)(2,1)} %get-tuple-element.50), channel_id=1, source_target_pairs={{0,2},{1,3},{2,0},{3,1},{4,6},{5,7},{6,4},{7,5},{8,10},{9,11},{10,... | collective-permute-start | bytes 270344 | tf_op jit(solution)/shard_map/ppermute | solution.py:222
  15.9 18.2 %all-to-all-start = ((bf16[8,16,1152]{2,1,0:T(8,128)(2,1)}), bf16[8,16,1152]{2,1,0:T(8,128)(2,1)S(1)}, u32[]{:S(2)}, u32[]{:S(2)}) async-start(bf16[8,16,1152]{2,1,0:T(8,128)(2,1)} %shard_map.204), calls=%async_computation | async-start | bytes 589824 | tf_op jit(solution)/shard_map/all_to_all | solution.py:844
  21.9 6.9 %collective-permute-start.4 = (bf16[3,16,2816]{2,1,0:T(8,128)(2,1)S(1)}, bf16[3,16,2816]{2,1,0:T(8,128)(2,1)S(1)}, u32[]{:S(2)}, u32[]{:S(2)}) collective-permute-start(bf16[3,16,2816]{2,1,0:T(8,128)(2,1)S(1)} %pad_maximum_fusion.1), channel_id=1, source_target_pairs={{0,2},{1,3},{2,0},{3,1},{4,6},{5,7},{6,4},{7,5},{8,10},{9,11},{10,... | collective-permute-start | bytes 811016 | tf_op jit(solution)/shard_map/ppermute | solution.py:222
  22.6 11.5 %collective-permute-start.5 = (bf16[4,16,2816]{2,1,0:T(8,128)(2,1)S(1)}, bf16[4,16,2816]{2,1,0:T(8,128)(2,1)S(1)}, u32[]{:S(2)}, u32[]{:S(2)}) collective-permute-start(bf16[4,16,2816]{2,1,0:T(8,128)(2,1)S(1)} %pad_maximum_fusion.refs_2_), channel_id=1, source_target_pairs={{0,1},{1,0},{2,3},{3,2},{4,5},{5,4},{6,7},{7,6},{8,9},{9,8},{10,11... | collective-permute-start | bytes 1081352 | tf_op jit(solution)/shard_map/ppermute | solution.py:222
  29.3 13.2 %collective-permute-start.8 = (bf16[4,96,128]{2,1,0:T(8,128)(2,1)S(1)}, bf16[4,96,128]{2,1,0:T(8,128)(2,1)S(1)}, u32[]{:S(2)}, u32[]{:S(2)}) collective-permute-start(bf16[4,96,128]{2,1,0:T(8,128)(2,1)S(1)} %get-tuple-element.66), channel_id=1, source_target_pairs={{0,4},{1,5},{2,6},{3,7},{4,0},{5,1},{6,2},{7,3},{8,12},{9,13},{10,... | collective-permute-start | bytes 294920 | tf_op jit(solution)/shard_map/ppermute | solution.py:222
  31.0 11.5 %collective-permute-start.9 = (bf16[4,96,128]{2,1,0:T(8,128)(2,1)S(1)}, bf16[4,96,128]{2,1,0:T(8,128)(2,1)S(1)}, u32[]{:S(2)}, u32[]{:S(2)}) collective-permute-start(bf16[4,96,128]{2,1,0:T(8,128)(2,1)S(1)} %get-tuple-element.67), channel_id=1, source_target_pairs={{0,8},{1,9},{2,10},{3,11},{4,12},{5,13},{6,14},{7,15},{8,0},{9,1},... | collective-permute-start | bytes 294920 | tf_op jit(solution)/shard_map/ppermute | solution.py:222
  33.4 9.1 %collective-permute-start.10 = (bf16[4,96,128]{2,1,0:T(8,128)(2,1)S(1)}, bf16[4,96,128]{2,1,0:T(8,128)(2,1)S(1)}, u32[]{:S(2)}, u32[]{:S(2)}) collective-permute-start(bf16[4,96,128]{2,1,0:T(8,128)(2,1)S(1)} %get-tuple-element.68), channel_id=1, source_target_pairs={{0,12},{1,13},{2,14},{3,15},{4,8},{5,9},{6,10},{7,11},{8,4},{9,5},... | collective-permute-start | bytes 294920 | tf_op jit(solution)/shard_map/ppermute | solution.py:222
  37.1 20.8 %all-to-all-start.1 = ((bf16[8,16,2176]{2,1,0:T(8,128)(2,1)}), bf16[8,16,2176]{2,1,0:T(8,128)(2,1)S(1)}, u32[]{:S(2)}, u32[]{:S(2)}) async-start(bf16[8,16,2176]{2,1,0:T(8,128)(2,1)} %get-tuple-element.64), calls=%async_computation.1 | async-start | bytes 1114112 | tf_op jit(solution)/shard_map/all_to_all | solution.py:888
  44.7 6.1 %collective-permute-start.11 = (bf16[8,96,128]{2,1,0:T(8,128)(2,1)S(1)}, bf16[8,96,128]{2,1,0:T(8,128)(2,1)S(1)}, u32[]{:S(2)}, u32[]{:S(2)}) collective-permute-start(bf16[8,96,128]{2,1,0:T(8,128)(2,1)S(1)} %pad_maximum_fusion.2), channel_id=1, source_target_pairs={{0,2},{1,3},{2,0},{3,1},{4,6},{5,7},{6,4},{7,5},{8,10},{9,11},{10,... | collective-permute-start | bytes 589832 | tf_op jit(solution)/shard_map/ppermute | solution.py:222
  58.1 8.8 %collective-permute-start.16 = (bf16[16,2176]{1,0:T(8,128)(2,1)S(1)}, bf16[16,2176]{1,0:T(8,128)(2,1)S(1)}, u32[]{:S(2)}, u32[]{:S(2)}) collective-permute-start(bf16[16,2176]{1,0:T(8,128)(2,1)S(1)} %get-tuple-element.84), channel_id=1, source_target_pairs={{0,12},{1,13},{2,14},{3,15},{4,8},{5,9},{6,10},{7,11},{8,4},{9,5},... | collective-permute-start | bytes 208904 | tf_op jit(solution)/shard_map/ppermute | solution.py:222
  60.2 6.7 %collective-permute-start.15 = (bf16[16,2176]{1,0:T(8,128)(2,1)S(1)}, bf16[16,2176]{1,0:T(8,128)(2,1)S(1)}, u32[]{:S(2)}, u32[]{:S(2)}) collective-permute-start(bf16[16,2176]{1,0:T(8,128)(2,1)S(1)} %get-tuple-element.84), channel_id=1, source_target_pairs={{0,8},{1,9},{2,10},{3,11},{4,12},{5,13},{6,14},{7,15},{8,0},{9,1},... | collective-permute-start | bytes 208904 | tf_op jit(solution)/shard_map/ppermute | solution.py:222
  65.5 6.5 %collective-permute-start.19 = (bf16[32,2176]{1,0:T(8,128)(2,1)S(1)}, bf16[32,2176]{1,0:T(8,128)(2,1)S(1)}, u32[]{:S(2)}, u32[]{:S(2)}) collective-permute-start(bf16[32,2176]{1,0:T(8,128)(2,1)S(1)} %constant_dynamic-update-slice_fusion.rest_0_), channel_id=1, source_target_pairs={{0,16},{16,0},{1,17},{17,1},{2,18},{18,2},{3,19},{19,3},{4,20},{20... | collective-permute-start | bytes 417800 | tf_op jit(solution)/shard_map/ppermute | solution.py:222
  66.4 6.4 %collective-permute-start.17 = (bf16[32,2176]{1,0:T(8,128)(2,1)S(1)}, bf16[32,2176]{1,0:T(8,128)(2,1)S(1)}, u32[]{:S(2)}, u32[]{:S(2)}) collective-permute-start(bf16[32,2176]{1,0:T(8,128)(2,1)S(1)} %constant_dynamic-update-slice_fusion.rest_0_), channel_id=1, source_target_pairs={{0,2},{1,3},{2,0},{3,1},{4,6},{5,7},{6,4},{7,5},{8,10},{9,11},{10,... | collective-permute-start | bytes 417800 | tf_op jit(solution)/shard_map/ppermute | solution.py:222
  66.9 7.6 %collective-permute-start.20 = (bf16[32,2176]{1,0:T(8,128)(2,1)S(1)}, bf16[32,2176]{1,0:T(8,128)(2,1)S(1)}, u32[]{:S(2)}, u32[]{:S(2)}) collective-permute-start(bf16[32,2176]{1,0:T(8,128)(2,1)S(1)} %constant_dynamic-update-slice_fusion.2.rest_1_), channel_id=1, source_target_pairs={{0,16},{16,0},{1,17},{17,1},{2,18},{18,2},{3,19},{19,3},{4,20},{20... | collective-permute-start | bytes 417800 | tf_op jit(solution)/shard_map/ppermute | solution.py:222
  68.2 6.9 %collective-permute-start.24 = (bf16[32,2176]{1,0:T(8,128)(2,1)S(1)}, bf16[32,2176]{1,0:T(8,128)(2,1)S(1)}, u32[]{:S(2)}, u32[]{:S(2)}) collective-permute-start(bf16[32,2176]{1,0:T(8,128)(2,1)S(1)} %constant_dynamic-update-slice_fusion.2.rest_1_), channel_id=1, source_target_pairs={{0,1},{1,0},{2,3},{3,2},{4,5},{5,4},{6,7},{7,6},{8,9},{9,8},{10,11... | collective-permute-start | bytes 417800 | tf_op jit(solution)/shard_map/ppermute | solution.py:222
  68.2 6.9 %collective-permute-start.18 = (bf16[32,2176]{1,0:T(8,128)(2,1)S(1)}, bf16[32,2176]{1,0:T(8,128)(2,1)S(1)}, u32[]{:S(2)}, u32[]{:S(2)}) collective-permute-start(bf16[32,2176]{1,0:T(8,128)(2,1)S(1)} %constant_dynamic-update-slice_fusion.2.rest_1_), channel_id=1, source_target_pairs={{0,2},{1,3},{2,0},{3,1},{4,6},{5,7},{6,4},{7,5},{8,10},{9,11},{10,... | collective-permute-start | bytes 417800 | tf_op jit(solution)/shard_map/ppermute | solution.py:222
  86.2 11.6 %collective-permute-start.31 = (bf16[224,384]{1,0:T(8,128)(2,1)S(1)}, bf16[224,384]{1,0:T(8,128)(2,1)S(1)}, u32[]{:S(2)}, u32[]{:S(2)}) collective-permute-start(bf16[224,384]{1,0:T(8,128)(2,1)S(1)} %get-tuple-element.88.act_a_ref), channel_id=1, source_target_pairs={{0,16},{16,0},{1,17},{17,1},{2,18},{18,2},{3,19},{19,3},{4,20},{20... | collective-permute-start | bytes 516104 | tf_op jit(solution)/shard_map/ppermute | solution.py:222
  88.2 9.5 %collective-permute-start.32 = (bf16[224,320]{1,0:T(8,128)(2,1)S(1)}, bf16[224,320]{1,0:T(8,128)(2,1)S(1)}, u32[]{:S(2)}, u32[]{:S(2)}) collective-permute-start(bf16[224,320]{1,0:T(8,128)(2,1)S(1)} %shard_map.211.act_b_ref), channel_id=1, source_target_pairs={{0,16},{16,0},{1,17},{17,1},{2,18},{18,2},{3,19},{19,3},{4,20},{20... | collective-permute-start | bytes 430088 | tf_op jit(solution)/shard_map/ppermute | solution.py:222
  89.5 8.2 %collective-permute-start.34 = (bf16[44,1024]{1,0:T(8,128)(2,1)S(1)}, bf16[44,1024]{1,0:T(8,128)(2,1)S(1)}, u32[]{:S(2)}, u32[]{:S(2)}) collective-permute-start(bf16[44,1024]{1,0:T(8,128)(2,1)S(1)} %get-tuple-element.92), channel_id=1, source_target_pairs={{0,0},{1,2},{2,4},{3,6},{4,8},{5,10},{6,12},{7,14},{8,1},{9,3},{10... | collective-permute-start | bytes 270344 | tf_op jit(solution)/shard_map/ppermute | solution.py:945
  90.2 7.6 %collective-permute-start.35 = (bf16[44,1024]{1,0:T(8,128)(2,1)S(1)}, bf16[44,1024]{1,0:T(8,128)(2,1)S(1)}, u32[]{:S(2)}, u32[]{:S(2)}) collective-permute-start(bf16[44,1024]{1,0:T(8,128)(2,1)S(1)} %get-tuple-element.93), channel_id=1, source_target_pairs={{0,1},{1,3},{2,5},{3,7},{4,9},{5,11},{6,13},{7,15},{8,0},{9,2},{10... | collective-permute-start | bytes 270344 | tf_op jit(solution)/shard_map/ppermute | solution.py:950
  92.1 5.6 %collective-permute-start.33 = (bf16[272,128]{1,0:T(8,128)(2,1)S(1)}, bf16[272,128]{1,0:T(8,128)(2,1)S(1)}, u32[]{:S(2)}, u32[]{:S(2)}) collective-permute-start(bf16[272,128]{1,0:T(8,128)(2,1)S(1)} %get-tuple-element.91.shared_ref), channel_id=1, source_target_pairs={{0,16},{16,0},{1,17},{17,1},{2,18},{18,2},{3,19},{19,3},{4,20},{20... | collective-permute-start | bytes 208904 | tf_op jit(solution)/shard_map/ppermute | solution.py:222
  (26 other events, 196.1 us)

commit v4 on v3

--- a/solution.py
+++ b/solution.py
@@ -222,6 +222,11 @@
     return lax.ppermute(value, axis, [(i, i ^ bit) for i in range(size)])
 
 
+def line_swaps(blocks, inner):
+    got = {i: swap(blocks[i], "expert", i * inner) for i in reversed(range(1, len(blocks)))}
+    return [blocks[0]] + [got[i] for i in range(1, len(blocks))]
+
+
 def call(kernel, out_shapes, args, scratch=(), scalars=0, flops=0, vmem=10, moved=(), late=(), rows=None):
     specs = []
     for i in range(len(args)):
@@ -434,7 +439,9 @@
 
 
 def project_kernel(place_ref, att_ref, *rest):
-    piece_refs, (out_ref, router_ref, routes_ref, rows_ref, fold_ref, uv_ref) = rest[:-6], rest[-6:]
+    piece_refs, outs = rest[:-7], rest[-7:]
+    kept_ref, sent_ref, router_ref, routes_ref, rows_ref, fold_ref, uv_ref = outs
+    group, outer = place_ref[1], place_ref[0] // place_ref[2]
     pieces = [(ref, i) for ref in piece_refs for i in range(ref.shape[0])]
     for step, (ref, i) in enumerate(pieces):
         router_ref[step] = ref[i, :, -2 * LANES : -LANES]
@@ -484,12 +491,27 @@
     out_rows = jnp.concatenate([ref[i, :, :D] for ref, i in pieces], axis=0)
     partial_rows = jnp.dot(head_values, out_rows, preferred_element_type=jnp.float32)
     split = blocks * span
-    out_ref[:, :, :D] = partial_rows[:split].astype(jnp.bfloat16).reshape(blocks, span, D)
     for part in range(TILE):
         fold_ref[pl.ds(part, blocks, stride=TILE), :] = partial_rows[
             split : split + blocks, part * LANES : (part + 1) * LANES
         ]
-    out_ref[:, :, D:] = fold_ref[...].astype(jnp.bfloat16).reshape(blocks, TILE, LANES)
+    for block in range(blocks):
+        rows = slice(block * TILE, (block + 1) * TILE)
+        step = (block % OUTER) ^ outer
+
+        def store(ref):
+            ref[step, :, :D] = partial_rows[rows].astype(jnp.bfloat16)
+            ref[step, :, D:] = fold_ref[rows].astype(jnp.bfloat16)
+
+        pl.when(group == block // OUTER)(partial(store, kept_ref))
+        pl.when(group != block // OUTER)(partial(store, sent_ref))
+
+
+def pair_kernel(kept_ref, other_ref, *out_refs):
+    for step, out_ref in enumerate(out_refs):
+        out_ref[...] = (
+            kept_ref[step].astype(jnp.float32) + other_ref[step].astype(jnp.float32)
+        ).astype(jnp.bfloat16)
 
 
 def chain_offset(step, members):
@@ -578,10 +600,11 @@
     return last * members + (home_group ^ group) * half + member // 2
 
 
-def norm_kernel(partial_ref, resid_ref, gain_ref, hidden_ref, normed_ref):
-    summed = partial_ref[0].astype(jnp.float32)
-    for i in range(1, partial_ref.shape[0]):
-        summed = summed + partial_ref[i].astype(jnp.float32)
+def norm_kernel(resid_ref, gain_ref, *rest):
+    partial_refs, (hidden_ref, normed_ref) = rest[:-2], rest[-2:]
+    summed = partial_refs[0][...].astype(jnp.float32)
+    for ref in partial_refs[1:]:
+        summed = summed + ref[...].astype(jnp.float32)
     hidden = (resid_ref[...].astype(jnp.float32) + summed).astype(jnp.bfloat16)
     hidden_ref[...] = hidden
     hidden = hidden.astype(jnp.float32)
@@ -593,9 +616,8 @@
     normed_ref[:, D:] = (dec * lax.rsqrt(dec_mean + NORM_EPS) * gain[:, D:]).astype(jnp.bfloat16)
 
 
-def expert_kernel(units, small_ref, select_ref, chosen_ref, gate_ref, up_ref, *rest):
-    piece_refs, outs = rest[:-7], rest[-7:]
-    act_ref, shared_ref, rows_ref, weight_ref, fold_ref, pre_ref, dec_ref = outs
+def expert_kernel(select_ref, gate_ref, up_ref, *rest):
+    piece_refs, (act_ref, pre_ref, dec_ref, fold_ref) = rest[:-4], rest[-4:]
     pre_total = pre_ref.shape[0]
     homes = pre_total // TILE
     row = 0
@@ -608,18 +630,32 @@
         dec_ref[:, part * LANES : (part + 1) * LANES] = fold_ref[
             pl.ds(part, homes, stride=TILE), :
         ].astype(jnp.bfloat16)
-    pre = pre_ref[...]
-    dec = dec_ref[...]
+    select = select_ref[...]
+    rows = (
+        jnp.dot(select[:, :pre_total], pre_ref[...], preferred_element_type=jnp.float32)
+        + jnp.dot(select[:, pre_total:], dec_ref[...], preferred_element_type=jnp.float32)
+    ).astype(jnp.bfloat16)
+    gate = lax.dot_general(rows, gate_ref[0], ROWS_CONTRACT, preferred_element_type=jnp.float32)
+    up = lax.dot_general(rows, up_ref[0], ROWS_CONTRACT, preferred_element_type=jnp.float32)
+    act_ref[...] = (gate / (1.0 + jnp.exp(-gate)) * up).astype(jnp.bfloat16)
+
+
+def shared_kernel(
+    units, members, small_ref, select_ref, chosen_ref, pre_ref, dec_ref, shared_ref, weight_ref
+):
+    pre_total = pre_ref.shape[0]
+    homes = pre_total // TILE
     small = small_ref[...]
     first = jnp.concatenate(
         [
-            lax.dot_general(pre, small, ROWS_CONTRACT, preferred_element_type=jnp.float32),
-            lax.dot_general(dec, small, ROWS_CONTRACT, preferred_element_type=jnp.float32),
+            lax.dot_general(
+                ref[...], small, ROWS_CONTRACT, preferred_element_type=jnp.float32
+            )
+            for ref in (pre_ref, dec_ref)
         ],
         axis=0,
     )
     half = LANES // 2
-    members = len(piece_refs)
     gate_part = first[:, :units]
     up_part = first[:, half : half + units]
     shared_act = (gate_part / (1.0 + jnp.exp(-gate_part)) * up_part).astype(jnp.bfloat16)
@@ -641,46 +677,28 @@
     rest = token_weight - high.astype(jnp.float32)
     middle = rest.astype(jnp.bfloat16)
     rest = (rest - middle.astype(jnp.float32)).astype(jnp.bfloat16)
-    select = select_ref[...]
     weights = jnp.dot(
-        select, jnp.concatenate([high, middle, rest], axis=1), preferred_element_type=jnp.float32
+        select_ref[...],
+        jnp.concatenate([high, middle, rest], axis=1),
+        preferred_element_type=jnp.float32,
     )
     weight_ref[...] = jnp.broadcast_to(jnp.sum(weights, axis=1, keepdims=True), weight_ref.shape)
-    rows_ref[...] = (
-        jnp.dot(select[:, :pre_total], pre, preferred_element_type=jnp.float32)
-        + jnp.dot(select[:, pre_total:], dec, preferred_element_type=jnp.float32)
-    ).astype(jnp.bfloat16)
-    hidden_kernel(0, rows_ref, weight_ref, gate_ref, up_ref, act_ref)
-
-
-def hidden_kernel(start, rows_ref, weight_ref, gate_ref, up_ref, act_ref):
-    rows = rows_ref[...]
-    count = act_ref.shape[1]
-    gate = lax.dot_general(
-        rows, gate_ref[0, start : start + count], ROWS_CONTRACT, preferred_element_type=jnp.float32
-    )
-    up = lax.dot_general(
-        rows, up_ref[0, start : start + count], ROWS_CONTRACT, preferred_element_type=jnp.float32
-    )
-    act_ref[...] = (gate / (1.0 + jnp.exp(-gate)) * up * weight_ref[:, :1]).astype(jnp.bfloat16)
 
 
 def down_kernel(
-    place_ref, act_a_ref, act_b_ref, other_a_ref, other_b_ref, shared_ref, shared_other_ref,
-    down_ref, down_a_ref, down_b_ref, scatter_ref, kept_ref, sent_ref, fold_ref,
+    place_ref, act_ref, act_other_ref, shared_ref, shared_other_ref,
+    down_ref, down_a_ref, down_b_ref, scatter_ref, weight_ref, kept_ref, sent_ref, fold_ref,
 ):
     me, group = place_ref[0], place_ref[1]
     columns = down_ref.shape[2]
     units = down_a_ref.shape[0]
     width = down_ref.shape[1] // 2
-    routed = jnp.zeros((act_a_ref.shape[0], columns), jnp.float32)
-    for refs, which in (((act_a_ref, act_b_ref), group), ((other_a_ref, other_b_ref), 1 - group)):
-        row = which * width
-        for ref in refs:
-            rows = down_ref[0, pl.ds(pl.multiple_of(row, TILE), ref.shape[1]), :]
-            routed = routed + jnp.dot(ref[...], rows, preferred_element_type=jnp.float32)
-            row = row + ref.shape[1]
-    routed = routed.astype(jnp.bfloat16)
+    own = down_ref[0, pl.ds(pl.multiple_of(group * width, TILE), width), :]
+    other = down_ref[0, pl.ds(pl.multiple_of((1 - group) * width, TILE), width), :]
+    routed = jnp.dot(act_ref[...], own, preferred_element_type=jnp.float32) + jnp.dot(
+        act_other_ref[...], other, preferred_element_type=jnp.float32
+    )
+    routed = (routed * weight_ref[:, :1]).astype(jnp.bfloat16)
     mine_first = lax.rem(me, 2) == group
     own_down = jnp.where(mine_first, down_a_ref[...], down_b_ref[...])
     other_down = jnp.where(mine_first, down_b_ref[...], down_a_ref[...])
@@ -793,27 +811,13 @@
         scratch=[pltpu.VMEM((TILE, 2 * LANES), jnp.float32)],
         scalars=1,
         moved=(1, 2, 3, 4),
-        vmem=60,
+        flops=10_000_000_000,
     )
     pair_bit = inner // 2
-    near = [blocks[0]] + [swap(blocks[i], "expert", i * inner) for i in range(1, OUTER)]
+    near = line_swaps(blocks, inner)
     own_pair = swap(blocks[0], "expert", pair_bit)
     line = jnp.concatenate(near, axis=0)
     far_in, own_pair = lax.optimization_barrier((line[1:], own_pair))
-    far_pair = swap(far_in, "expert", pair_bit)
-    units = shared_gate.shape[1] // members
-    padded = -(-units // TILE) * TILE
-    depth = shared_gate.shape[0]
-    line, line_gate = lax.optimization_barrier((line, shared_gate))
-    *spread, down_a, down_b = call(
-        partial(spread_kernel, units),
-        [low((inner, 2 * padded, depth))] * OUTER + [low((units, shared_down.shape[1]))] * 2,
-        [place_ids, line_gate.T, shared_up.T, shared_down],
-        scalars=1,
-    )
-    far_pair, *spread = lax.optimization_barrier((far_pair, *spread))
-    pieces = [line, own_pair, far_pair]
-    pieces = pieces + [swap(piece, "expert", 1) for piece in pieces]
 
     pre_query, blocks = lax.optimization_barrier((pre_query, blocks))
     peers = groups * OUTER
@@ -833,20 +837,32 @@
         ],
         scalars=1,
         flops=100_000_000,
-        moved=(1, 2, 3, 4, 5),
-        vmem=60,
     )
     lines = [
         [g * members + o * inner + i for g in range(groups) for o in range(OUTER)]
         for i in range(inner)
     ]
     both = ("dp", "expert")
+    far_pair = swap(far_in, "expert", pair_bit)
     att_got = lax.all_to_all(
         att_blocks, both, split_axis=0, concat_axis=0, axis_index_groups=lines, tiled=True
     )
-    partial_blocks, router_blocks, routes_plane = call(
+    units = shared_gate.shape[1] // members
+    padded = -(-units // TILE) * TILE
+    depth = shared_gate.shape[0]
+    line, line_gate = lax.optimization_barrier((line, shared_gate))
+    *spread, down_a, down_b = call(
+        partial(spread_kernel, units),
+        [low((inner, 2 * padded, depth))] * OUTER + [low((units, shared_down.shape[1]))] * 2,
+        [place_ids, line_gate.T, shared_up.T, shared_down],
+        scalars=1,
+    )
+    far_pair, *spread = lax.optimization_barrier((far_pair, *spread))
+    pieces = [line, own_pair, far_pair]
+    pieces = pieces + [swap(piece, "expert", 1) for piece in pieces]
+    kept_sums, sent_sums, router_blocks, routes_plane = call(
         project_kernel,
-        [low((peers, pre_rows, D + LANES))] + [low((members, TILE, LANES))] * 2,
+        [low((OUTER, pre_rows, D + LANES))] * 2 + [low((members, TILE, LANES))] * 2,
         [place_ids, att_got, *pieces],
         scratch=[
             pltpu.VMEM((peers * pre_rows + TILE, heads_block), jnp.bfloat16),
@@ -857,13 +873,11 @@
         flops=300_000_000,
         moved=tuple(range(2, 2 + len(pieces))),
     )
+    other_sums = swap(sent_sums, "dp", 1)
     routes_other = swap(routes_plane, "dp", 1)
 
-    shared_got = [spread[0]] + [swap(spread[i], "expert", i * inner) for i in range(1, OUTER)]
-    _, *shared_got = lax.optimization_barrier((partial_blocks, *shared_got))
-    kept = jnp.concatenate([block[:pair_bit] for block in shared_got], axis=0)
-    sent = jnp.concatenate([block[pair_bit:] for block in shared_got], axis=0)
-    far = swap(sent, "expert", pair_bit)
+    _, *spread = lax.optimization_barrier((kept_sums, *spread))
+    shared_got = line_swaps(spread, inner)
     pre_total = homes * pre_rows
     total = pre_total + homes
     slots = homes * capacity
@@ -874,7 +888,19 @@
         scalars=1,
         vmem=16,
     )
-    far, select = lax.optimization_barrier((far, select))
+    resid = jnp.concatenate([pre_resid, fold_row(dec_resid)], axis=1)
+    gain = jnp.concatenate(
+        [jnp.broadcast_to(norm_gain[None], (TILE, D)), norm_gain.reshape(TILE, LANES)], axis=1
+    )
+    other_sums, select, scatter, chosen = lax.optimization_barrier(
+        (other_sums, select, scatter, chosen)
+    )
+    sums = call(pair_kernel, [low(resid.shape)] * OUTER, [kept_sums, other_sums], flops=1_000_000)
+    sums_got = line_swaps(sums, inner)
+    _, *shared_got = lax.optimization_barrier((sums[0], *shared_got))
+    kept = jnp.concatenate([block[:pair_bit] for block in shared_got], axis=0)
+    sent = jnp.concatenate([block[pair_bit:] for block in shared_got], axis=0)
+    far = swap(sent, "expert", pair_bit)
     shared_kept = jnp.concatenate([kept[::pair_bit], far[::pair_bit]], axis=0)
     shared_sent = jnp.concatenate([kept[1::pair_bit], far[1::pair_bit]], axis=0)
     shared_far = swap(shared_sent, "expert", 1)
@@ -885,22 +911,12 @@
         scratch=[pltpu.VMEM((members * TILE, LANES), jnp.float32)],
         scalars=1,
     )
-    partial_got = lax.all_to_all(
-        partial_blocks, both, split_axis=0, concat_axis=0, axis_index_groups=lines, tiled=True
-    )
     middle = OUTER // 2
-    partial_got, select, scatter, chosen, small = lax.optimization_barrier(
-        (partial_got, select, scatter, chosen, small)
-    )
-    resid = jnp.concatenate([pre_resid, fold_row(dec_resid)], axis=1)
-    gain = jnp.concatenate(
-        [jnp.broadcast_to(norm_gain[None], (TILE, D)), norm_gain.reshape(TILE, LANES)], axis=1
-    )
     hidden, normed = call(
-        norm_kernel, [low(resid.shape)] * 2, [partial_got, resid, gain], flops=20_000_000_000
-    )
-
-    line = [normed] + [swap(normed, "expert", step * inner) for step in range(1, OUTER)]
+        norm_kernel, [low(resid.shape)] * 2, [resid, gain, *sums_got], flops=20_000_000_000
+    )
+
+    line = line_swaps([normed] * OUTER, inner)
     middle = OUTER // 2
     row_pieces = []
     for part in (line[:middle], line[middle:]):
@@ -913,34 +929,25 @@
     row_pieces = row_pieces + [swap(piece, "expert", 1) for piece in row_pieces]
 
     width = gate_weight.shape[2]
-    first_width = -(-width // (2 * LANES)) * LANES
     gate_rows, up_rows = gate_weight.swapaxes(1, 2), up_weight.swapaxes(1, 2)
-    act_a, shared_act, expert_rows, slot_weight = call(
-        partial(expert_kernel, units),
-        [
-            low((slots, first_width)), low((total // 2, LANES)), low((slots, D)),
-            jax.ShapeDtypeStruct((slots, LANES), jnp.float32),
-        ],
-        [small, select, chosen, gate_rows, up_rows, *row_pieces],
-        scratch=[
-            pltpu.VMEM((pre_total, LANES), jnp.float32),
-            pltpu.VMEM((pre_total, D), jnp.bfloat16),
-            pltpu.VMEM((homes, D), jnp.bfloat16),
-        ],
+    expert_act, pre_tokens, dec_tokens = call(
+        expert_kernel,
+        [low((slots, width)), low((pre_total, D)), low((homes, D))],
+        [select, gate_rows, up_rows, *row_pieces],
+        scratch=[pltpu.VMEM((pre_total, LANES), jnp.float32)],
         flops=2_000_000_000,
         vmem=20,
     )
-    act_a_other = swap(act_a, "dp", 1)
-    act_b = call(
-        partial(hidden_kernel, first_width),
-        low((slots, width - first_width)),
-        [expert_rows, slot_weight, gate_rows, up_rows],
-        flops=1_000_000_000,
+    expert_act_other = swap(expert_act, "dp", 1)
+    shared_act, slot_weight = call(
+        partial(shared_kernel, units, members),
+        [low((total // 2, LANES)), jax.ShapeDtypeStruct((slots, LANES), jnp.float32)],
+        [small, select, chosen, pre_tokens, dec_tokens],
+        flops=500_000_000,
         vmem=12,
     )
-    act_b_other = swap(act_b, "dp", 1)
     shared_act_other = swap(shared_act, "dp", 1)
-    act_a, down_a, down_b = lax.optimization_barrier((act_a, down_a, down_b))
+    shared_act, down_a, down_b = lax.optimization_barrier((shared_act, down_a, down_b))
     half = members // 2
     down_a = lax.ppermute(
         down_a,
@@ -957,8 +964,8 @@
         down_kernel,
         [low((homes // 2, TILE, col_width + LANES))] * 2,
         [
-            place_ids, act_a, act_b, act_a_other, act_b_other, shared_act, shared_act_other,
-            down_weight, down_a, down_b, scatter,
+            place_ids, expert_act, expert_act_other, shared_act, shared_act_other,
+            down_weight, down_a, down_b, scatter, slot_weight,
         ],
         scratch=[pltpu.VMEM((pre_total, LANES), jnp.float32)],
         scalars=1,

time: 127 us -> 122 us (0.961)
  Pallas kernels: 23.5 us -> 17.5 us
  local copies, waits for them, and re-layouts: 0.16 us -> 3.35 us
    pallas_call x11 -> x12, Pallas kernels: 23.5 us -> 17.5 us  [call(): pl.pallas_call(body, out_shape=out_shapes, in_specs=specs, out_specs=pl.B...]
    all_to_all x1 -> x0, starting transfers between devices: 5.42 us -> none  [token_shards(): lax.all_to_all(partial_blocks, both, split_axis=0, concat_axis=0, axis_in...]
    all_to_all x1 -> x0, waiting for transfers between devices: 4.81 us -> none  [token_shards(): lax.all_to_all(partial_blocks, both, split_axis=0, concat_axis=0, axis_in...]
    ppermute x35 -> x38, starting transfers between devices: 30.3 us -> 34.9 us  [swap(): return lax.ppermute(value, axis, [(i, i ^ bit) for i in range(size)])]
    unnamed x24 -> x40, local copies, waits for them, and re-layouts: 0.07 us -> 3.26 us
    ppermute x35 -> x38, waiting for transfers between devices: 27.6 us -> 30.8 us  [swap(): return lax.ppermute(value, axis, [(i, i ^ bit) for i in range(size)])]
  transfers between devices with their start and end apart: 39 -> 41, of which waited for: 13 -> 16; matrix products, arithmetic and copies ran while one was open for 0% -> 0% of each run, Pallas kernels for 10% -> 9%
where the time goes in v4:
time: 122 us; the launch traced here: 121 us
  starting transfers between devices  43.3 us (35%)
  waiting for transfers between devices  31.7 us (26%)
  blocking collectives  23.4 us (19%)
  Pallas kernels  17.5 us (14%)
  local copies, waits for them, and re-layouts  3.35 us (3%)
  between operations  1.76 us (1%)
    ppermute x38, starting transfers between devices, swap(): return lax.ppermute(value, axis, [(i, i ^ bit) for i in range(size)])  34.9 us
    ppermute x38, waiting for transfers between devices, swap(): return lax.ppermute(value, axis, [(i, i ^ bit) for i in range(size)])  30.8 us
    all_to_all x1, blocking collectives, token_shards(): lax.all_to_all(pair_sum, both, split_axis=0, concat_axis=0, axis_index_gr...  23.4 us
    pallas_call x12, Pallas kernels, call(): pl.pallas_call(body, out_shape=out_shapes, in_specs=specs, out_specs=pl.B...  17.5 us
    all_to_all x1, starting transfers between devices, token_shards(): lax.all_to_all(att_blocks, both, split_axis=0, concat_axis=0, axis_index_...  5.96 us
    unnamed x40, local copies, waits for them, and re-layouts  3.26 us
  transfers between devices with their start and end apart: 41, of which 16 were waited for; matrix products, arithmetic and copies ran while one was open for 0% of the time, Pallas kernels for 9%

profile of v4, /device:TPU:0, one launch (start us, length us, event | category | flops | bytes accessed | tf_op | source)
XLA Modules:
  0.0 121.4 jit_solution(15561813342136622123)
XLA Ops:
  4.7 3.1 %collective-permute-start = (bf16[1,16,2816]{2,1,0:T(8,128)(2,1)S(1)}, bf16[1,16,2816]{2,1,0:T(8,128)(2,1)S(1)}, u32[]{:S(2)}, u32[]{:S(2)}) collective-permute-start(bf16[1,16,2816]{2,1,0:T(8,128)(2,1)S(1)} %get-tuple-element.58), channel_id=1, source_target_pairs={{0,4},{1,5},{2,6},{3,7},{4,0},{5,1},{6,2},{7,3},{8,12},{9,13},{10,... | collective-permute-start | bytes 270344 | tf_op jit(solution)/shard_map/ppermute | solution.py:222
  7.8 2.6 %collective-permute-start.1 = (bf16[1,16,2816]{2,1,0:T(8,128)(2,1)S(1)}, bf16[1,16,2816]{2,1,0:T(8,128)(2,1)S(1)}, u32[]{:S(2)}, u32[]{:S(2)}) collective-permute-start(bf16[1,16,2816]{2,1,0:T(8,128)(2,1)S(1)} %get-tuple-element.59), channel_id=1, source_target_pairs={{0,8},{1,9},{2,10},{3,11},{4,12},{5,13},{6,14},{7,15},{8,0},{9,1},... | collective-permute-start | bytes 270344 | tf_op jit(solution)/shard_map/ppermute | solution.py:222
  12.8 1.9 %shard_map.204 = bf16[8,16,1152]{2,1,0:T(8,128)(2,1)} custom-call(s32[1]{0:T(128)S(6)} %copy.24.length_ref, bf16[16,16,576]{2,1,0:T(8,128)(2,1)S(1)} %copy-done.4, bf16[16,576]{1,0:T(8,128)(2,1)S(1)} %copy-done.8, bf16[1,16,576]{2,1,0:T(8,128)(2,1)S(1)} %copy-done.9, bf16[1,576]{1,0:T(2,128)(2,1)S(1)} %copy-done.10, bf16[1,576,1024]{2,1,0:T(8,128)(2,1)S(1)} %bitcast.14, ...), custom_call_target="tpu_custom_call" | custom-call | flops 100000000 | bytes 1512644 | tf_op jit(solution)/shard_map/pallas_call | solution.py:271
  14.7 6.0 %all-to-all-start = ((bf16[8,16,1152]{2,1,0:T(8,128)(2,1)}), bf16[8,16,1152]{2,1,0:T(8,128)(2,1)S(1)}, u32[]{:S(2)}, u32[]{:S(2)}) async-start(bf16[8,16,1152]{2,1,0:T(8,128)(2,1)} %shard_map.204), calls=%async_computation | async-start | bytes 589824 | tf_op jit(solution)/shard_map/all_to_all | solution.py:847
  22.6 5.0 %collective-permute-done.4.refs_4_ = bf16[3,16,2816]{2,1,0:T(8,128)(2,1)S(1)} collective-permute-done((bf16[3,16,2816]{2,1,0:T(8,128)(2,1)S(1)}, bf16[3,16,2816]{2,1,0:T(8,128)(2,1)S(1)}, u32[]{:S(2)}, u32[]{:S(2)}) %collective-permute-start.4) | collective-permute-done | bytes 270368 | tf_op jit(solution)/shard_map/ppermute | solution.py:222
  30.2 2.4 %shard_map.206 = (bf16[4,16,2176]{2,1,0:T(8,128)(2,1)S(1)}, bf16[4,16,2176]{2,1,0:T(8,128)(2,1)S(1)}, bf16[16,16,128]{2,1,0:T(8,128)(2,1)S(1)}, bf16[16,16,128]{2,1,0:T(8,128)(2,1)S(1)}) custom-call(s32[3]{0:T(128)S(1)} %pad_add_fusion.refs_0_.place_ref, bf16[8,16,1152]{2,1,0:T(8,128)(2,1)S(1)} %all-to-all-done.refs_1_, ...), custom_call_target="tpu_custom_call" | custom-call | flops 300000000 | bytes 1736716 | tf_op jit(solution)/shard_map/pallas_call | solution.py:271
  35.0 2.4 %collective-permute-start.32 = (bf16[4,96,128]{2,1,0:T(8,128)(2,1)S(1)}, bf16[4,96,128]{2,1,0:T(8,128)(2,1)S(1)}, u32[]{:S(2)}, u32[]{:S(2)}) collective-permute-start(bf16[4,96,128]{2,1,0:T(8,128)(2,1)S(1)} %get-tuple-element.91), channel_id=1, source_target_pairs={{0,8},{1,9},{2,10},{3,11},{4,12},{5,13},{6,14},{7,15},{8,0},{9,1},... | collective-permute-start | bytes 294920 | tf_op jit(solution)/shard_map/ppermute | solution.py:222
  39.1 2.8 %shard_map.207 = (bf16[224,544]{1,0:T(8,128)(2,1)S(1)}, bf16[544,224]{1,0:T(8,128)(2,1)S(1)}, bf16[544,128]{1,0:T(8,128)(2,1)S(1)}) custom-call(s32[3]{0:T(128)S(1)} %pad_add_fusion.refs_0_.place_ref, bf16[16,16,128]{2,1,0:T(8,128)(2,1)S(1)} %get-tuple-element.72.plane_ref, bf16[16,16,128]{2,1,0:T(8,128)(2,1)S(1)} %collective-permute-done.9.other_ref), custom_call_target="tpu_custom_call" | custom-call | bytes 131084 | tf_op jit(solution)/shard_map/pallas_call | solution.py:271
  41.9 3.6 %collective-permute-done.8.other_ref = bf16[4,16,2176]{2,1,0:T(8,128)(2,1)S(1)} collective-permute-done((bf16[4,16,2176]{2,1,0:T(8,128)(2,1)S(1)}, bf16[4,16,2176]{2,1,0:T(8,128)(2,1)S(1)}, u32[]{:S(2)}, u32[]{:S(2)}) %collective-permute-start.8) | collective-permute-done | bytes 278560 | tf_op jit(solution)/shard_map/ppermute | solution.py:222
  47.1 2.4 %collective-permute-start.11 = (bf16[16,2176]{1,0:T(8,128)(2,1)S(1)}, bf16[16,2176]{1,0:T(8,128)(2,1)S(1)}, u32[]{:S(2)}, u32[]{:S(2)}) collective-permute-start(bf16[16,2176]{1,0:T(8,128)(2,1)S(1)} %get-tuple-element.81), channel_id=1, source_target_pairs={{0,8},{1,9},{2,10},{3,11},{4,12},{5,13},{6,14},{7,15},{8,0},{9,1},... | collective-permute-start | bytes 208904 | tf_op jit(solution)/shard_map/ppermute | solution.py:222
  50.8 3.0 %collective-permute-done.11.rest_2_ = bf16[16,2176]{1,0:T(8,128)(2,1)S(1)} collective-permute-done((bf16[16,2176]{1,0:T(8,128)(2,1)S(1)}, bf16[16,2176]{1,0:T(8,128)(2,1)S(1)}, u32[]{:S(2)}, u32[]{:S(2)}) %collective-permute-start.11) | collective-permute-done | bytes 69664 | tf_op jit(solution)/shard_map/ppermute | solution.py:222
  53.8 1.8 %collective-permute-done.12.rest_3_ = bf16[16,2176]{1,0:T(8,128)(2,1)S(1)} collective-permute-done((bf16[16,2176]{1,0:T(8,128)(2,1)S(1)}, bf16[16,2176]{1,0:T(8,128)(2,1)S(1)}, u32[]{:S(2)}, u32[]{:S(2)}) %collective-permute-start.12) | collective-permute-done | bytes 69664 | tf_op jit(solution)/shard_map/ppermute | solution.py:222
  57.2 3.0 %collective-permute-start.13 = (bf16[16,2176]{1,0:T(8,128)(2,1)S(1)}, bf16[16,2176]{1,0:T(8,128)(2,1)S(1)}, u32[]{:S(2)}, u32[]{:S(2)}) collective-permute-start(bf16[16,2176]{1,0:T(8,128)(2,1)S(1)} %get-tuple-element.83), channel_id=1, source_target_pairs={{0,4},{1,5},{2,6},{3,7},{4,0},{5,1},{6,2},{7,3},{8,12},{9,13},{10,... | collective-permute-start | bytes 208904 | tf_op jit(solution)/shard_map/ppermute | solution.py:222
  60.3 2.6 %collective-permute-done.13 = bf16[16,2176]{1,0:T(8,128)(2,1)S(1)} collective-permute-done((bf16[16,2176]{1,0:T(8,128)(2,1)S(1)}, bf16[16,2176]{1,0:T(8,128)(2,1)S(1)}, u32[]{:S(2)}, u32[]{:S(2)}) %collective-permute-start.13) | collective-permute-done | bytes 69664 | tf_op jit(solution)/shard_map/ppermute | solution.py:222
  67.3 2.1 %collective-permute-done.18.rest_4_ = bf16[32,2176]{1,0:T(8,128)(2,1)S(1)} collective-permute-done((bf16[32,2176]{1,0:T(8,128)(2,1)S(1)}, bf16[32,2176]{1,0:T(8,128)(2,1)S(1)}, u32[]{:S(2)}, u32[]{:S(2)}) %collective-permute-start.18) | collective-permute-done | bytes 139296 | tf_op jit(solution)/shard_map/ppermute | solution.py:222
  69.7 1.9 %collective-permute-start.20 = (bf16[32,2176]{1,0:T(8,128)(2,1)S(1)}, bf16[32,2176]{1,0:T(8,128)(2,1)S(1)}, u32[]{:S(2)}, u32[]{:S(2)}) collective-permute-start(bf16[32,2176]{1,0:T(8,128)(2,1)S(1)} %collective-permute-done.16.rest_2_), channel_id=1, source_target_pairs={{0,16},{16,0},{1,17},{17,1},{2,18},{18,2},{3,19},{19,3},{4,20},{20... | collective-permute-start | bytes 417800 | tf_op jit(solution)/shard_map/ppermute | solution.py:222
  73.2 2.3 %collective-permute-done.20.rest_6_ = bf16[32,2176]{1,0:T(8,128)(2,1)S(1)} collective-permute-done((bf16[32,2176]{1,0:T(8,128)(2,1)S(1)}, bf16[32,2176]{1,0:T(8,128)(2,1)S(1)}, u32[]{:S(2)}, u32[]{:S(2)}) %collective-permute-start.20) | collective-permute-done | bytes 139296 | tf_op jit(solution)/shard_map/ppermute | solution.py:222
  78.6 2.6 %shard_map.210 = (bf16[224,704]{1,0:T(8,128)(2,1)S(1)}, bf16[512,2048]{1,0:T(8,128)(2,1)S(1)}, bf16[32,2048]{1,0:T(8,128)(2,1)S(1)}) custom-call(bf16[224,544]{1,0:T(8,128)(2,1)S(1)} %get-tuple-element.76.select_ref, bf16[1,704,2048]{2,1,0:T(8,128)(2,1)S(1)} %bitcast.12, bf16[1,704,2048]{2,1,0:T(8,128)(2,1)S(1)} %bitcast.13, ...), custom_call_target="tpu_custom_call" | custom-call | flops 2000000000 | bytes 8239104 | tf_op jit(solution)/shard_map/pallas_call | solution.py:271
  82.6 2.1 %shard_map.212 = (bf16[272,128]{1,0:T(8,128)(2,1)S(1)}, f32[224,128]{1,0:T(8,128)S(1)}) custom-call(bf16[128,2048]{1,0:T(8,128)(2,1)S(1)} %shard_map.211.small_ref, bf16[224,544]{1,0:T(8,128)(2,1)S(1)} %get-tuple-element.76.select_ref, bf16[544,128]{1,0:T(8,128)(2,1)S(1)} %get-tuple-element.98.chosen_ref, bf16[512,2048]{1,0:T(8,128)(2,1)S(1)} %get-tuple-element.99.pre_ref, ...), custom_call_target="tpu_custom_call" | custom-call | flops 500000000 | bytes 3135488 | tf_op jit(solution)/shard_map/pallas_call | solution.py:271
  85.4 1.8 %collective-permute-start.38 = (bf16[44,1024]{1,0:T(8,128)(2,1)S(1)}, bf16[44,1024]{1,0:T(8,128)(2,1)S(1)}, u32[]{:S(2)}, u32[]{:S(2)}) collective-permute-start(bf16[44,1024]{1,0:T(8,128)(2,1)S(1)} %get-tuple-element.106), channel_id=1, source_target_pairs={{0,1},{1,3},{2,5},{3,7},{4,9},{5,11},{6,13},{7,15},{8,0},{9,2},{10... | collective-permute-start | bytes 270344 | tf_op jit(solution)/shard_map/ppermute | solution.py:957
  88.8 4.0 %collective-permute-done.36.shared_other_ref = bf16[272,128]{1,0:T(8,128)(2,1)S(1)} collective-permute-done((bf16[272,128]{1,0:T(8,128)(2,1)S(1)}, bf16[272,128]{1,0:T(8,128)(2,1)S(1)}, u32[]{:S(2)}, u32[]{:S(2)}) %collective-permute-start.36) | collective-permute-done | bytes 69664 | tf_op jit(solution)/shard_map/ppermute | solution.py:222
  92.9 2.1 %shard_map.213 = (bf16[16,16,1152]{2,1,0:T(8,128)(2,1)S(1)}, bf16[16,16,1152]{2,1,0:T(8,128)(2,1)S(1)}) custom-call(s32[3]{0:T(128)S(1)} %pad_add_fusion.refs_0_.place_ref, bf16[224,704]{1,0:T(8,128)(2,1)S(1)} %get-tuple-element.84.act_ref, bf16[224,704]{1,0:T(8,128)(2,1)S(1)} %collective-permute-done.30.act_other_ref, ...), custom_call_target="tpu_custom_call" | custom-call | flops 1000000000 | bytes 4192268 | tf_op jit(solution)/shard_map/pallas_call | solution.py:271
  95.1 2.0 %collective-permute-done.39 = bf16[16,16,1152]{2,1,0:T(8,128)(2,1)S(1)} collective-permute-done((bf16[16,16,1152]{2,1,0:T(8,128)(2,1)S(1)}, bf16[16,16,1152]{2,1,0:T(8,128)(2,1)S(1)}, u32[]{:S(2)}, u32[]{:S(2)}) %collective-permute-start.39) | collective-permute-done | bytes 589856 | tf_op jit(solution)/shard_map/ppermute | solution.py:222
  97.3 23.4 %all_to_all.10.got_ref = bf16[16,16,1152]{2,1,0:T(8,128)(2,1)S(1)} all-to-all(bf16[16,16,1152]{2,1,0:T(8,128)(2,1)S(1)} %add_convert_fusion), channel_id=1, replica_groups={{0,2,4,6,8,10,12,14,16,18,20,22,24,26,28,30},{1,3,5,7,9,11,13,15,17,19,..., dimensions={0} | all-to-all | bytes 1179648 | tf_op jit(solution)/shard_map/all_to_all | solution.py:982
  (128 shorter events, 32.6 us)
Async XLA Ops:
  4.7 16.0 %collective-permute-start = (bf16[1,16,2816]{2,1,0:T(8,128)(2,1)S(1)}, bf16[1,16,2816]{2,1,0:T(8,128)(2,1)S(1)}, u32[]{:S(2)}, u32[]{:S(2)}) collective-permute-start(bf16[1,16,2816]{2,1,0:T(8,128)(2,1)S(1)} %get-tuple-element.58), channel_id=1, source_target_pairs={{0,4},{1,5},{2,6},{3,7},{4,0},{5,1},{6,2},{7,3},{8,12},{9,13},{10,... | collective-permute-start | bytes 270344 | tf_op jit(solution)/shard_map/ppermute | solution.py:222
  7.8 12.9 %collective-permute-start.1 = (bf16[1,16,2816]{2,1,0:T(8,128)(2,1)S(1)}, bf16[1,16,2816]{2,1,0:T(8,128)(2,1)S(1)}, u32[]{:S(2)}, u32[]{:S(2)}) collective-permute-start(bf16[1,16,2816]{2,1,0:T(8,128)(2,1)S(1)} %get-tuple-element.59), channel_id=1, source_target_pairs={{0,8},{1,9},{2,10},{3,11},{4,12},{5,13},{6,14},{7,15},{8,0},{9,1},... | collective-permute-start | bytes 270344 | tf_op jit(solution)/shard_map/ppermute | solution.py:222
  10.4 10.3 %collective-permute-start.2 = (bf16[1,16,2816]{2,1,0:T(8,128)(2,1)S(1)}, bf16[1,16,2816]{2,1,0:T(8,128)(2,1)S(1)}, u32[]{:S(2)}, u32[]{:S(2)}) collective-permute-start(bf16[1,16,2816]{2,1,0:T(8,128)(2,1)S(1)} %get-tuple-element.60), channel_id=1, source_target_pairs={{0,12},{1,13},{2,14},{3,15},{4,8},{5,9},{6,10},{7,11},{8,4},{9,5},... | collective-permute-start | bytes 270344 | tf_op jit(solution)/shard_map/ppermute | solution.py:222
  10.4 10.4 %collective-permute-start.3 = (bf16[1,16,2816]{2,1,0:T(8,128)(2,1)S(1)}, bf16[1,16,2816]{2,1,0:T(8,128)(2,1)S(1)}, u32[]{:S(2)}, u32[]{:S(2)}) collective-permute-start(bf16[1,16,2816]{2,1,0:T(8,128)(2,1)S(1)} %get-tuple-element.57), channel_id=1, source_target_pairs={{0,2},{1,3},{2,0},{3,1},{4,6},{5,7},{6,4},{7,5},{8,10},{9,11},{10,... | collective-permute-start | bytes 270344 | tf_op jit(solution)/shard_map/ppermute | solution.py:222
  14.7 15.4 %all-to-all-start = ((bf16[8,16,1152]{2,1,0:T(8,128)(2,1)}), bf16[8,16,1152]{2,1,0:T(8,128)(2,1)S(1)}, u32[]{:S(2)}, u32[]{:S(2)}) async-start(bf16[8,16,1152]{2,1,0:T(8,128)(2,1)} %shard_map.204), calls=%async_computation | async-start | bytes 589824 | tf_op jit(solution)/shard_map/all_to_all | solution.py:847
  20.8 6.9 %collective-permute-start.4 = (bf16[3,16,2816]{2,1,0:T(8,128)(2,1)S(1)}, bf16[3,16,2816]{2,1,0:T(8,128)(2,1)S(1)}, u32[]{:S(2)}, u32[]{:S(2)}) collective-permute-start(bf16[3,16,2816]{2,1,0:T(8,128)(2,1)S(1)} %pad_maximum_fusion.1), channel_id=1, source_target_pairs={{0,2},{1,3},{2,0},{3,1},{4,6},{5,7},{6,4},{7,5},{8,10},{9,11},{10,... | collective-permute-start | bytes 811016 | tf_op jit(solution)/shard_map/ppermute | solution.py:222
  21.4 7.9 %collective-permute-start.5 = (bf16[4,16,2816]{2,1,0:T(8,128)(2,1)S(1)}, bf16[4,16,2816]{2,1,0:T(8,128)(2,1)S(1)}, u32[]{:S(2)}, u32[]{:S(2)}) collective-permute-start(bf16[4,16,2816]{2,1,0:T(8,128)(2,1)S(1)} %pad_maximum_fusion.refs_2_), channel_id=1, source_target_pairs={{0,1},{1,0},{2,3},{3,2},{4,5},{5,4},{6,7},{7,6},{8,9},{9,8},{10,11... | collective-permute-start | bytes 1081352 | tf_op jit(solution)/shard_map/ppermute | solution.py:222
  32.6 6.5 %collective-permute-start.9 = (bf16[16,16,128]{2,1,0:T(8,128)(2,1)S(1)}, bf16[16,16,128]{2,1,0:T(8,128)(2,1)S(1)}, u32[]{:S(2)}, u32[]{:S(2)}) collective-permute-start(bf16[16,16,128]{2,1,0:T(8,128)(2,1)S(1)} %get-tuple-element.72.plane_ref), channel_id=1, source_target_pairs={{0,16},{16,0},{1,17},{17,1},{2,18},{18,2},{3,19},{19,3},{4,20},{20... | collective-permute-start | bytes 196616 | tf_op jit(solution)/shard_map/ppermute | solution.py:222
  33.6 12.0 %collective-permute-start.31 = (bf16[4,96,128]{2,1,0:T(8,128)(2,1)S(1)}, bf16[4,96,128]{2,1,0:T(8,128)(2,1)S(1)}, u32[]{:S(2)}, u32[]{:S(2)}) collective-permute-start(bf16[4,96,128]{2,1,0:T(8,128)(2,1)S(1)} %get-tuple-element.90), channel_id=1, source_target_pairs={{0,4},{1,5},{2,6},{3,7},{4,0},{5,1},{6,2},{7,3},{8,12},{9,13},{10,... | collective-permute-start | bytes 294920 | tf_op jit(solution)/shard_map/ppermute | solution.py:222
  35.0 10.6 %collective-permute-start.32 = (bf16[4,96,128]{2,1,0:T(8,128)(2,1)S(1)}, bf16[4,96,128]{2,1,0:T(8,128)(2,1)S(1)}, u32[]{:S(2)}, u32[]{:S(2)}) collective-permute-start(bf16[4,96,128]{2,1,0:T(8,128)(2,1)S(1)} %get-tuple-element.91), channel_id=1, source_target_pairs={{0,8},{1,9},{2,10},{3,11},{4,12},{5,13},{6,14},{7,15},{8,0},{9,1},... | collective-permute-start | bytes 294920 | tf_op jit(solution)/shard_map/ppermute | solution.py:222
  37.4 8.2 %collective-permute-start.33 = (bf16[4,96,128]{2,1,0:T(8,128)(2,1)S(1)}, bf16[4,96,128]{2,1,0:T(8,128)(2,1)S(1)}, u32[]{:S(2)}, u32[]{:S(2)}) collective-permute-start(bf16[4,96,128]{2,1,0:T(8,128)(2,1)S(1)} %get-tuple-element.92), channel_id=1, source_target_pairs={{0,12},{1,13},{2,14},{3,15},{4,8},{5,9},{6,10},{7,11},{8,4},{9,5},... | collective-permute-start | bytes 294920 | tf_op jit(solution)/shard_map/ppermute | solution.py:222
  38.0 7.6 %collective-permute-start.8 = (bf16[4,16,2176]{2,1,0:T(8,128)(2,1)S(1)}, bf16[4,16,2176]{2,1,0:T(8,128)(2,1)S(1)}, u32[]{:S(2)}, u32[]{:S(2)}) collective-permute-start(bf16[4,16,2176]{2,1,0:T(8,128)(2,1)S(1)} %get-tuple-element.71), channel_id=1, source_target_pairs={{0,16},{16,0},{1,17},{17,1},{2,18},{18,2},{3,19},{19,3},{4,20},{20... | collective-permute-start | bytes 835592 | tf_op jit(solution)/shard_map/ppermute | solution.py:222
  47.1 6.7 %collective-permute-start.11 = (bf16[16,2176]{1,0:T(8,128)(2,1)S(1)}, bf16[16,2176]{1,0:T(8,128)(2,1)S(1)}, u32[]{:S(2)}, u32[]{:S(2)}) collective-permute-start(bf16[16,2176]{1,0:T(8,128)(2,1)S(1)} %get-tuple-element.81), channel_id=1, source_target_pairs={{0,8},{1,9},{2,10},{3,11},{4,12},{5,13},{6,14},{7,15},{8,0},{9,1},... | collective-permute-start | bytes 208904 | tf_op jit(solution)/shard_map/ppermute | solution.py:222
  49.5 6.1 %collective-permute-start.12 = (bf16[16,2176]{1,0:T(8,128)(2,1)S(1)}, bf16[16,2176]{1,0:T(8,128)(2,1)S(1)}, u32[]{:S(2)}, u32[]{:S(2)}) collective-permute-start(bf16[16,2176]{1,0:T(8,128)(2,1)S(1)} %get-tuple-element.82), channel_id=1, source_target_pairs={{0,12},{1,13},{2,14},{3,15},{4,8},{5,9},{6,10},{7,11},{8,4},{9,5},... | collective-permute-start | bytes 208904 | tf_op jit(solution)/shard_map/ppermute | solution.py:222
  50.2 15.5 %collective-permute-start.34 = (bf16[8,96,128]{2,1,0:T(8,128)(2,1)S(1)}, bf16[8,96,128]{2,1,0:T(8,128)(2,1)S(1)}, u32[]{:S(2)}, u32[]{:S(2)}) collective-permute-start(bf16[8,96,128]{2,1,0:T(8,128)(2,1)S(1)} %pad_maximum_fusion.3), channel_id=1, source_target_pairs={{0,2},{1,3},{2,0},{3,1},{4,6},{5,7},{6,4},{7,5},{8,10},{9,11},{10,... | collective-permute-start | bytes 589832 | tf_op jit(solution)/shard_map/ppermute | solution.py:222
  55.8 8.3 %collective-permute-start.15 = (bf16[16,2176]{1,0:T(8,128)(2,1)S(1)}, bf16[16,2176]{1,0:T(8,128)(2,1)S(1)}, u32[]{:S(2)}, u32[]{:S(2)}) collective-permute-start(bf16[16,2176]{1,0:T(8,128)(2,1)S(1)} %get-tuple-element.83), channel_id=1, source_target_pairs={{0,12},{1,13},{2,14},{3,15},{4,8},{5,9},{6,10},{7,11},{8,4},{9,5},... | collective-permute-start | bytes 208904 | tf_op jit(solution)/shard_map/ppermute | solution.py:222
  57.2 6.3 %collective-permute-start.14 = (bf16[16,2176]{1,0:T(8,128)(2,1)S(1)}, bf16[16,2176]{1,0:T(8,128)(2,1)S(1)}, u32[]{:S(2)}, u32[]{:S(2)}) collective-permute-start(bf16[16,2176]{1,0:T(8,128)(2,1)S(1)} %get-tuple-element.83), channel_id=1, source_target_pairs={{0,8},{1,9},{2,10},{3,11},{4,12},{5,13},{6,14},{7,15},{8,0},{9,1},... | collective-permute-start | bytes 208904 | tf_op jit(solution)/shard_map/ppermute | solution.py:222
  62.9 6.5 %collective-permute-start.18 = (bf16[32,2176]{1,0:T(8,128)(2,1)S(1)}, bf16[32,2176]{1,0:T(8,128)(2,1)S(1)}, u32[]{:S(2)}, u32[]{:S(2)}) collective-permute-start(bf16[32,2176]{1,0:T(8,128)(2,1)S(1)} %constant_dynamic-update-slice_fusion.rest_0_), channel_id=1, source_target_pairs={{0,16},{16,0},{1,17},{17,1},{2,18},{18,2},{3,19},{19,3},{4,20},{20... | collective-permute-start | bytes 417800 | tf_op jit(solution)/shard_map/ppermute | solution.py:222
  64.1 7.9 %collective-permute-start.19 = (bf16[32,2176]{1,0:T(8,128)(2,1)S(1)}, bf16[32,2176]{1,0:T(8,128)(2,1)S(1)}, u32[]{:S(2)}, u32[]{:S(2)}) collective-permute-start(bf16[32,2176]{1,0:T(8,128)(2,1)S(1)} %constant_dynamic-update-slice_fusion.2.rest_1_), channel_id=1, source_target_pairs={{0,16},{16,0},{1,17},{17,1},{2,18},{18,2},{3,19},{19,3},{4,20},{20... | collective-permute-start | bytes 417800 | tf_op jit(solution)/shard_map/ppermute | solution.py:222
  65.7 6.9 %collective-permute-start.23 = (bf16[32,2176]{1,0:T(8,128)(2,1)S(1)}, bf16[32,2176]{1,0:T(8,128)(2,1)S(1)}, u32[]{:S(2)}, u32[]{:S(2)}) collective-permute-start(bf16[32,2176]{1,0:T(8,128)(2,1)S(1)} %constant_dynamic-update-slice_fusion.2.rest_1_), channel_id=1, source_target_pairs={{0,1},{1,0},{2,3},{3,2},{4,5},{5,4},{6,7},{7,6},{8,9},{9,8},{10,11... | collective-permute-start | bytes 417800 | tf_op jit(solution)/shard_map/ppermute | solution.py:222
  65.8 6.9 %collective-permute-start.17 = (bf16[32,2176]{1,0:T(8,128)(2,1)S(1)}, bf16[32,2176]{1,0:T(8,128)(2,1)S(1)}, u32[]{:S(2)}, u32[]{:S(2)}) collective-permute-start(bf16[32,2176]{1,0:T(8,128)(2,1)S(1)} %constant_dynamic-update-slice_fusion.2.rest_1_), channel_id=1, source_target_pairs={{0,2},{1,3},{2,0},{3,1},{4,6},{5,7},{6,4},{7,5},{8,10},{9,11},{10,... | collective-permute-start | bytes 417800 | tf_op jit(solution)/shard_map/ppermute | solution.py:222
  81.2 11.7 %collective-permute-start.30 = (bf16[224,704]{1,0:T(8,128)(2,1)S(1)}, bf16[224,704]{1,0:T(8,128)(2,1)S(1)}, u32[]{:S(2)}, u32[]{:S(2)}) collective-permute-start(bf16[224,704]{1,0:T(8,128)(2,1)S(1)} %get-tuple-element.84.act_ref), channel_id=1, source_target_pairs={{0,16},{16,0},{1,17},{17,1},{2,18},{18,2},{3,19},{19,3},{4,20},{20... | collective-permute-start | bytes 946184 | tf_op jit(solution)/shard_map/ppermute | solution.py:222
  84.7 8.1 %collective-permute-start.37 = (bf16[44,1024]{1,0:T(8,128)(2,1)S(1)}, bf16[44,1024]{1,0:T(8,128)(2,1)S(1)}, u32[]{:S(2)}, u32[]{:S(2)}) collective-permute-start(bf16[44,1024]{1,0:T(8,128)(2,1)S(1)} %get-tuple-element.105), channel_id=1, source_target_pairs={{0,0},{1,2},{2,4},{3,6},{4,8},{5,10},{6,12},{7,14},{8,1},{9,3},{10... | collective-permute-start | bytes 270344 | tf_op jit(solution)/shard_map/ppermute | solution.py:952
  85.4 7.5 %collective-permute-start.38 = (bf16[44,1024]{1,0:T(8,128)(2,1)S(1)}, bf16[44,1024]{1,0:T(8,128)(2,1)S(1)}, u32[]{:S(2)}, u32[]{:S(2)}) collective-permute-start(bf16[44,1024]{1,0:T(8,128)(2,1)S(1)} %get-tuple-element.106), channel_id=1, source_target_pairs={{0,1},{1,3},{2,5},{3,7},{4,9},{5,11},{6,13},{7,15},{8,0},{9,2},{10... | collective-permute-start | bytes 270344 | tf_op jit(solution)/shard_map/ppermute | solution.py:957
  (36 other events, 288.4 us)

commit v5 on v4

--- a/solution.py
+++ b/solution.py
@@ -446,6 +446,11 @@
     for step, (ref, i) in enumerate(pieces):
         router_ref[step] = ref[i, :, -2 * LANES : -LANES]
         routes_ref[step] = ref[i, :, -LANES:]
+        near, row = step // OUTER, (step // OUTER % 2) * (TILE // 2)
+        at = D + LANES + near // 2 * LANES
+        sent_ref[step % OUTER, row : row + TILE // 2, at : at + LANES] = ref[
+            i, : TILE // 2, -LANES:
+        ]
     me = place_ref[0]
     blocks, span, width = att_ref.shape
     width -= LANES
@@ -501,7 +506,7 @@
 
         def store(ref):
             ref[step, :, :D] = partial_rows[rows].astype(jnp.bfloat16)
-            ref[step, :, D:] = fold_ref[rows].astype(jnp.bfloat16)
+            ref[step, :, D : D + LANES] = fold_ref[rows].astype(jnp.bfloat16)
 
         pl.when(group == block // OUTER)(partial(store, kept_ref))
         pl.when(group != block // OUTER)(partial(store, sent_ref))
@@ -510,7 +515,8 @@
 def pair_kernel(kept_ref, other_ref, *out_refs):
     for step, out_ref in enumerate(out_refs):
         out_ref[...] = (
-            kept_ref[step].astype(jnp.float32) + other_ref[step].astype(jnp.float32)
+            kept_ref[step].astype(jnp.float32)
+            + other_ref[step, :, : D + LANES].astype(jnp.float32)
         ).astype(jnp.bfloat16)
 
 
@@ -565,7 +571,11 @@
     chosen = jnp.zeros((total, LANES), jnp.float32)
     mine = jnp.zeros((total, LANES), jnp.float32)
     for k in range(TOPK):
-        table = jnp.concatenate([plane_ref[:, k, :], other_ref[:, k, :]], axis=0)
+        parts = [plane_ref[:, k, :].astype(jnp.float32)]
+        for near in range(members // OUTER):
+            at = D + LANES + near // 2 * LANES
+            parts.append(other_ref[:, (near % 2) * (TILE // 2) + k, at : at + LANES].astype(jnp.float32))
+        table = jnp.concatenate(parts, axis=0).astype(jnp.bfloat16)
         spread = jnp.dot(pick, table, preferred_element_type=jnp.float32)
         expert = jnp.sum(jnp.where(own_row, spread, 0.0), axis=1, keepdims=True)
         chosen = chosen + jnp.where(expert == lane_expert, 1.0, 0.0)
@@ -641,8 +651,10 @@
 
 
 def shared_kernel(
-    units, members, small_ref, select_ref, chosen_ref, pre_ref, dec_ref, shared_ref, weight_ref
+    units, members, place_ref, kept_ref, far_ref, router_ref, select_ref, chosen_ref, pre_ref,
+    dec_ref, shared_ref, weight_ref, small_ref, fold_ref,
 ):
+    small_kernel(place_ref, kept_ref, far_ref, router_ref, small_ref, fold_ref)
     pre_total = pre_ref.shape[0]
     homes = pre_total // TILE
     small = small_ref[...]
@@ -862,7 +874,11 @@
     pieces = pieces + [swap(piece, "expert", 1) for piece in pieces]
     kept_sums, sent_sums, router_blocks, routes_plane = call(
         project_kernel,
-        [low((OUTER, pre_rows, D + LANES))] * 2 + [low((members, TILE, LANES))] * 2,
+        [
+            low((OUTER, pre_rows, D + LANES)),
+            low((OUTER, pre_rows, D + LANES * (1 + members // (2 * OUTER)))),
+        ]
+        + [low((members, TILE, LANES))] * 2,
         [place_ids, att_got, *pieces],
         scratch=[
             pltpu.VMEM((peers * pre_rows + TILE, heads_block), jnp.bfloat16),
@@ -874,29 +890,28 @@
         moved=tuple(range(2, 2 + len(pieces))),
     )
     other_sums = swap(sent_sums, "dp", 1)
-    routes_other = swap(routes_plane, "dp", 1)
-
-    _, *spread = lax.optimization_barrier((kept_sums, *spread))
+
     shared_got = line_swaps(spread, inner)
     pre_total = homes * pre_rows
     total = pre_total + homes
     slots = homes * capacity
+    resid = jnp.concatenate([pre_resid, fold_row(dec_resid)], axis=1)
+    gain = jnp.concatenate(
+        [jnp.broadcast_to(norm_gain[None], (TILE, D)), norm_gain.reshape(TILE, LANES)], axis=1
+    )
+    sums = call(pair_kernel, [low(resid.shape)] * OUTER, [kept_sums, other_sums], flops=1_000_000)
+    sums_got = line_swaps(sums, inner)
+    _, other_routes = lax.optimization_barrier((sums[0], other_sums))
     select, scatter, chosen = call(
         route_kernel,
         [low((slots, total)), low((total, slots)), low((total, LANES))],
-        [place_ids, routes_plane, routes_other],
+        [place_ids, routes_plane, other_routes],
         scalars=1,
         vmem=16,
     )
-    resid = jnp.concatenate([pre_resid, fold_row(dec_resid)], axis=1)
-    gain = jnp.concatenate(
-        [jnp.broadcast_to(norm_gain[None], (TILE, D)), norm_gain.reshape(TILE, LANES)], axis=1
-    )
-    other_sums, select, scatter, chosen = lax.optimization_barrier(
-        (other_sums, select, scatter, chosen)
-    )
-    sums = call(pair_kernel, [low(resid.shape)] * OUTER, [kept_sums, other_sums], flops=1_000_000)
-    sums_got = line_swaps(sums, inner)
+    select, scatter, chosen, *sums_got = lax.optimization_barrier(
+        (select, scatter, chosen, *sums_got)
+    )
     _, *shared_got = lax.optimization_barrier((sums[0], *shared_got))
     kept = jnp.concatenate([block[:pair_bit] for block in shared_got], axis=0)
     sent = jnp.concatenate([block[pair_bit:] for block in shared_got], axis=0)
@@ -904,13 +919,6 @@
     shared_kept = jnp.concatenate([kept[::pair_bit], far[::pair_bit]], axis=0)
     shared_sent = jnp.concatenate([kept[1::pair_bit], far[1::pair_bit]], axis=0)
     shared_far = swap(shared_sent, "expert", 1)
-    small = call(
-        small_kernel,
-        low((LANES, D)),
-        [place_ids, shared_kept, shared_far, router_blocks],
-        scratch=[pltpu.VMEM((members * TILE, LANES), jnp.float32)],
-        scalars=1,
-    )
     middle = OUTER // 2
     hidden, normed = call(
         norm_kernel, [low(resid.shape)] * 2, [resid, gain, *sums_got], flops=20_000_000_000
@@ -942,7 +950,15 @@
     shared_act, slot_weight = call(
         partial(shared_kernel, units, members),
         [low((total // 2, LANES)), jax.ShapeDtypeStruct((slots, LANES), jnp.float32)],
-        [small, select, chosen, pre_tokens, dec_tokens],
+        [
+            place_ids, shared_kept, shared_far, router_blocks, select, chosen, pre_tokens,
+            dec_tokens,
+        ],
+        scratch=[
+            pltpu.VMEM((LANES, D), jnp.bfloat16),
+            pltpu.VMEM((members * TILE, LANES), jnp.float32),
+        ],
+        scalars=1,
         flops=500_000_000,
         vmem=12,
     )

time: 122 us -> 120 us (0.984)
  starting transfers between devices: 43.3 us -> 41.2 us
  waiting for transfers between devices: 31.7 us -> 33.3 us
    ppermute x38 -> x37, starting transfers between devices: 34.9 us -> 32.6 us  [swap(): return lax.ppermute(value, axis, [(i, i ^ bit) for i in range(size)])]
    ppermute x38 -> x37, waiting for transfers between devices: 30.8 us -> 32 us  [swap(): return lax.ppermute(value, axis, [(i, i ^ bit) for i in range(size)])]
    pallas_call x12 -> x11, Pallas kernels: 17.5 us -> 17.5 us  [call(): pl.pallas_call(body, out_shape=out_shapes, in_specs=specs, out_specs=pl.B...]
  transfers between devices with their start and end apart: 41 -> 40, of which waited for: 16 -> 14; matrix products, arithmetic and copies ran while one was open for 0% -> 0% of each run, Pallas kernels for 9% -> 12%
where the time goes in v5:
time: 120 us
  starting transfers between devices  41.2 us (34%)
  waiting for transfers between devices  33.3 us (28%)
  blocking collectives  22.4 us (19%)
  Pallas kernels  17.5 us (15%)
  local copies, waits for them, and re-layouts  3.35 us (3%)
  between operations  1.76 us (1%)
    ppermute x37, starting transfers between devices, swap(): return lax.ppermute(value, axis, [(i, i ^ bit) for i in range(size)])  32.6 us
    ppermute x37, waiting for transfers between devices, swap(): return lax.ppermute(value, axis, [(i, i ^ bit) for i in range(size)])  32 us
    all_to_all x1, blocking collectives, token_shards(): lax.all_to_all(pair_sum, both, split_axis=0, concat_axis=0, axis_index_gr...  22.4 us
    pallas_call x11, Pallas kernels, call(): pl.pallas_call(body, out_shape=out_shapes, in_specs=specs, out_specs=pl.B...  17.5 us
    all_to_all x1, starting transfers between devices, token_shards(): lax.all_to_all(att_blocks, both, split_axis=0, concat_axis=0, axis_index_...  5.96 us
    unnamed x40, local copies, waits for them, and re-layouts  3.26 us
  transfers between devices with their start and end apart: 40, of which 14 were waited for; matrix products, arithmetic and copies ran while one was open for 0% of the time, Pallas kernels for 12%

profile of v5, /device:TPU:0, one launch (start us, length us, event | category | flops | bytes accessed | tf_op | source)
XLA Modules:
  0.0 119.8 jit_solution(9115300452944708104)
XLA Ops:
  4.7 3.1 %collective-permute-start = (bf16[1,16,2816]{2,1,0:T(8,128)(2,1)S(1)}, bf16[1,16,2816]{2,1,0:T(8,128)(2,1)S(1)}, u32[]{:S(2)}, u32[]{:S(2)}) collective-permute-start(bf16[1,16,2816]{2,1,0:T(8,128)(2,1)S(1)} %get-tuple-element.58), channel_id=1, source_target_pairs={{0,4},{1,5},{2,6},{3,7},{4,0},{5,1},{6,2},{7,3},{8,12},{9,13},{10,... | collective-permute-start | bytes 270344 | tf_op jit(solution)/shard_map/ppermute | solution.py:222
  7.8 2.6 %collective-permute-start.1 = (bf16[1,16,2816]{2,1,0:T(8,128)(2,1)S(1)}, bf16[1,16,2816]{2,1,0:T(8,128)(2,1)S(1)}, u32[]{:S(2)}, u32[]{:S(2)}) collective-permute-start(bf16[1,16,2816]{2,1,0:T(8,128)(2,1)S(1)} %get-tuple-element.59), channel_id=1, source_target_pairs={{0,8},{1,9},{2,10},{3,11},{4,12},{5,13},{6,14},{7,15},{8,0},{9,1},... | collective-permute-start | bytes 270344 | tf_op jit(solution)/shard_map/ppermute | solution.py:222
  10.4 1.7 %collective-permute-start.3 = (bf16[1,16,2816]{2,1,0:T(8,128)(2,1)S(1)}, bf16[1,16,2816]{2,1,0:T(8,128)(2,1)S(1)}, u32[]{:S(2)}, u32[]{:S(2)}) collective-permute-start(bf16[1,16,2816]{2,1,0:T(8,128)(2,1)S(1)} %get-tuple-element.57), channel_id=1, source_target_pairs={{0,2},{1,3},{2,0},{3,1},{4,6},{5,7},{6,4},{7,5},{8,10},{9,11},{10,... | collective-permute-start | bytes 270344 | tf_op jit(solution)/shard_map/ppermute | solution.py:222
  12.8 1.9 %shard_map.204 = bf16[8,16,1152]{2,1,0:T(8,128)(2,1)} custom-call(s32[1]{0:T(128)S(6)} %copy.24.length_ref, bf16[16,16,576]{2,1,0:T(8,128)(2,1)S(1)} %copy-done.4, bf16[16,576]{1,0:T(8,128)(2,1)S(1)} %copy-done.8, bf16[1,16,576]{2,1,0:T(8,128)(2,1)S(1)} %copy-done.9, bf16[1,576]{1,0:T(2,128)(2,1)S(1)} %copy-done.10, bf16[1,576,1024]{2,1,0:T(8,128)(2,1)S(1)} %bitcast.14, ...), custom_call_target="tpu_custom_call" | custom-call | flops 100000000 | bytes 1512644 | tf_op jit(solution)/shard_map/pallas_call | solution.py:271
  14.7 6.0 %all-to-all-start = ((bf16[8,16,1152]{2,1,0:T(8,128)(2,1)}), bf16[8,16,1152]{2,1,0:T(8,128)(2,1)S(1)}, u32[]{:S(2)}, u32[]{:S(2)}) async-start(bf16[8,16,1152]{2,1,0:T(8,128)(2,1)} %shard_map.204), calls=%async_computation | async-start | bytes 589824 | tf_op jit(solution)/shard_map/all_to_all | solution.py:859
  22.6 5.0 %collective-permute-done.4.refs_4_ = bf16[3,16,2816]{2,1,0:T(8,128)(2,1)S(1)} collective-permute-done((bf16[3,16,2816]{2,1,0:T(8,128)(2,1)S(1)}, bf16[3,16,2816]{2,1,0:T(8,128)(2,1)S(1)}, u32[]{:S(2)}, u32[]{:S(2)}) %collective-permute-start.4) | collective-permute-done | bytes 270368 | tf_op jit(solution)/shard_map/ppermute | solution.py:222
  28.2 1.8 %collective-permute-start.30 = (bf16[4,96,128]{2,1,0:T(8,128)(2,1)S(1)}, bf16[4,96,128]{2,1,0:T(8,128)(2,1)S(1)}, u32[]{:S(2)}, u32[]{:S(2)}) collective-permute-start(bf16[4,96,128]{2,1,0:T(8,128)(2,1)S(1)} %get-tuple-element.90), channel_id=1, source_target_pairs={{0,4},{1,5},{2,6},{3,7},{4,0},{5,1},{6,2},{7,3},{8,12},{9,13},{10,... | collective-permute-start | bytes 294920 | tf_op jit(solution)/shard_map/ppermute | solution.py:222
  30.0 2.4 %collective-permute-start.31 = (bf16[4,96,128]{2,1,0:T(8,128)(2,1)S(1)}, bf16[4,96,128]{2,1,0:T(8,128)(2,1)S(1)}, u32[]{:S(2)}, u32[]{:S(2)}) collective-permute-start(bf16[4,96,128]{2,1,0:T(8,128)(2,1)S(1)} %get-tuple-element.91), channel_id=1, source_target_pairs={{0,8},{1,9},{2,10},{3,11},{4,12},{5,13},{6,14},{7,15},{8,0},{9,1},... | collective-permute-start | bytes 294920 | tf_op jit(solution)/shard_map/ppermute | solution.py:222
  32.9 2.4 %shard_map.206 = (bf16[4,16,2176]{2,1,0:T(8,128)(2,1)S(1)}, bf16[4,16,2432]{2,1,0:T(8,128)(2,1)S(1)}, bf16[16,16,128]{2,1,0:T(8,128)(2,1)S(1)}, bf16[16,16,128]{2,1,0:T(8,128)(2,1)S(1)}) custom-call(s32[3]{0:T(128)S(1)} %pad_add_fusion.refs_0_.place_ref, bf16[8,16,1152]{2,1,0:T(8,128)(2,1)S(1)} %all-to-all-done.refs_1_, ...), custom_call_target="tpu_custom_call" | custom-call | flops 300000000 | bytes 1736716 | tf_op jit(solution)/shard_map/pallas_call | solution.py:271
  35.3 1.6 %collective-permute-start.8 = (bf16[4,16,2432]{2,1,0:T(8,128)(2,1)S(1)}, bf16[4,16,2432]{2,1,0:T(8,128)(2,1)S(1)}, u32[]{:S(2)}, u32[]{:S(2)}) collective-permute-start(bf16[4,16,2432]{2,1,0:T(8,128)(2,1)S(1)} %get-tuple-element.73), channel_id=1, source_target_pairs={{0,16},{16,0},{1,17},{17,1},{2,18},{18,2},{3,19},{19,3},{4,20},{20... | collective-permute-start | bytes 933896 | tf_op jit(solution)/shard_map/ppermute | solution.py:222
  36.9 7.6 %collective-permute-done.8.other_ref = bf16[4,16,2432]{2,1,0:T(8,128)(2,1)S(1)} collective-permute-done((bf16[4,16,2432]{2,1,0:T(8,128)(2,1)S(1)}, bf16[4,16,2432]{2,1,0:T(8,128)(2,1)S(1)}, u32[]{:S(2)}, u32[]{:S(2)}) %collective-permute-start.8) | collective-permute-done | bytes 311328 | tf_op jit(solution)/shard_map/ppermute | solution.py:222
  44.7 3.2 %collective-permute-start.10 = (bf16[16,2176]{1,0:T(8,128)(2,1)S(1)}, bf16[16,2176]{1,0:T(8,128)(2,1)S(1)}, u32[]{:S(2)}, u32[]{:S(2)}) collective-permute-start(bf16[16,2176]{1,0:T(8,128)(2,1)S(1)} %get-tuple-element.80), channel_id=1, source_target_pairs={{0,8},{1,9},{2,10},{3,11},{4,12},{5,13},{6,14},{7,15},{8,0},{9,1},... | collective-permute-start | bytes 208904 | tf_op jit(solution)/shard_map/ppermute | solution.py:222
  49.7 2.8 %shard_map.208 = (bf16[224,544]{1,0:T(8,128)(2,1)S(1)}, bf16[544,224]{1,0:T(8,128)(2,1)S(1)}, bf16[544,128]{1,0:T(8,128)(2,1)S(1)}) custom-call(s32[3]{0:T(128)S(1)} %pad_add_fusion.refs_0_.place_ref, bf16[16,16,128]{2,1,0:T(8,128)(2,1)S(1)} %get-tuple-element.71.plane_ref, bf16[4,16,2432]{2,1,0:T(8,128)(2,1)S(1)} %collective-permute-done.8.other_ref), custom_call_target="tpu_custom_call" | custom-call | bytes 376844 | tf_op jit(solution)/shard_map/pallas_call | solution.py:271
  55.6 3.0 %collective-permute-start.12 = (bf16[16,2176]{1,0:T(8,128)(2,1)S(1)}, bf16[16,2176]{1,0:T(8,128)(2,1)S(1)}, u32[]{:S(2)}, u32[]{:S(2)}) collective-permute-start(bf16[16,2176]{1,0:T(8,128)(2,1)S(1)} %get-tuple-element.87), channel_id=1, source_target_pairs={{0,4},{1,5},{2,6},{3,7},{4,0},{5,1},{6,2},{7,3},{8,12},{9,13},{10,... | collective-permute-start | bytes 208904 | tf_op jit(solution)/shard_map/ppermute | solution.py:222
  58.6 2.6 %collective-permute-done.12 = bf16[16,2176]{1,0:T(8,128)(2,1)S(1)} collective-permute-done((bf16[16,2176]{1,0:T(8,128)(2,1)S(1)}, bf16[16,2176]{1,0:T(8,128)(2,1)S(1)}, u32[]{:S(2)}, u32[]{:S(2)}) %collective-permute-start.12) | collective-permute-done | bytes 69664 | tf_op jit(solution)/shard_map/ppermute | solution.py:222
  65.7 2.1 %collective-permute-done.17.rest_4_ = bf16[32,2176]{1,0:T(8,128)(2,1)S(1)} collective-permute-done((bf16[32,2176]{1,0:T(8,128)(2,1)S(1)}, bf16[32,2176]{1,0:T(8,128)(2,1)S(1)}, u32[]{:S(2)}, u32[]{:S(2)}) %collective-permute-start.17) | collective-permute-done | bytes 139296 | tf_op jit(solution)/shard_map/ppermute | solution.py:222
  72.0 2.3 %collective-permute-done.19.rest_6_ = bf16[32,2176]{1,0:T(8,128)(2,1)S(1)} collective-permute-done((bf16[32,2176]{1,0:T(8,128)(2,1)S(1)}, bf16[32,2176]{1,0:T(8,128)(2,1)S(1)}, u32[]{:S(2)}, u32[]{:S(2)}) %collective-permute-start.19) | collective-permute-done | bytes 139296 | tf_op jit(solution)/shard_map/ppermute | solution.py:222
  76.9 2.6 %shard_map.210 = (bf16[224,704]{1,0:T(8,128)(2,1)S(1)}, bf16[512,2048]{1,0:T(8,128)(2,1)S(1)}, bf16[32,2048]{1,0:T(8,128)(2,1)S(1)}) custom-call(bf16[224,544]{1,0:T(8,128)(2,1)S(1)} %get-tuple-element.82.select_ref, bf16[1,704,2048]{2,1,0:T(8,128)(2,1)S(1)} %bitcast.12, bf16[1,704,2048]{2,1,0:T(8,128)(2,1)S(1)} %bitcast.13, ...), custom_call_target="tpu_custom_call" | custom-call | flops 2000000000 | bytes 8239104 | tf_op jit(solution)/shard_map/pallas_call | solution.py:271
  81.1 2.8 %shard_map.211 = (bf16[272,128]{1,0:T(8,128)(2,1)S(1)}, f32[224,128]{1,0:T(8,128)S(1)}) custom-call(s32[3]{0:T(128)S(1)} %pad_add_fusion.refs_0_.place_ref, bf16[8,96,128]{2,1,0:T(8,128)(2,1)S(1)} %pad_maximum_fusion.4.kept_ref, bf16[8,96,128]{2,1,0:T(8,128)(2,1)S(1)} %collective-permute-done.34.far_ref, ...), custom_call_target="tpu_custom_call" | custom-call | flops 500000000 | bytes 3069964 | tf_op jit(solution)/shard_map/pallas_call | solution.py:271
  84.6 2.0 %collective-permute-start.37 = (bf16[44,1024]{1,0:T(8,128)(2,1)S(1)}, bf16[44,1024]{1,0:T(8,128)(2,1)S(1)}, u32[]{:S(2)}, u32[]{:S(2)}) collective-permute-start(bf16[44,1024]{1,0:T(8,128)(2,1)S(1)} %get-tuple-element.106), channel_id=1, source_target_pairs={{0,1},{1,3},{2,5},{3,7},{4,9},{5,11},{6,13},{7,15},{8,0},{9,2},{10... | collective-permute-start | bytes 270344 | tf_op jit(solution)/shard_map/ppermute | solution.py:973
  87.0 4.1 %collective-permute-done.35.shared_other_ref = bf16[272,128]{1,0:T(8,128)(2,1)S(1)} collective-permute-done((bf16[272,128]{1,0:T(8,128)(2,1)S(1)}, bf16[272,128]{1,0:T(8,128)(2,1)S(1)}, u32[]{:S(2)}, u32[]{:S(2)}) %collective-permute-start.35) | collective-permute-done | bytes 69664 | tf_op jit(solution)/shard_map/ppermute | solution.py:222
  92.4 2.1 %shard_map.212 = (bf16[16,16,1152]{2,1,0:T(8,128)(2,1)S(1)}, bf16[16,16,1152]{2,1,0:T(8,128)(2,1)S(1)}) custom-call(s32[3]{0:T(128)S(1)} %pad_add_fusion.refs_0_.place_ref, bf16[224,704]{1,0:T(8,128)(2,1)S(1)} %get-tuple-element.88.act_ref, bf16[224,704]{1,0:T(8,128)(2,1)S(1)} %collective-permute-done.29.act_other_ref, ...), custom_call_target="tpu_custom_call" | custom-call | flops 1000000000 | bytes 4192268 | tf_op jit(solution)/shard_map/pallas_call | solution.py:271
  94.6 2.0 %collective-permute-done.38 = bf16[16,16,1152]{2,1,0:T(8,128)(2,1)S(1)} collective-permute-done((bf16[16,16,1152]{2,1,0:T(8,128)(2,1)S(1)}, bf16[16,16,1152]{2,1,0:T(8,128)(2,1)S(1)}, u32[]{:S(2)}, u32[]{:S(2)}) %collective-permute-start.38) | collective-permute-done | bytes 589856 | tf_op jit(solution)/shard_map/ppermute | solution.py:222
  96.7 22.4 %all_to_all.10.got_ref = bf16[16,16,1152]{2,1,0:T(8,128)(2,1)S(1)} all-to-all(bf16[16,16,1152]{2,1,0:T(8,128)(2,1)S(1)} %add_convert_fusion), channel_id=1, replica_groups={{0,2,4,6,8,10,12,14,16,18,20,22,24,26,28,30},{1,3,5,7,9,11,13,15,17,19,..., dimensions={0} | all-to-all | bytes 1179648 | tf_op jit(solution)/shard_map/all_to_all | solution.py:998
  (125 shorter events, 28.0 us)
Async XLA Ops:
  4.7 16.0 %collective-permute-start = (bf16[1,16,2816]{2,1,0:T(8,128)(2,1)S(1)}, bf16[1,16,2816]{2,1,0:T(8,128)(2,1)S(1)}, u32[]{:S(2)}, u32[]{:S(2)}) collective-permute-start(bf16[1,16,2816]{2,1,0:T(8,128)(2,1)S(1)} %get-tuple-element.58), channel_id=1, source_target_pairs={{0,4},{1,5},{2,6},{3,7},{4,0},{5,1},{6,2},{7,3},{8,12},{9,13},{10,... | collective-permute-start | bytes 270344 | tf_op jit(solution)/shard_map/ppermute | solution.py:222
  7.8 12.9 %collective-permute-start.1 = (bf16[1,16,2816]{2,1,0:T(8,128)(2,1)S(1)}, bf16[1,16,2816]{2,1,0:T(8,128)(2,1)S(1)}, u32[]{:S(2)}, u32[]{:S(2)}) collective-permute-start(bf16[1,16,2816]{2,1,0:T(8,128)(2,1)S(1)} %get-tuple-element.59), channel_id=1, source_target_pairs={{0,8},{1,9},{2,10},{3,11},{4,12},{5,13},{6,14},{7,15},{8,0},{9,1},... | collective-permute-start | bytes 270344 | tf_op jit(solution)/shard_map/ppermute | solution.py:222
  10.4 10.3 %collective-permute-start.2 = (bf16[1,16,2816]{2,1,0:T(8,128)(2,1)S(1)}, bf16[1,16,2816]{2,1,0:T(8,128)(2,1)S(1)}, u32[]{:S(2)}, u32[]{:S(2)}) collective-permute-start(bf16[1,16,2816]{2,1,0:T(8,128)(2,1)S(1)} %get-tuple-element.60), channel_id=1, source_target_pairs={{0,12},{1,13},{2,14},{3,15},{4,8},{5,9},{6,10},{7,11},{8,4},{9,5},... | collective-permute-start | bytes 270344 | tf_op jit(solution)/shard_map/ppermute | solution.py:222
  10.4 10.4 %collective-permute-start.3 = (bf16[1,16,2816]{2,1,0:T(8,128)(2,1)S(1)}, bf16[1,16,2816]{2,1,0:T(8,128)(2,1)S(1)}, u32[]{:S(2)}, u32[]{:S(2)}) collective-permute-start(bf16[1,16,2816]{2,1,0:T(8,128)(2,1)S(1)} %get-tuple-element.57), channel_id=1, source_target_pairs={{0,2},{1,3},{2,0},{3,1},{4,6},{5,7},{6,4},{7,5},{8,10},{9,11},{10,... | collective-permute-start | bytes 270344 | tf_op jit(solution)/shard_map/ppermute | solution.py:222
  14.7 18.1 %all-to-all-start = ((bf16[8,16,1152]{2,1,0:T(8,128)(2,1)}), bf16[8,16,1152]{2,1,0:T(8,128)(2,1)S(1)}, u32[]{:S(2)}, u32[]{:S(2)}) async-start(bf16[8,16,1152]{2,1,0:T(8,128)(2,1)} %shard_map.204), calls=%async_computation | async-start | bytes 589824 | tf_op jit(solution)/shard_map/all_to_all | solution.py:859
  20.8 6.9 %collective-permute-start.4 = (bf16[3,16,2816]{2,1,0:T(8,128)(2,1)S(1)}, bf16[3,16,2816]{2,1,0:T(8,128)(2,1)S(1)}, u32[]{:S(2)}, u32[]{:S(2)}) collective-permute-start(bf16[3,16,2816]{2,1,0:T(8,128)(2,1)S(1)} %pad_maximum_fusion.1), channel_id=1, source_target_pairs={{0,2},{1,3},{2,0},{3,1},{4,6},{5,7},{6,4},{7,5},{8,10},{9,11},{10,... | collective-permute-start | bytes 811016 | tf_op jit(solution)/shard_map/ppermute | solution.py:222
  21.4 11.5 %collective-permute-start.5 = (bf16[4,16,2816]{2,1,0:T(8,128)(2,1)S(1)}, bf16[4,16,2816]{2,1,0:T(8,128)(2,1)S(1)}, u32[]{:S(2)}, u32[]{:S(2)}) collective-permute-start(bf16[4,16,2816]{2,1,0:T(8,128)(2,1)S(1)} %pad_maximum_fusion.refs_2_), channel_id=1, source_target_pairs={{0,1},{1,0},{2,3},{3,2},{4,5},{5,4},{6,7},{7,6},{8,9},{9,8},{10,11... | collective-permute-start | bytes 1081352 | tf_op jit(solution)/shard_map/ppermute | solution.py:222
  28.2 16.4 %collective-permute-start.30 = (bf16[4,96,128]{2,1,0:T(8,128)(2,1)S(1)}, bf16[4,96,128]{2,1,0:T(8,128)(2,1)S(1)}, u32[]{:S(2)}, u32[]{:S(2)}) collective-permute-start(bf16[4,96,128]{2,1,0:T(8,128)(2,1)S(1)} %get-tuple-element.90), channel_id=1, source_target_pairs={{0,4},{1,5},{2,6},{3,7},{4,0},{5,1},{6,2},{7,3},{8,12},{9,13},{10,... | collective-permute-start | bytes 294920 | tf_op jit(solution)/shard_map/ppermute | solution.py:222
  30.0 14.6 %collective-permute-start.31 = (bf16[4,96,128]{2,1,0:T(8,128)(2,1)S(1)}, bf16[4,96,128]{2,1,0:T(8,128)(2,1)S(1)}, u32[]{:S(2)}, u32[]{:S(2)}) collective-permute-start(bf16[4,96,128]{2,1,0:T(8,128)(2,1)S(1)} %get-tuple-element.91), channel_id=1, source_target_pairs={{0,8},{1,9},{2,10},{3,11},{4,12},{5,13},{6,14},{7,15},{8,0},{9,1},... | collective-permute-start | bytes 294920 | tf_op jit(solution)/shard_map/ppermute | solution.py:222
  32.4 12.2 %collective-permute-start.32 = (bf16[4,96,128]{2,1,0:T(8,128)(2,1)S(1)}, bf16[4,96,128]{2,1,0:T(8,128)(2,1)S(1)}, u32[]{:S(2)}, u32[]{:S(2)}) collective-permute-start(bf16[4,96,128]{2,1,0:T(8,128)(2,1)S(1)} %get-tuple-element.92), channel_id=1, source_target_pairs={{0,12},{1,13},{2,14},{3,15},{4,8},{5,9},{6,10},{7,11},{8,4},{9,5},... | collective-permute-start | bytes 294920 | tf_op jit(solution)/shard_map/ppermute | solution.py:222
  35.3 9.2 %collective-permute-start.8 = (bf16[4,16,2432]{2,1,0:T(8,128)(2,1)S(1)}, bf16[4,16,2432]{2,1,0:T(8,128)(2,1)S(1)}, u32[]{:S(2)}, u32[]{:S(2)}) collective-permute-start(bf16[4,16,2432]{2,1,0:T(8,128)(2,1)S(1)} %get-tuple-element.73), channel_id=1, source_target_pairs={{0,16},{16,0},{1,17},{17,1},{2,18},{18,2},{3,19},{19,3},{4,20},{20... | collective-permute-start | bytes 933896 | tf_op jit(solution)/shard_map/ppermute | solution.py:222
  44.6 7.9 %collective-permute-start.9 = (bf16[16,2176]{1,0:T(8,128)(2,1)S(1)}, bf16[16,2176]{1,0:T(8,128)(2,1)S(1)}, u32[]{:S(2)}, u32[]{:S(2)}) collective-permute-start(bf16[16,2176]{1,0:T(8,128)(2,1)S(1)} %get-tuple-element.79), channel_id=1, source_target_pairs={{0,4},{1,5},{2,6},{3,7},{4,0},{5,1},{6,2},{7,3},{8,12},{9,13},{10,... | collective-permute-start | bytes 208904 | tf_op jit(solution)/shard_map/ppermute | solution.py:222
  44.7 7.9 %collective-permute-start.10 = (bf16[16,2176]{1,0:T(8,128)(2,1)S(1)}, bf16[16,2176]{1,0:T(8,128)(2,1)S(1)}, u32[]{:S(2)}, u32[]{:S(2)}) collective-permute-start(bf16[16,2176]{1,0:T(8,128)(2,1)S(1)} %get-tuple-element.80), channel_id=1, source_target_pairs={{0,8},{1,9},{2,10},{3,11},{4,12},{5,13},{6,14},{7,15},{8,0},{9,1},... | collective-permute-start | bytes 208904 | tf_op jit(solution)/shard_map/ppermute | solution.py:222
  49.1 14.9 %collective-permute-start.33 = (bf16[8,96,128]{2,1,0:T(8,128)(2,1)S(1)}, bf16[8,96,128]{2,1,0:T(8,128)(2,1)S(1)}, u32[]{:S(2)}, u32[]{:S(2)}) collective-permute-start(bf16[8,96,128]{2,1,0:T(8,128)(2,1)S(1)} %pad_maximum_fusion.3), channel_id=1, source_target_pairs={{0,2},{1,3},{2,0},{3,1},{4,6},{5,7},{6,4},{7,5},{8,10},{9,11},{10,... | collective-permute-start | bytes 589832 | tf_op jit(solution)/shard_map/ppermute | solution.py:222
  54.2 9.2 %collective-permute-start.14 = (bf16[16,2176]{1,0:T(8,128)(2,1)S(1)}, bf16[16,2176]{1,0:T(8,128)(2,1)S(1)}, u32[]{:S(2)}, u32[]{:S(2)}) collective-permute-start(bf16[16,2176]{1,0:T(8,128)(2,1)S(1)} %get-tuple-element.87), channel_id=1, source_target_pairs={{0,12},{1,13},{2,14},{3,15},{4,8},{5,9},{6,10},{7,11},{8,4},{9,5},... | collective-permute-start | bytes 208904 | tf_op jit(solution)/shard_map/ppermute | solution.py:222
  55.5 7.3 %collective-permute-start.13 = (bf16[16,2176]{1,0:T(8,128)(2,1)S(1)}, bf16[16,2176]{1,0:T(8,128)(2,1)S(1)}, u32[]{:S(2)}, u32[]{:S(2)}) collective-permute-start(bf16[16,2176]{1,0:T(8,128)(2,1)S(1)} %get-tuple-element.87), channel_id=1, source_target_pairs={{0,8},{1,9},{2,10},{3,11},{4,12},{5,13},{6,14},{7,15},{8,0},{9,1},... | collective-permute-start | bytes 208904 | tf_op jit(solution)/shard_map/ppermute | solution.py:222
  61.3 6.5 %collective-permute-start.17 = (bf16[32,2176]{1,0:T(8,128)(2,1)S(1)}, bf16[32,2176]{1,0:T(8,128)(2,1)S(1)}, u32[]{:S(2)}, u32[]{:S(2)}) collective-permute-start(bf16[32,2176]{1,0:T(8,128)(2,1)S(1)} %constant_dynamic-update-slice_fusion.rest_0_), channel_id=1, source_target_pairs={{0,16},{16,0},{1,17},{17,1},{2,18},{18,2},{3,19},{19,3},{4,20},{20... | collective-permute-start | bytes 417800 | tf_op jit(solution)/shard_map/ppermute | solution.py:222
  62.8 6.5 %collective-permute-start.15 = (bf16[32,2176]{1,0:T(8,128)(2,1)S(1)}, bf16[32,2176]{1,0:T(8,128)(2,1)S(1)}, u32[]{:S(2)}, u32[]{:S(2)}) collective-permute-start(bf16[32,2176]{1,0:T(8,128)(2,1)S(1)} %constant_dynamic-update-slice_fusion.rest_0_), channel_id=1, source_target_pairs={{0,2},{1,3},{2,0},{3,1},{4,6},{5,7},{6,4},{7,5},{8,10},{9,11},{10,... | collective-permute-start | bytes 417800 | tf_op jit(solution)/shard_map/ppermute | solution.py:222
  63.4 6.9 %collective-permute-start.18 = (bf16[32,2176]{1,0:T(8,128)(2,1)S(1)}, bf16[32,2176]{1,0:T(8,128)(2,1)S(1)}, u32[]{:S(2)}, u32[]{:S(2)}) collective-permute-start(bf16[32,2176]{1,0:T(8,128)(2,1)S(1)} %constant_dynamic-update-slice_fusion.2.rest_1_), channel_id=1, source_target_pairs={{0,16},{16,0},{1,17},{17,1},{2,18},{18,2},{3,19},{19,3},{4,20},{20... | collective-permute-start | bytes 417800 | tf_op jit(solution)/shard_map/ppermute | solution.py:222
  64.1 6.9 %collective-permute-start.22 = (bf16[32,2176]{1,0:T(8,128)(2,1)S(1)}, bf16[32,2176]{1,0:T(8,128)(2,1)S(1)}, u32[]{:S(2)}, u32[]{:S(2)}) collective-permute-start(bf16[32,2176]{1,0:T(8,128)(2,1)S(1)} %constant_dynamic-update-slice_fusion.2.rest_1_), channel_id=1, source_target_pairs={{0,1},{1,0},{2,3},{3,2},{4,5},{5,4},{6,7},{7,6},{8,9},{9,8},{10,11... | collective-permute-start | bytes 417800 | tf_op jit(solution)/shard_map/ppermute | solution.py:222
  64.2 7.4 %collective-permute-start.16 = (bf16[32,2176]{1,0:T(8,128)(2,1)S(1)}, bf16[32,2176]{1,0:T(8,128)(2,1)S(1)}, u32[]{:S(2)}, u32[]{:S(2)}) collective-permute-start(bf16[32,2176]{1,0:T(8,128)(2,1)S(1)} %constant_dynamic-update-slice_fusion.2.rest_1_), channel_id=1, source_target_pairs={{0,2},{1,3},{2,0},{3,1},{4,6},{5,7},{6,4},{7,5},{8,10},{9,11},{10,... | collective-permute-start | bytes 417800 | tf_op jit(solution)/shard_map/ppermute | solution.py:222
  79.5 12.8 %collective-permute-start.29 = (bf16[224,704]{1,0:T(8,128)(2,1)S(1)}, bf16[224,704]{1,0:T(8,128)(2,1)S(1)}, u32[]{:S(2)}, u32[]{:S(2)}) collective-permute-start(bf16[224,704]{1,0:T(8,128)(2,1)S(1)} %get-tuple-element.88.act_ref), channel_id=1, source_target_pairs={{0,16},{16,0},{1,17},{17,1},{2,18},{18,2},{3,19},{19,3},{4,20},{20... | collective-permute-start | bytes 946184 | tf_op jit(solution)/shard_map/ppermute | solution.py:222
  83.9 7.2 %collective-permute-start.36 = (bf16[44,1024]{1,0:T(8,128)(2,1)S(1)}, bf16[44,1024]{1,0:T(8,128)(2,1)S(1)}, u32[]{:S(2)}, u32[]{:S(2)}) collective-permute-start(bf16[44,1024]{1,0:T(8,128)(2,1)S(1)} %get-tuple-element.105), channel_id=1, source_target_pairs={{0,0},{1,2},{2,4},{3,6},{4,8},{5,10},{6,12},{7,14},{8,1},{9,3},{10... | collective-permute-start | bytes 270344 | tf_op jit(solution)/shard_map/ppermute | solution.py:968
  84.6 7.7 %collective-permute-start.37 = (bf16[44,1024]{1,0:T(8,128)(2,1)S(1)}, bf16[44,1024]{1,0:T(8,128)(2,1)S(1)}, u32[]{:S(2)}, u32[]{:S(2)}) collective-permute-start(bf16[44,1024]{1,0:T(8,128)(2,1)S(1)} %get-tuple-element.106), channel_id=1, source_target_pairs={{0,1},{1,3},{2,5},{3,7},{4,9},{5,11},{6,13},{7,15},{8,0},{9,2},{10... | collective-permute-start | bytes 270344 | tf_op jit(solution)/shard_map/ppermute | solution.py:973
  (35 other events, 286.5 us)
